TPU v7x, 512 devices: a whole 4x8x8 slice. The times are simulated.
512 devices in a mesh: frame: 16 (over z, core), head: 8 (over x, y_lo), dp: 4 (over y_hi).
Axes of the slice: x: 4, y: 8 (y_hi: 4, y_lo: 2; y = y_hi * 2 + y_lo), z: 8, core: 2. Of those that a mesh axis runs over, the one named last changes fastest.
Arguments:
- latents: bfloat16 [64, 512, 1152], P(('dp', 'frame'), None, 'head'), parts along dimension 0, may hold values from -36 to 36
- modulation: float32 [36, 1152], P('dp'), parts along dimension 0, may hold values from -3 to 3
- spatial_qkv: bfloat16 [1152, 3, 1152], P('frame', None, 'head'), may hold values from -1 to 1
- spatial_out: bfloat16 [1152, 1152], P('head', 'frame'), may hold values from -0.25 to 0.25
- temporal_qkv: bfloat16 [1152, 3, 1152], P('frame', None, 'head'), may hold values from -0.1875 to 0.1875
- temporal_out: bfloat16 [1152, 1152], P('head', 'frame'), may hold values from -0.25 to 0.25
- mlp_up: bfloat16 [1152, 4608], P('frame', 'head'), may hold values from -0.1875 to 0.1875
- mlp_down: bfloat16 [4608, 1152], P('head', 'frame'), may hold values from -0.125 to 0.125
Outputs:
- block_out: bfloat16 [64, 512, 1152], P(('dp', 'frame'), None, 'head'), parts along dimension 0
There are 4 independent parts, one for each index of `dp`. A program takes and returns all parts, laid end to end along the dimension named above; an argument that names none is the same for every part. Nothing has to cross between parts.
All inputs are finite; a program needn't handle non-finite values.
Results may differ from a plain program's by a relative error of at most 0.023.
Values may be sent and summed in bfloat16 or wider, within the bound.
No kernel may reach another device: no remote copies, remote signals or barrier semaphores. Data moves between devices by JAX's collectives and lax.ppermute only.
A program may use at most 64 MiB of HBM per device.

v0:
```python
import math

import jax
import jax.numpy as jnp
from jax import lax
from jax.sharding import PartitionSpec as P

HEAD_DIM = 72


norm_eps = 1e-06


def layer_mod(values, shift_row, scale_row):
    floats = values.astype(jnp.float32)
    center = floats - jnp.mean(floats, axis=-1, keepdims=True)
    spread = jnp.mean(center * center, axis=-1, keepdims=True)
    normal = center * lax.rsqrt(spread + norm_eps)
    return (normal * (1.0 + scale_row) + shift_row).astype(jnp.bfloat16)


def rms_scale(tensor):
    return tensor * lax.rsqrt(jnp.mean(tensor * tensor, axis=-1, keepdims=True) + norm_eps)


def split_heads(mixed_qkv):
    qkv_parts = mixed_qkv.reshape(mixed_qkv.shape[0], 3, -1, HEAD_DIM)
    query_rows = rms_scale(qkv_parts[:, 0]).astype(jnp.bfloat16)
    key_rows = rms_scale(qkv_parts[:, 1]).astype(jnp.bfloat16)
    value_rows = qkv_parts[:, 2].astype(jnp.bfloat16)
    return (query_rows, key_rows, value_rows)


def widen_stream(stream):
    return lax.all_gather(stream, "head", axis=1, tiled=True)


def add_branch(partial_sum, stream, gate_row):
    summed = lax.psum_scatter(
        partial_sum.astype(jnp.bfloat16), "head", scatter_dimension=1, tiled=True
    ).astype(jnp.float32)
    share_width = summed.shape[1]
    gate_part = lax.dynamic_slice_in_dim(
        gate_row, lax.axis_index("head") * share_width, share_width, 0
    )
    return (stream.astype(jnp.float32) + gate_part * summed).astype(jnp.bfloat16)


def project_in(hidden, weight):
    return jnp.dot(
        hidden,
        lax.all_gather(weight, "frame", axis=0, tiled=True),
        preferred_element_type=jnp.float32,
    )


def project_out(values, weight):
    return jnp.dot(
        values,
        lax.all_gather(weight, "frame", axis=1, tiled=True),
        preferred_element_type=jnp.float32,
    )


def spatial_attention(query_rows, key_rows, value_rows):
    row_count = query_rows.shape[0]
    block_rows = min(row_count, 512)
    factor = 1.0 / math.sqrt(HEAD_DIM)
    query_blocks = query_rows.reshape(
        row_count // block_rows, block_rows, query_rows.shape[1], HEAD_DIM
    )

    def one_block(query_block):
        scores = (
            jnp.einsum("qhd,khd->hqk", query_block, key_rows, preferred_element_type=jnp.float32)
            * factor
        )
        weights = jnp.exp(scores)
        weights = (weights / jnp.sum(weights, axis=-1, keepdims=True)).astype(jnp.bfloat16)
        attended = jnp.einsum(
            "hqk,khd->qhd", weights, value_rows, preferred_element_type=jnp.float32
        )
        return attended.astype(jnp.bfloat16)

    attended = lax.map(one_block, query_blocks)
    return attended.reshape(row_count, -1)


def temporal_attention(query_rows, key_rows, value_rows):
    factor = 1.0 / math.sqrt(HEAD_DIM)
    scores = (
        jnp.einsum("fphd,gphd->phfg", query_rows, key_rows, preferred_element_type=jnp.float32)
        * factor
    )
    weights = jnp.exp(scores)
    weights = (weights / jnp.sum(weights, axis=-1, keepdims=True)).astype(jnp.bfloat16)
    attended = jnp.einsum(
        "phfg,gphd->fphd", weights, value_rows, preferred_element_type=jnp.float32
    )
    return attended.astype(jnp.bfloat16).reshape(query_rows.shape[0], query_rows.shape[1], -1)


def mlp_branch(stream, modulation, mlp_up, mlp_down):
    hidden = layer_mod(widen_stream(stream), modulation[6], modulation[7])
    activation = jax.nn.gelu(project_in(hidden, mlp_up), approximate=True).astype(jnp.bfloat16)
    return add_branch(project_out(activation, mlp_down), stream, modulation[8])


def per_device(
    latents, modulation, spatial_qkv, spatial_out, temporal_qkv, temporal_out, mlp_up, mlp_down
):
    patch_count = latents.shape[1]
    local_width = latents.shape[2]
    frame_count = lax.axis_size("frame")
    place_count = patch_count // frame_count
    stream = latents.reshape(patch_count, local_width)
    spatial_weight = spatial_qkv.reshape(spatial_qkv.shape[0], -1)
    temporal_weight = temporal_qkv.reshape(temporal_qkv.shape[0], -1)
    hidden = layer_mod(widen_stream(stream), modulation[0], modulation[1])
    query_rows, key_rows, value_rows = split_heads(project_in(hidden, spatial_weight))
    attended = spatial_attention(query_rows, key_rows, value_rows)
    stream = add_branch(project_out(attended, spatial_out), stream, modulation[2])
    stream_width = stream.shape[1]
    hidden = layer_mod(widen_stream(stream), modulation[3], modulation[4])
    query_rows, key_rows, value_rows = split_heads(project_in(hidden, temporal_weight))
    head_width = query_rows.shape[1] * HEAD_DIM
    moved_query, moved_key, moved_value = (
        lax.all_to_all(
            query_rows.reshape(1, patch_count, head_width),
            "frame",
            split_axis=1,
            concat_axis=0,
            tiled=True,
        ),
        lax.all_to_all(
            key_rows.reshape(1, patch_count, head_width),
            "frame",
            split_axis=1,
            concat_axis=0,
            tiled=True,
        ),
        lax.all_to_all(
            value_rows.reshape(1, patch_count, head_width),
            "frame",
            split_axis=1,
            concat_axis=0,
            tiled=True,
        ),
    )
    attended = temporal_attention(
        moved_query.reshape(frame_count, place_count, -1, HEAD_DIM),
        moved_key.reshape(frame_count, place_count, -1, HEAD_DIM),
        moved_value.reshape(frame_count, place_count, -1, HEAD_DIM),
    )
    returned = lax.all_to_all(attended, "frame", split_axis=0, concat_axis=1, tiled=True)
    stream = add_branch(
        project_out(returned.reshape(patch_count, head_width), temporal_out), stream, modulation[5]
    )
    stream = mlp_branch(stream, modulation, mlp_up, mlp_down)
    result = stream.reshape(1, patch_count, stream_width)
    return result


def solution(mesh):
    placed = (
        P(("dp", "frame"), None, "head"),
        P("dp", None),
        P("frame", None, "head"),
        P("head", "frame"),
        P("frame", None, "head"),
        P("head", "frame"),
        P("frame", "head"),
        P("head", "frame"),
    )
    return jax.shard_map(
        per_device,
        mesh=mesh,
        in_specs=placed,
        out_specs=P(("dp", "frame"), None, "head"),
        check_vma=False,
    )
```

profile of v0, /device:TPU:1, one launch (start us, length us, event | category | flops | bytes accessed | tf_op | source)
XLA Modules:
  0.0 470.7 jit_solution(6990037503766344398)
XLA Ops:
  9.3 26.1 %all_gather.29 = bf16[144,1152]{0,1:T(8,128)(2,1)S(1)} all-gather(bf16[144,72]{0,1:T(8,128)(2,1)S(1)} %copy.38), channel_id=1, replica_groups=mesh['frame'=16,'head'=8,'dp'=4] {'frame'}, dimensions={1}, use_global_device_ids=true | all-gather | bytes 352512 | tf_op jit(solution)/shard_map/all_gather | solution.py:60
  36.8 18.0 %all_gather.28 = bf16[1152,432]{1,0:T(8,128)(2,1)S(1)} all-gather(bf16[72,432]{1,0:T(8,128)(2,1)S(1)} %copy.36), channel_id=1, replica_groups=mesh['frame'=16,'head'=8,'dp'=4] {'frame'}, dimensions={0}, use_global_device_ids=true | all-gather | bytes 1057536 | tf_op jit(solution)/shard_map/all_gather | solution.py:52
  56.0 1.6 convert_reduce_fusion
  62.0 46.0 %reduce-scatter.4.cloned.1.call-done = bf16[512,144]{0,1:T(8,128)(2,1)} async-done(((bf16[512,1152]{0,1:T(8,128)(2,1)}), bf16[512,144]{0,1:T(8,128)(2,1)}) %reduce-scatter.4.cloned.1.call-update) | async-done | bytes 147472 | tf_op jit(solution)/shard_map/reduce_scatter | solution.py:39
  108.0 1.7 fusion.56
  110.0 26.9 %all_gather.31 = bf16[1152,432]{1,0:T(8,128)(2,1)S(1)} all-gather(bf16[72,432]{1,0:T(8,128)(2,1)S(1)} %copy.40), channel_id=1, replica_groups=mesh['frame'=16,'head'=8,'dp'=4] {'frame'}, dimensions={0}, use_global_device_ids=true | all-gather | bytes 1057536 | tf_op jit(solution)/shard_map/all_gather | solution.py:52
  136.9 17.4 %all-gather.7.cloned.1.call-done = bf16[512,1152]{0,1:T(8,128)(2,1)} async-done(((bf16[512,144]{0,1:T(8,128)(2,1)}), bf16[512,1152]{0,1:T(8,128)(2,1)}) %all-gather.7.cloned.1.call-update) | async-done | bytes 1179664 | tf_op jit(solution)/shard_map/all_gather | solution.py:35
  154.3 1.6 convert_reduce_fusion.2
  158.5 2.2 reduce.22
  161.8 13.0 %all-to-all-start.1 = ((bf16[16,2,2304]{2,1,0:T(2,128)(2,1)}), bf16[16,2,2304]{2,1,0:T(2,128)(2,1)S(1)}, u32[]{:S(2)}, u32[]{:S(2)}) async-start(bf16[16,2,2304]{2,1,0:T(2,128)(2,1)} %reshape.219), calls=%async_computation.2 | async-start | bytes 294912 | tf_op jit(solution)/shard_map/all_to_all | solution.py:128
  175.3 2.2 reduce.21
  178.6 5.5 %all-to-all-done.1 = bf16[16,2,2304]{2,1,0:T(2,128)(2,1)S(1)} async-done(((bf16[16,2,2304]{2,1,0:T(2,128)(2,1)}), bf16[16,2,2304]{2,1,0:T(2,128)(2,1)S(1)}, u32[]{:S(2)}, u32[]{:S(2)}) %all-to-all-start.1) | async-done | bytes 147488 | tf_op jit(solution)/shard_map/all_to_all | solution.py:128
  184.1 3.6 all-to-all-start.2
  188.2 2.2 reduce.23
  192.3 4.2 all-to-all-done.2
  196.5 3.4 all-to-all-start
  199.9 1.5 bitcast_reduce_fusion.1
  202.4 1.5 bitcast_reduce_fusion.2
  204.1 4.8 %all-to-all-done = bf16[16,2,2304]{2,1,0:T(2,128)(2,1)S(1)} async-done(((bf16[16,2,2304]{2,1,0:T(2,128)(2,1)}), bf16[16,2,2304]{2,1,0:T(2,128)(2,1)S(1)}, u32[]{:S(2)}, u32[]{:S(2)}) %all-to-all-start) | async-done | bytes 147488 | tf_op jit(solution)/shard_map/all_to_all | solution.py:142
  209.7 1.5 bitcast_reduce_fusion
  213.2 3.4 all-to-all-start.3
  216.8 21.7 %all_gather.32 = bf16[144,1152]{0,1:T(8,128)(2,1)S(1)} all-gather(bf16[144,72]{0,1:T(8,128)(2,1)S(1)} %copy.49), channel_id=1, replica_groups=mesh['frame'=16,'head'=8,'dp'=4] {'frame'}, dimensions={1}, use_global_device_ids=true | all-gather | bytes 352512 | tf_op jit(solution)/shard_map/all_gather | solution.py:60
  238.6 1.5 convolution_convert_fusion.1
  240.2 39.0 %reduce-scatter.6.cloned.1.call-done = bf16[512,144]{0,1:T(8,128)(2,1)} async-done(((bf16[512,1152]{0,1:T(8,128)(2,1)}), bf16[512,144]{0,1:T(8,128)(2,1)}) %reduce-scatter.6.cloned.1.call-update) | async-done | bytes 147472 | tf_op jit(solution)/shard_map/reduce_scatter | solution.py:39
  279.3 1.7 add_convert_fusion.1
  282.6 43.0 %all-gather.9.cloned.1.call-done = bf16[512,1152]{0,1:T(8,128)(2,1)} async-done(((bf16[512,144]{0,1:T(8,128)(2,1)}), bf16[512,1152]{0,1:T(8,128)(2,1)}) %all-gather.9.cloned.1.call-update) | async-done | bytes 1179664 | tf_op jit(solution)/shard_map/all_gather | solution.py:35
  325.5 1.6 convert_reduce_fusion.1
  327.6 46.8 %all-gather.11.cloned.1.call-done = bf16[1152,576]{1,0:T(8,128)(2,1)} async-done(((bf16[72,576]{1,0:T(8,128)(2,1)}), bf16[1152,576]{1,0:T(8,128)(2,1)}) %all-gather.11.cloned.1.call-update) | async-done | bytes 1327120 | tf_op jit(solution)/shard_map/all_gather | solution.py:52
  374.3 42.7 %all-gather.13.cloned.1.call-done = bf16[576,1152]{0,1:T(8,128)(2,1)} async-done(((bf16[576,72]{0,1:T(8,128)(2,1)}), bf16[576,1152]{0,1:T(8,128)(2,1)}) %all-gather.13.cloned.1.call-update) | async-done | bytes 1327120 | tf_op jit(solution)/shard_map/all_gather | solution.py:60
  417.0 5.2 %convolution_convert_fusion = bf16[512,1152]{0,1:T(8,128)(2,1)} fusion(bf16[576,1152]{0,1:T(8,128)(2,1)} %all-gather.13.cloned.1.call-done, bf16[1152,576]{1,0:T(8,128)(2,1)} %all-gather.11.cloned.1.call-done, bf16[512,1152]{0,1:T(8,128)(2,1)S(1)} %copy-done, f32[1152]{0:T(1024)S(1)} %get-tuple-element.35, f32[1152]{0:T(1024)S(1)} %get-tuple-element.40, ...), kind=kOutput, calls=%fused_computation | convolution fusion | flops 1365737472 | bytes 5026816 | tf_op jit(solution)/shard_map/dot_general | solution.py:58
  422.3 39.8 %reduce-scatter.8.cloned.1.call-done = bf16[512,144]{0,1:T(8,128)(2,1)} async-done(((bf16[512,1152]{0,1:T(8,128)(2,1)}), bf16[512,144]{0,1:T(8,128)(2,1)}) %reduce-scatter.8.cloned.1.call-update) | async-done | bytes 147472 | tf_op jit(solution)/shard_map/reduce_scatter | solution.py:39
  462.2 1.7 fusion.65
  (83 shorter events, 23.8 us)
Async XLA Ops:
  6.5 49.5 %all-gather.15.cloned.1.call-start = ((), (), s32[]{:S(2)}) async-start(), calls=%async_computation.14 | async-start | bytes 1327104 | tf_op jit(solution)/shard_map/all_gather | solution.py:35
  7.3 100.7 %reduce-scatter.4.cloned.1.call-start = ((), (), s32[]{:S(2)}) async-start(), calls=%async_computation.7 | async-start | bytes 1327104 | tf_op jit(solution)/shard_map/reduce_scatter | solution.py:39
  56.0 1.6 copy-start.1
  60.3 47.6 %copy-start.5 = (bf16[1,512,144]{1,2,0:T(8,128)(2,1)S(1)}, bf16[1,512,144]{1,2,0:T(8,128)(2,1)}, u32[]{:S(2)}) copy-start(bf16[1,512,144]{1,2,0:T(8,128)(2,1)} %param.8) | copy-start | bytes 442372
  60.3 49.4 %copy-start.6 = (bf16[72,3,144]{2,0,1:T(8,128)(2,1)S(1)}, bf16[72,3,144]{2,0,1:T(8,128)(2,1)}, u32[]{:S(2)}) copy-start(bf16[72,3,144]{2,0,1:T(8,128)(2,1)} %param.12) | copy-start | bytes 186628
  61.8 92.5 %all-gather.7.cloned.1.call-start = ((), (), s32[]{:S(2)}) async-start(), calls=%async_computation.8 | async-start | bytes 1327104 | tf_op jit(solution)/shard_map/all_gather | solution.py:35
  154.3 1.6 copy-start.2
  161.8 22.3 %all-to-all-start.1 = ((bf16[16,2,2304]{2,1,0:T(2,128)(2,1)}), bf16[16,2,2304]{2,1,0:T(2,128)(2,1)S(1)}, u32[]{:S(2)}, u32[]{:S(2)}) async-start(bf16[16,2,2304]{2,1,0:T(2,128)(2,1)} %reshape.219), calls=%async_computation.2 | async-start | bytes 294912 | tf_op jit(solution)/shard_map/all_to_all | solution.py:128
  184.1 12.4 %all-to-all-start.2 = ((bf16[16,2,2304]{2,1,0:T(2,128)(2,1)}), bf16[16,2,2304]{2,1,0:T(2,128)(2,1)S(1)}, u32[]{:S(2)}, u32[]{:S(2)}) async-start(bf16[16,2,2304]{2,1,0:T(2,128)(2,1)} %reshape.217), calls=%async_computation.3 | async-start | bytes 294912 | tf_op jit(solution)/shard_map/all_to_all | solution.py:135
  196.5 12.3 %all-to-all-start = ((bf16[16,2,2304]{2,1,0:T(2,128)(2,1)}), bf16[16,2,2304]{2,1,0:T(2,128)(2,1)S(1)}, u32[]{:S(2)}, u32[]{:S(2)}) async-start(bf16[16,2,2304]{2,1,0:T(2,128)(2,1)} %reshape.221), calls=%async_computation.1 | async-start | bytes 294912 | tf_op jit(solution)/shard_map/all_to_all | solution.py:142
  211.8 5.0 %copy-start.7 = (bf16[144,72]{1,0:T(8,128)(2,1)S(1)}, bf16[144,72]{1,0:T(8,128)(2,1)}, u32[]{:S(2)}) copy-start(bf16[144,72]{1,0:T(8,128)(2,1)} %param.13) | copy-start | bytes 62212
  213.2 25.3 %all-to-all-start.3 = ((bf16[16,32,144]{2,1,0:T(8,128)(2,1)}), bf16[16,32,144]{2,1,0:T(8,128)(2,1)S(1)}, u32[]{:S(2)}, u32[]{:S(2)}) async-start(bf16[16,32,144]{2,1,0:T(8,128)(2,1)} %reshape.202), calls=%async_computation.4 | async-start | bytes 524288 | tf_op jit(solution)/shard_map/all_to_all | solution.py:155
  216.7 62.6 %reduce-scatter.6.cloned.1.call-start = ((), (), s32[]{:S(2)}) async-start(), calls=%async_computation.9 | async-start | bytes 1327104 | tf_op jit(solution)/shard_map/reduce_scatter | solution.py:39
  238.5 40.7 %copy-start.3 = (bf16[512,144]{0,1:T(8,128)(2,1)S(1)}, bf16[512,144]{0,1:T(8,128)(2,1)}, u32[]{:S(2)}) copy-start(bf16[512,144]{0,1:T(8,128)(2,1)} %fusion.56) | copy-start | bytes 442372
  240.1 85.5 %all-gather.9.cloned.1.call-start = ((), (), s32[]{:S(2)}) async-start(), calls=%async_computation.10 | async-start | bytes 1327104 | tf_op jit(solution)/shard_map/all_gather | solution.py:35
  281.0 93.3 %all-gather.11.cloned.1.call-start = ((), (), s32[]{:S(2)}) async-start(), calls=%async_computation.11 | async-start | bytes 1566720 | tf_op jit(solution)/shard_map/all_gather | solution.py:52
  281.5 135.5 %all-gather.13.cloned.1.call-start = ((), (), s32[]{:S(2)}) async-start(), calls=%async_computation.12 | async-start | bytes 1566720 | tf_op jit(solution)/shard_map/all_gather | solution.py:60
  282.3 179.9 %reduce-scatter.8.cloned.1.call-start = ((), (), s32[]{:S(2)}) async-start(), calls=%async_computation.13 | async-start | bytes 1327104 | tf_op jit(solution)/shard_map/reduce_scatter | solution.py:39
  325.5 1.6 copy-start
  417.0 45.1 %copy-start.4 = (bf16[512,144]{0,1:T(8,128)(2,1)S(1)}, bf16[512,144]{0,1:T(8,128)(2,1)}, u32[]{:S(2)}) copy-start(bf16[512,144]{0,1:T(8,128)(2,1)} %add_convert_fusion.1) | copy-start | bytes 442372
Sparse Core Ops, SparseCore 0:
  9.4 46.5 all-gather.14
  62.0 45.9 reduce-scatter.3
  110.1 44.2 all-gather.6
  240.2 39.0 reduce-scatter.5
  281.2 44.3 all-gather.8
  327.5 46.7 all-gather.10
  376.4 40.5 all-gather.12
  422.4 39.7 reduce-scatter.7
where the time goes:
time: 476 us; the launch traced here: 471 us
  waiting for transfers between devices  293 us (62%)
  blocking collectives  92.7 us (19%)
  starting transfers between devices  23.9 us (5%)
  other arithmetic  19.2 us (4%)
  local copies, waits for them, and re-layouts  16.2 us (3%)
  between operations  13.8 us (3%)
  matrix products  12.2 us (3%)
    reduce_scatter x3, waiting for transfers between devices, add_branch(): lax.psum_scatter(partial_sum.astype(jnp.bfloat16), 'head', scatter_dimens...  125 us
    all_gather x3, waiting for transfers between devices, widen_stream(): return lax.all_gather(stream, 'head', axis=1, tiled=True)  61.7 us
    all_gather x2, blocking collectives, project_out(): lax.all_gather(weight, 'frame', axis=1, tiled=True)  47.8 us
    all_gather x1, waiting for transfers between devices, project_in(): lax.all_gather(weight, 'frame', axis=0, tiled=True)  46.8 us
    all_gather x2, blocking collectives, project_in(): lax.all_gather(weight, 'frame', axis=0, tiled=True)  44.9 us
    all_gather x1, waiting for transfers between devices, project_out(): lax.all_gather(weight, 'frame', axis=1, tiled=True)  42.7 us
    all_to_all x1, starting transfers between devices, per_device(): lax.all_to_all(query_rows.reshape(1, patch_count, head_width), 'frame', s...  13 us
  transfers between devices with their start and end apart: 12, of which 11 were waited for; matrix products, arithmetic and copies ran while one was open for 4% of the time, Pallas kernels for 0%

commit v1 on v0

v1 whole, which is shorter than its diff:
```python
import math

import jax
import jax.numpy as jnp
from jax import lax
from jax.sharding import PartitionSpec as P

HEAD_DIM = 72
EPS = 1e-06
FACTOR = 1.0 / math.sqrt(HEAD_DIM)


def norm_columns(values, shift, scale):
    center = values - jnp.mean(values, axis=0, keepdims=True)
    spread = jnp.mean(center * center, axis=0, keepdims=True)
    normal = center * lax.rsqrt(spread + EPS)
    return (normal * (1.0 + scale) + shift).astype(jnp.bfloat16)


def gather_head(block):
    count = lax.axis_size("head")
    copies = jnp.broadcast_to(block[None], (count,) + block.shape)
    return lax.all_to_all(copies, "head", 0, 0, tiled=True)


def swap_frames(block):
    count = lax.axis_size("frame")
    width, rows = block.shape
    inner = rows // count
    cut = block.reshape(width, count, inner).transpose(1, 0, 2).reshape(count, width * inner)
    moved = lax.all_to_all(cut, "frame", 0, 0, tiled=True)
    return moved.reshape(count, width, inner).transpose(1, 0, 2).reshape(width, rows)


def project(weight, hidden):
    return lax.dot_general(
        weight, hidden, (((0,), (0,)), ((), ())), preferred_element_type=jnp.float32
    )


def attention(mixed, mask):
    rows = mixed.shape[1]
    parts = mixed.reshape(3, -1, HEAD_DIM, rows)

    def rms(u):
        return (u * lax.rsqrt(jnp.mean(u * u, axis=1, keepdims=True) + EPS)).astype(jnp.bfloat16)

    query, key, value = rms(parts[0]), rms(parts[1]), parts[2].astype(jnp.bfloat16)
    scores = jnp.einsum("hdk,hdq->hkq", key, query, preferred_element_type=jnp.float32) * FACTOR
    weights = jnp.exp(scores)
    if mask is not None:
        weights = jnp.where(mask[None], weights, 0.0)
    weights = (weights / jnp.sum(weights, axis=1, keepdims=True)).astype(jnp.bfloat16)
    out = jnp.einsum("hdk,hkq->hdq", value, weights, preferred_element_type=jnp.float32)
    return out.astype(jnp.bfloat16).reshape(-1, rows)


def per_device(
    latents, modulation, spatial_qkv, spatial_out, temporal_qkv, temporal_out, mlp_up, mlp_down
):
    rows, width = latents.shape[1], latents.shape[2]
    heads_n, frames_n = lax.axis_size("head"), lax.axis_size("frame")
    full = width * heads_n
    place = rows // frames_n
    mine = lax.axis_index("head") * width
    depth = spatial_qkv.shape[0]
    mod = modulation.T
    col = lambda i: mod[:, i : i + 1]

    outs = jnp.stack([spatial_out.T, temporal_out.T])
    outs = gather_head(outs).transpose(1, 2, 0, 3).reshape(2, depth, full)
    t_qkv = temporal_qkv.reshape(depth, -1)
    pad = lambda a: jnp.pad(a, ((0, 0), (0, -a.shape[1] % 128)))
    pieces = [outs[0], outs[1], pad(t_qkv), pad(mlp_up), mlp_down.T]
    packed = lax.all_gather(jnp.concatenate(pieces, axis=1), "frame", axis=0, tiled=True)
    at, cuts = 0, []
    for piece, real in zip(pieces, (full, full, t_qkv.shape[1], mlp_up.shape[1], mlp_down.shape[0])):
        cuts.append(packed[:, at : at + real])
        at += piece.shape[1]
    s_out, t_out, t_qkv, w_up, w_down = cuts
    s_qkv = lax.all_gather(spatial_qkv.reshape(depth, -1), "frame", axis=0, tiled=True)

    own = latents.reshape(rows, width).T
    frame_latents = gather_head(own).reshape(full, rows).astype(jnp.float32)
    place_latents = gather_head(swap_frames(own)).reshape(full, rows)

    hidden = norm_columns(frame_latents, col(0), col(1))
    attended = attention(project(s_qkv, hidden), None)
    attended = gather_head(swap_frames(attended)).reshape(full, rows)

    branch = jnp.dot(s_out, attended, preferred_element_type=jnp.float32)
    stream = (place_latents.astype(jnp.float32) + col(2) * branch).astype(jnp.bfloat16)
    hidden = norm_columns(stream.astype(jnp.float32), col(3), col(4))
    spot = lax.broadcasted_iota(jnp.int32, (rows, rows), 0) % place
    spot_q = lax.broadcasted_iota(jnp.int32, (rows, rows), 1) % place
    attended = attention(project(t_qkv, hidden), spot == spot_q)
    attended = gather_head(attended).reshape(full, rows)

    branch = jnp.dot(t_out, attended, preferred_element_type=jnp.float32)
    stream = (stream.astype(jnp.float32) + col(5) * branch).astype(jnp.bfloat16)
    hidden = norm_columns(stream.astype(jnp.float32), col(6), col(7))
    active = jax.nn.gelu(project(w_up, hidden), approximate=True).astype(jnp.bfloat16)
    partial = jnp.dot(w_down, active, preferred_element_type=jnp.float32).astype(jnp.bfloat16)
    partial = lax.all_to_all(partial.reshape(heads_n, width, rows), "head", 0, 0, tiled=True)
    summed = jnp.sum(partial.astype(jnp.float32), axis=0)
    share = lax.dynamic_slice_in_dim(stream, mine, width, 0).astype(jnp.float32)
    gate = lax.dynamic_slice_in_dim(col(8), mine, width, 0)
    result = swap_frames((share + gate * summed).astype(jnp.bfloat16))
    return result.T.reshape(1, rows, width)


def solution(mesh):
    placed = (
        P(("dp", "frame"), None, "head"),
        P("dp", None),
        P("frame", None, "head"),
        P("head", "frame"),
        P("frame", None, "head"),
        P("head", "frame"),
        P("frame", "head"),
        P("head", "frame"),
    )
    return jax.shard_map(
        per_device,
        mesh=mesh,
        in_specs=placed,
        out_specs=P(("dp", "frame"), None, "head"),
        check_vma=False,
    )
```

time: 476 us -> 223 us (0.47)
  waiting for transfers between devices: 293 us -> 67.7 us
  blocking collectives: 92.7 us -> 70.9 us
  other arithmetic: 19.2 us -> 10.9 us
  starting transfers between devices: 23.9 us -> 29 us
    all_gather x5 -> x1, waiting for transfers between devices: 151 us -> 0.01 us  [per_device(): lax.all_gather(jnp.concatenate(pieces, axis=1), 'frame', axis=0, tiled=True)]
    reduce_scatter x3 -> x0, waiting for transfers between devices: 125 us -> none  [add_branch(): lax.psum_scatter(partial_sum.astype(jnp.bfloat16), 'head', scatter_dimens...]
    all_gather x4 -> x1, blocking collectives: 92.7 us -> 36.1 us  [per_device(): lax.all_gather(spatial_qkv.reshape(depth, -1), 'frame', axis=0, tiled=True)]
    all_to_all x4 -> x7, waiting for transfers between devices: 14.5 us -> 67.7 us  [the longest x4 38.7 us: gather_head(): return lax.all_to_all(copies, 'head', 0, 0, tiled=True)]
    all_to_all x0 -> x2, blocking collectives: none -> 34.8 us  [the longest x1 20 us: gather_head(): return lax.all_to_all(copies, 'head', 0, 0, tiled=True)]
    all_to_all x0 -> x6, other arithmetic: none -> 7.32 us  [swap_frames(): moved = lax.all_to_all(cut, 'frame', 0, 0, tiled=True)]
    unnamed x3 -> x0, other arithmetic: 6.64 us -> none
    all_to_all x4 -> x7, starting transfers between devices: 23.4 us -> 28.9 us  [the longest x4 18.5 us: gather_head(): return lax.all_to_all(copies, 'head', 0, 0, tiled=True)]
  transfers between devices with their start and end apart: 12 -> 8, of which waited for: 11 -> 6; matrix products, arithmetic and copies ran while one was open for 4% -> 8% of each run, Pallas kernels for 0% -> 0%
where the time goes in v1:
time: 223 us; the launch traced here: 222 us
  blocking collectives  70.9 us (32%)
  waiting for transfers between devices  67.7 us (30%)
  starting transfers between devices  29 us (13%)
  local copies, waits for them, and re-layouts  15 us (7%)
  matrix products  15 us (7%)
  between operations  13.9 us (6%)
  other arithmetic  10.9 us (5%)
    all_to_all x4, waiting for transfers between devices, gather_head(): return lax.all_to_all(copies, 'head', 0, 0, tiled=True)  38.7 us
    all_gather x1, blocking collectives, per_device(): lax.all_gather(spatial_qkv.reshape(depth, -1), 'frame', axis=0, tiled=True)  36.1 us
    all_to_all x1, blocking collectives, gather_head(): return lax.all_to_all(copies, 'head', 0, 0, tiled=True)  20 us
    all_to_all x4, starting transfers between devices, gather_head(): return lax.all_to_all(copies, 'head', 0, 0, tiled=True)  18.5 us
    all_to_all x1, waiting for transfers between devices, per_device(): lax.all_to_all(partial.reshape(heads_n, width, rows), 'head', 0, 0, tiled...  15.1 us
    all_to_all x1, blocking collectives, swap_frames(): moved = lax.all_to_all(cut, 'frame', 0, 0, tiled=True)  14.8 us
    all_to_all x2, waiting for transfers between devices, swap_frames(): moved = lax.all_to_all(cut, 'frame', 0, 0, tiled=True)  14 us
    all_to_all x6, other arithmetic, swap_frames(): moved = lax.all_to_all(cut, 'frame', 0, 0, tiled=True)  7.32 us
  transfers between devices with their start and end apart: 8, of which 6 were waited for; matrix products, arithmetic and copies ran while one was open for 8% of the time, Pallas kernels for 0%

profile of v1, /device:TPU:1, one launch (start us, length us, event | category | flops | bytes accessed | tf_op | source)
XLA Modules:
  0.0 222.4 jit_solution(7201325726964893687)
XLA Ops:
  6.5 0.8 pad_maximum_fusion
  7.5 0.8 broadcast_in_dim.26
  8.3 5.9 %all-to-all-start.2 = ((bf16[8,2,72,144]{3,2,1,0:T(8,128)(2,1)}), bf16[8,2,72,144]{3,2,1,0:T(8,128)(2,1)S(1)}, u32[]{:S(2)}, u32[]{:S(2)}) async-start(bf16[8,2,72,144]{3,2,1,0:T(8,128)(2,1)} %broadcast_in_dim.26), calls=%async_computation.2 | async-start | bytes 1179648 | tf_op jit(solution)/shard_map/all_to_all | solution.py:23
  14.5 7.6 %all-to-all-done.2 = bf16[8,2,72,144]{3,2,1,0:T(8,128)(2,1)S(1)} async-done(((bf16[8,2,72,144]{3,2,1,0:T(8,128)(2,1)}), bf16[8,2,72,144]{3,2,1,0:T(8,128)(2,1)S(1)}, u32[]{:S(2)}, u32[]{:S(2)}) %all-to-all-start.2) | async-done | bytes 331808 | tf_op jit(solution)/shard_map/all_to_all | solution.py:23
  23.0 0.8 copy-done
  23.9 1.1 broadcast_in_dim.27
  25.0 3.6 %all-to-all-start.3 = ((bf16[8,144,512]{2,1,0:T(8,128)(2,1)}), bf16[8,144,512]{2,1,0:T(8,128)(2,1)S(1)}, u32[]{:S(2)}, u32[]{:S(2)}) async-start(bf16[8,144,512]{2,1,0:T(8,128)(2,1)} %broadcast_in_dim.27), calls=%async_computation.3 | async-start | bytes 2359296 | tf_op jit(solution)/shard_map/all_to_all | solution.py:23
  30.2 1.5 reduce.22
  32.6 36.1 %all_gather.7 = bf16[1152,432]{1,0:T(8,128)(2,1)S(1)} all-gather(bf16[72,432]{1,0:T(8,128)(2,1)S(1)} %copy.62), channel_id=1, replica_groups=mesh['frame'=16,'head'=8,'dp'=4] {'frame'}, dimensions={0}, use_global_device_ids=true | all-gather | bytes 1057536 | tf_op jit(solution)/shard_map/all_gather | solution.py:81
  68.7 3.5 %all-to-all-start = ((bf16[16,2,2304]{2,1,0:T(2,128)(2,1)}), bf16[16,2,2304]{2,1,0:T(2,128)(2,1)S(1)}, u32[]{:S(2)}, u32[]{:S(2)}) async-start(bf16[16,2,2304]{2,1,0:T(2,128)(2,1)} %reshape.267), calls=%async_computation | async-start | bytes 294912 | tf_op jit(solution)/shard_map/all_to_all | solution.py:31
  76.2 1.6 reduce.21
  78.5 4.8 %all-to-all-done = bf16[16,2,2304]{2,1,0:T(2,128)(2,1)S(1)} async-done(((bf16[16,2,2304]{2,1,0:T(2,128)(2,1)}), bf16[16,2,2304]{2,1,0:T(2,128)(2,1)S(1)}, u32[]{:S(2)}, u32[]{:S(2)}) %all-to-all-start) | async-done | bytes 147488 | tf_op jit(solution)/shard_map/all_to_all | solution.py:31
  83.3 3.4 %all-to-all-start.4 = ((bf16[16,2,2304]{2,1,0:T(2,128)(2,1)}), bf16[16,2,2304]{2,1,0:T(2,128)(2,1)S(1)}, u32[]{:S(2)}, u32[]{:S(2)}) async-start(bf16[16,2,2304]{2,1,0:T(2,128)(2,1)} %reshape.265), calls=%async_computation.4 | async-start | bytes 294912 | tf_op jit(solution)/shard_map/all_to_all | solution.py:31
  86.8 0.9 reduce.2
  88.5 9.2 %all-to-all-done.4 = bf16[16,2,2304]{2,1,0:T(2,128)(2,1)S(1)} async-done(((bf16[16,2,2304]{2,1,0:T(2,128)(2,1)}), bf16[16,2,2304]{2,1,0:T(2,128)(2,1)S(1)}, u32[]{:S(2)}, u32[]{:S(2)}) %all-to-all-start.4) | async-done | bytes 147488 | tf_op jit(solution)/shard_map/all_to_all | solution.py:31
  97.7 1.1 broadcast_in_dim.25
  98.8 5.5 %all-to-all-start.1 = ((bf16[8,144,512]{2,1,0:T(8,128)(2,1)}), bf16[8,144,512]{2,1,0:T(8,128)(2,1)S(1)}, u32[]{:S(2)}, u32[]{:S(2)}) async-start(bf16[8,144,512]{2,1,0:T(8,128)(2,1)} %broadcast_in_dim.25), calls=%async_computation.1 | async-start | bytes 2359296 | tf_op jit(solution)/shard_map/all_to_all | solution.py:23
  104.4 0.9 reduce.6
  106.1 15.3 %all-to-all-done.1 = bf16[8,144,512]{2,1,0:T(8,128)(2,1)S(1)} async-done(((bf16[8,144,512]{2,1,0:T(8,128)(2,1)}), bf16[8,144,512]{2,1,0:T(8,128)(2,1)S(1)}, u32[]{:S(2)}, u32[]{:S(2)}) %all-to-all-start.1) | async-done | bytes 1179680 | tf_op jit(solution)/shard_map/all_to_all | solution.py:23
  121.4 1.1 broadcast_in_dim.33
  122.5 3.6 %all-to-all-start.5 = ((bf16[8,144,512]{2,1,0:T(8,128)(2,1)}), bf16[8,144,512]{2,1,0:T(8,128)(2,1)S(1)}, u32[]{:S(2)}, u32[]{:S(2)}) async-start(bf16[8,144,512]{2,1,0:T(8,128)(2,1)} %broadcast_in_dim.33), calls=%async_computation.5 | async-start | bytes 2359296 | tf_op jit(solution)/shard_map/all_to_all | solution.py:23
  126.3 15.8 %all-to-all-done.5 = bf16[8,144,512]{2,1,0:T(8,128)(2,1)S(1)} async-done(((bf16[8,144,512]{2,1,0:T(8,128)(2,1)}), bf16[8,144,512]{2,1,0:T(8,128)(2,1)S(1)}, u32[]{:S(2)}, u32[]{:S(2)}) %all-to-all-start.5) | async-done | bytes 1179680 | tf_op jit(solution)/shard_map/all_to_all | solution.py:23
  142.1 3.7 %convert_reduce_fusion = (f32[512]{0:T(512)S(1)}, bf16[1152,512]{1,0:T(8,128)(2,1)S(1)}) fusion(bf16[1152,512]{1,0:T(8,128)(2,1)S(1)} %bitcast.80, bf16[1152,4032]{1,0:T(8,128)(2,1)} %all-gather.2.cloned.1.call-done, f32[1152]{0:T(1024)S(1)} %get-tuple-element.12, bf16[1152,512]{1,0:T(8,128)(2,1)S(1)} %bitcast.79), kind=kOutput, calls=%fused_computation.2 | convolution fusion | flops 1362492928 | bytes 6199808 | tf_op jit(solution)/shard_map/dot_general | solution.py:91
  146.6 1.0 fusion.39
  149.5 20.0 %all_to_all.60 = bf16[8,144,512]{2,1,0:T(8,128)(2,1)S(1)} all-to-all(bf16[8,144,512]{2,1,0:T(8,128)(2,1)S(1)} %broadcast_in_dim.37), channel_id=1, replica_groups=mesh['frame'=16,'head'=8,'dp'=4] {'head'}, dimensions={0} | all-to-all | bytes 2359296 | tf_op jit(solution)/shard_map/all_to_all | solution.py:23
  169.5 1.8 convert_reduce_fusion.1
  171.8 5.1 %convolution_convert_fusion = bf16[1152,512]{1,0:T(8,128)(2,1)} fusion(bf16[1152,4032]{1,0:T(8,128)(2,1)} %all-gather.2.cloned.1.call-done, bf16[1152,512]{1,0:T(8,128)(2,1)S(1)} %get-tuple-element.27, f32[1152]{0:T(1024)S(1)} %get-tuple-element.6, f32[1152]{0:T(1024)S(1)} %get-tuple-element.5, f32[512]{0:T(512)S(1)} %add_rsqrt_fusion.4, ...), kind=kOutput, calls=%fused_computation.7 | convolution fusion | flops 1365737472 | bytes 5321728 | tf_op jit(solution)/shard_map/dot_general | solution.py:103
  176.8 3.6 %all-to-all-start.7 = ((bf16[8,144,512]{2,1,0:T(8,128)(2,1)}), bf16[8,144,512]{2,1,0:T(8,128)(2,1)S(1)}, u32[]{:S(2)}, u32[]{:S(2)}) async-start(bf16[8,144,512]{2,1,0:T(8,128)(2,1)} %bitcast.33), calls=%async_computation.7 | async-start | bytes 2359296 | tf_op jit(solution)/shard_map/all_to_all | solution.py:104
  180.5 15.1 %all-to-all-done.7 = bf16[8,144,512]{2,1,0:T(8,128)(2,1)S(1)} async-done(((bf16[8,144,512]{2,1,0:T(8,128)(2,1)}), bf16[8,144,512]{2,1,0:T(8,128)(2,1)S(1)}, u32[]{:S(2)}, u32[]{:S(2)}) %all-to-all-start.7) | async-done | bytes 1179680 | tf_op jit(solution)/shard_map/all_to_all | solution.py:104
  196.6 1.6 reduce.23
  198.3 14.8 %all_to_all.61 = bf16[16,2,2304]{2,1,0:T(2,128)(2,1)S(1)} all-to-all(bf16[16,2,2304]{2,1,0:T(2,128)(2,1)S(1)} %reshape.269), channel_id=1, replica_groups=mesh['frame'=16,'head'=8,'dp'=4] {'frame'}, dimensions={0} | all-to-all | bytes 294912 | tf_op jit(solution)/shard_map/all_to_all | solution.py:31
  213.2 0.9 reduce.12
  (95 shorter events, 16.1 us)
Async XLA Ops:
  6.5 7.7 %copy-start.2 = (bf16[72,3,144]{2,0,1:T(8,128)(2,1)S(1)}, bf16[72,3,144]{2,0,1:T(8,128)(2,1)}, u32[]{:S(2)}) copy-start(bf16[72,3,144]{2,0,1:T(8,128)(2,1)} %param.12) | copy-start | bytes 186628
  8.3 13.8 %all-to-all-start.2 = ((bf16[8,2,72,144]{3,2,1,0:T(8,128)(2,1)}), bf16[8,2,72,144]{3,2,1,0:T(8,128)(2,1)S(1)}, u32[]{:S(2)}, u32[]{:S(2)}) async-start(bf16[8,2,72,144]{3,2,1,0:T(8,128)(2,1)} %broadcast_in_dim.26), calls=%async_computation.2 | async-start | bytes 1179648 | tf_op jit(solution)/shard_map/all_to_all | solution.py:23
  14.2 128.0 %all-gather.2.cloned.1.call-start = ((), (), s32[]{:S(2)}) async-start(), calls=%async_computation.9 | async-start | bytes 10027008 | tf_op jit(solution)/shard_map/all_gather | solution.py:75
  14.4 8.5 %copy-start.4 = (bf16[72,576]{1,0:T(8,128)(2,1)S(1)}, bf16[72,576]{1,0:T(8,128)(2,1)}, u32[]{:S(2)}) copy-start(bf16[72,576]{1,0:T(8,128)(2,1)} %param.14) | copy-start | bytes 248836
  22.1 0.9 copy-start.5
  22.1 1.7 copy-start.1
  23.0 0.8 copy-start
  23.8 4.8 %copy-start.3 = (bf16[72,3,144]{2,0,1:T(8,128)(2,1)S(1)}, bf16[72,3,144]{2,0,1:T(8,128)(2,1)}, u32[]{:S(2)}) copy-start(bf16[72,3,144]{2,0,1:T(8,128)(2,1)} %param.10) | copy-start | bytes 186628
  25.0 43.7 %all-to-all-start.3 = ((bf16[8,144,512]{2,1,0:T(8,128)(2,1)}), bf16[8,144,512]{2,1,0:T(8,128)(2,1)S(1)}, u32[]{:S(2)}, u32[]{:S(2)}) async-start(bf16[8,144,512]{2,1,0:T(8,128)(2,1)} %broadcast_in_dim.27), calls=%async_computation.3 | async-start | bytes 2359296 | tf_op jit(solution)/shard_map/all_to_all | solution.py:23
  28.5 3.9 %copy-start.6 = (f32[9,1152]{1,0:T(8,128)S(1)}, f32[9,1152]{1,0:T(8,128)}, u32[]{:S(2)}) copy-start(f32[9,1152]{1,0:T(8,128)} %param.9) | copy-start | bytes 124420
  68.7 14.6 %all-to-all-start = ((bf16[16,2,2304]{2,1,0:T(2,128)(2,1)}), bf16[16,2,2304]{2,1,0:T(2,128)(2,1)S(1)}, u32[]{:S(2)}, u32[]{:S(2)}) async-start(bf16[16,2,2304]{2,1,0:T(2,128)(2,1)} %reshape.267), calls=%async_computation | async-start | bytes 294912 | tf_op jit(solution)/shard_map/all_to_all | solution.py:31
  83.3 14.4 %all-to-all-start.4 = ((bf16[16,2,2304]{2,1,0:T(2,128)(2,1)}), bf16[16,2,2304]{2,1,0:T(2,128)(2,1)S(1)}, u32[]{:S(2)}, u32[]{:S(2)}) async-start(bf16[16,2,2304]{2,1,0:T(2,128)(2,1)} %reshape.265), calls=%async_computation.4 | async-start | bytes 294912 | tf_op jit(solution)/shard_map/all_to_all | solution.py:31
  98.8 22.6 %all-to-all-start.1 = ((bf16[8,144,512]{2,1,0:T(8,128)(2,1)}), bf16[8,144,512]{2,1,0:T(8,128)(2,1)S(1)}, u32[]{:S(2)}, u32[]{:S(2)}) async-start(bf16[8,144,512]{2,1,0:T(8,128)(2,1)} %broadcast_in_dim.25), calls=%async_computation.1 | async-start | bytes 2359296 | tf_op jit(solution)/shard_map/all_to_all | solution.py:23
  122.5 19.7 %all-to-all-start.5 = ((bf16[8,144,512]{2,1,0:T(8,128)(2,1)}), bf16[8,144,512]{2,1,0:T(8,128)(2,1)S(1)}, u32[]{:S(2)}, u32[]{:S(2)}) async-start(bf16[8,144,512]{2,1,0:T(8,128)(2,1)} %broadcast_in_dim.33), calls=%async_computation.5 | async-start | bytes 2359296 | tf_op jit(solution)/shard_map/all_to_all | solution.py:23
  142.1 4.5 %copy-start.7 = (bf16[1152,4032]{1,0:T(8,128)(2,1)S(1)}, bf16[1152,4032]{1,0:T(8,128)(2,1)}, u32[]{:S(2)}) copy-start(bf16[1152,4032]{1,0:T(8,128)(2,1)} %all-gather.2.cloned.1.call-done) | copy-start | bytes 27869188
  176.8 18.7 %all-to-all-start.7 = ((bf16[8,144,512]{2,1,0:T(8,128)(2,1)}), bf16[8,144,512]{2,1,0:T(8,128)(2,1)S(1)}, u32[]{:S(2)}, u32[]{:S(2)}) async-start(bf16[8,144,512]{2,1,0:T(8,128)(2,1)} %bitcast.33), calls=%async_computation.7 | async-start | bytes 2359296 | tf_op jit(solution)/shard_map/all_to_all | solution.py:104
Sparse Core Ops, SparseCore 0:
  24.0 81.8 all-gather.1

commit v2 on v1

v2 whole, which is shorter than its diff:
```python
import math

import jax
import jax.numpy as jnp
from jax import lax
from jax.experimental import pallas as pl
from jax.experimental.pallas import tpu as pltpu
from jax.sharding import PartitionSpec as P

HEAD_DIM = 72
EPS = 1e-06
FACTOR = 1.0 / math.sqrt(HEAD_DIM)
LANES = 128
PLACE = 32
PARTS = LANES // PLACE
BLOCK = 144
FEATURES = 432


def project(weight, hidden):
    return lax.dot_general(
        weight, hidden, (((0,), (0,)), ((), ())), preferred_element_type=jnp.float32
    )


def lane_part(rows):
    return lax.broadcasted_iota(jnp.int32, (rows, LANES), 1) // PLACE


def pack(block, out_ref, group):
    features, rows = block.shape
    counts = [(at, min(group, features - at)) for at in range(0, features, group)]
    for tile in range(rows // LANES):
        cut = block[:, tile * LANES : (tile + 1) * LANES]
        for spot in range(PARTS):
            total = None
            for part, (at, count) in enumerate(counts):
                piece = cut[at : at + count]
                turn = (part - spot) * PLACE % LANES
                piece = pltpu.roll(piece, turn, 1) if turn else piece
                if count < group:
                    piece = jnp.concatenate([piece, jnp.zeros((group - count, LANES), piece.dtype)], 0)
                total = piece if total is None else jnp.where(lane_part(group) == part, piece, total)
            out_ref[tile * PARTS + spot] = total.astype(out_ref.dtype)


def unpack(in_ref, features, group):
    count = in_ref.shape[0]
    groups = [(at, min(group, features - at)) for at in range(0, features, group)]
    tiles = []
    for tile in range(count // PARTS):
        held = [in_ref[tile * PARTS + spot].astype(jnp.float32) for spot in range(PARTS)]
        pieces = []
        for part, (at, size) in enumerate(groups):
            total = None
            for spot in range(PARTS):
                turn = (spot - part) * PLACE % LANES
                piece = held[spot][:size]
                piece = pltpu.roll(piece, turn, 1) if turn else piece
                total = piece if total is None else jnp.where(lane_part(size) == spot, piece, total)
            pieces.append(total)
        tiles.append(jnp.concatenate(pieces, 0))
    return jnp.concatenate(tiles, 1)


def norm_heads(mixed):
    features, rows = mixed.shape
    parts = mixed.reshape(features // HEAD_DIM, HEAD_DIM, rows)
    scale = lax.rsqrt(jnp.mean(parts * parts, axis=1, keepdims=True) + EPS)
    normed = (parts * scale).reshape(features, rows)
    pairs = 2 * features // 3
    return jnp.concatenate([normed[:pairs], mixed[pairs:]], 0)


def attend(mixed, same=None):
    third = mixed.shape[0] // 3
    outs = []
    for at in range(0, third, HEAD_DIM):
        query, key, value = (mixed[at + i * third : at + i * third + HEAD_DIM] for i in range(3))
        weights = jnp.exp(project(key, query) * FACTOR)
        if same is not None:
            weights = jnp.where(same, weights, 0.0)
        weights = (weights / jnp.sum(weights, axis=0, keepdims=True)).astype(jnp.bfloat16)
        outs.append(jnp.dot(value, weights, preferred_element_type=jnp.float32))
    return jnp.concatenate(outs, 0)


def norm_rows(read, full, shift, scale, hidden_ref):
    steps = range(0, full, BLOCK)
    mean = sum(jnp.sum(read(at), axis=0, keepdims=True) for at in steps) / full
    spread = 0.0
    for at in steps:
        center = read(at) - mean
        spread += jnp.sum(center * center, axis=0, keepdims=True)
    inverse = lax.rsqrt(spread / full + EPS)
    for at in steps:
        spot = slice(at, at + BLOCK)
        normal = (read(at) - mean) * inverse
        hidden_ref[spot] = (normal * (1.0 + scale[spot]) + shift[spot]).astype(jnp.bfloat16)


def add_branch(weight, hidden, stream, gate, out_ref, whole_ref):
    for at in range(0, hidden.shape[0], BLOCK):
        spot = slice(at, at + BLOCK)
        branch = jnp.dot(weight(at), hidden, preferred_element_type=jnp.float32)
        total = (stream(at).astype(jnp.float32) + gate[spot] * branch).astype(jnp.bfloat16)
        out_ref[spot] = total
        whole_ref[spot] = total.astype(jnp.float32)


def weight_copies(weight_ref, held, sems, full, cuts):
    spots = [(pl.ds(at, BLOCK), pl.ds(0, full)) for at in range(0, full, BLOCK)]
    spots += [(pl.ds(0, full), pl.ds(at, count)) for at, count in cuts]
    copies = [
        pltpu.make_async_copy(weight_ref.at[spot], held.at[spot], sems.at[i])
        for i, spot in enumerate(spots)
    ]
    for copy in copies:
        copy.start()
    return copies


def turned_copies_kernel(in_ref, out_ref):
    turned = in_ref[...].T
    for at in range(out_ref.shape[0]):
        out_ref[at] = turned


def opening_kernel(own_ref, late_ref, mod_ref, rows_ref, mod_out_ref):
    rows, cols = own_ref.shape[1], late_ref.shape[1]
    for at in range(rows_ref.shape[0]):
        rows_ref[at, :, :rows] = own_ref[...]
        rows_ref[at, :, rows : rows + cols] = late_ref[...]
    mod_out_ref[...] = mod_ref[...].T


def spatial_kernel(
    rows_ref, weight_ref, mod_ref, up_ref, down_ref, out_ref, late_ref, hidden, up, down, sems
):
    full, rows = hidden.shape
    copies = [
        pltpu.make_async_copy(up_ref, up, sems.at[0]),
        pltpu.make_async_copy(down_ref, down, sems.at[1]),
    ]
    for copy in copies:
        copy.start()
    depth, units = up.shape
    late_ref[:, :full] = jnp.concatenate(
        [rows_ref[at, :, rows : rows + depth].T for at in range(rows_ref.shape[0])], 1
    )
    read = lambda at: rows_ref[at // BLOCK, :, :rows].astype(jnp.float32)
    norm_rows(read, full, mod_ref[:, 0:1], mod_ref[:, 1:2], hidden)
    mixed = norm_heads(project(weight_ref[...], hidden[...])).astype(jnp.bfloat16)
    block = attend(mixed).astype(out_ref.dtype)
    for at in range(out_ref.shape[0]):
        out_ref[at] = block
    for at, copy, held in zip((full, full + units + -units % LANES), copies, (up, down)):
        copy.wait()
        late_ref[:, at : at + units] = held[...]


def spatial_end_kernel(
    gathered_ref, rows_ref, weight_ref, mod_ref, mixed_ref, stream_ref, whole, hidden, held, sems
):
    full, rows = stream_ref.shape
    copies = weight_copies(weight_ref, held, sems, full, [(full, held.shape[1] - full)])

    def weight(at):
        copies[at // BLOCK].wait()
        return held[at : at + BLOCK, :full]

    add_branch(
        weight,
        gathered_ref[...].reshape(full, rows),
        lambda at: rows_ref[at // BLOCK, :, :rows],
        mod_ref[:, 2:3],
        stream_ref,
        whole,
    )
    norm_rows(lambda at: whole[at : at + BLOCK], full, mod_ref[:, 3:4], mod_ref[:, 4:5], hidden)
    copies[-1].wait()
    mixed = project(held[:, full : full + FEATURES], hidden[...])
    pack(norm_heads(mixed), mixed_ref, mixed_ref.shape[1])


def temporal_kernel(moved_ref, out_ref):
    mixed = unpack(moved_ref, FEATURES, moved_ref.shape[1]).astype(jnp.bfloat16)
    rows = mixed.shape[1]
    spot = lax.broadcasted_iota(jnp.int32, (rows, rows), 0) % PLACE
    spot_q = lax.broadcasted_iota(jnp.int32, (rows, rows), 1) % PLACE
    pack(attend(mixed, spot == spot_q), out_ref, out_ref.shape[1])


def copies_kernel(moved_ref, out_ref):
    block = unpack(moved_ref, out_ref.shape[1], moved_ref.shape[1]).astype(out_ref.dtype)
    for at in range(out_ref.shape[0]):
        out_ref[at] = block


def mlp_kernel(
    mine_ref, gathered_ref, before_ref, weight_ref, mod_ref, partial_ref, share_ref,
    stream, whole, hidden, active, held, sems,
):
    full, rows = stream.shape
    units = active.shape[0]
    down = full + units + -units % LANES
    cuts = [(full, down - full), (down, held.shape[1] - down)]
    copies = weight_copies(weight_ref, held, sems, full, cuts)

    def weight(at):
        copies[at // BLOCK].wait()
        return held[at : at + BLOCK, :full]

    add_branch(
        weight,
        gathered_ref[...].reshape(full, rows),
        lambda at: before_ref[at : at + BLOCK],
        mod_ref[:, 5:6],
        stream,
        whole,
    )
    share_ref[...] = whole[pl.ds(pl.multiple_of(mine_ref[0] * BLOCK, BLOCK), BLOCK), :]
    norm_rows(lambda at: whole[at : at + BLOCK], full, mod_ref[:, 6:7], mod_ref[:, 7:8], hidden)
    copies[-2].wait()
    raised = project(held[:, full : full + units], hidden[...])
    active[...] = jax.nn.gelu(raised, approximate=True).astype(jnp.bfloat16)
    copies[-1].wait()
    for at in range(0, full, BLOCK):
        lowered = jnp.dot(
            held[at : at + BLOCK, down : down + units], active[...], preferred_element_type=jnp.float32
        )
        partial_ref[at // BLOCK] = lowered.astype(jnp.bfloat16)


def closing_kernel(mine_ref, partial_ref, share_ref, mod_ref, out_ref):
    summed = jnp.sum(partial_ref[...].astype(jnp.float32), axis=0)
    gate = mod_ref[pl.ds(pl.multiple_of(mine_ref[0] * BLOCK, BLOCK), BLOCK), 8:9]
    out_ref[...] = (share_ref[...] + gate * summed).astype(out_ref.dtype)


HERE = pl.BlockSpec(memory_space=pltpu.VMEM)
THERE = pl.BlockSpec(memory_space=pltpu.HBM)
SCALAR = pl.BlockSpec(memory_space=pltpu.SMEM)


def vmem_call(kernel, out_shape, in_specs, scratch=(), limit=32):
    return pl.pallas_call(
        kernel,
        out_shape=out_shape,
        in_specs=in_specs,
        scratch_shapes=list(scratch),
        compiler_params=pltpu.CompilerParams(vmem_limit_bytes=limit * 2**20),
    )


def per_device(
    latents, modulation, spatial_qkv, spatial_out, temporal_qkv, temporal_out, mlp_up, mlp_down
):
    rows, width = latents.shape[1], latents.shape[2]
    heads_n, frames_n = lax.axis_size("head"), lax.axis_size("frame")
    full = width * heads_n
    depth = spatial_qkv.shape[0]
    units = mlp_up.shape[1]
    mine = lax.axis_index("head").astype(jnp.int32).reshape(1)
    array = lambda *shape, dtype=jnp.bfloat16: jax.ShapeDtypeStruct(shape, dtype)
    bf16 = lambda *shape: pltpu.VMEM(shape, jnp.bfloat16)
    f32 = lambda *shape: pltpu.VMEM(shape, jnp.float32)
    sems = lambda count: pltpu.SemaphoreType.DMA((count,))
    spread = lambda copies: lax.all_to_all(copies, "head", 0, 0, tiled=True)
    swap = lambda chunks: lax.all_to_all(chunks, "frame", 0, 0, tiled=True)
    pad = lambda a: jnp.pad(a, ((0, 0), (0, -a.shape[1] % LANES)))

    gather_frame = lambda packed: lax.all_gather(packed, "frame", axis=0, tiled=True)

    out_copies = vmem_call(turned_copies_kernel, array(heads_n, depth, width), [HERE])(spatial_out)
    row_copies, mod = vmem_call(
        opening_kernel,
        (
            array(heads_n, width, rows + LANES),
            array(full, modulation.shape[0], dtype=jnp.float32),
        ),
        [HERE] * 3,
    )(latents.reshape(rows, width).T, temporal_out, modulation)

    s_out = spread(out_copies).transpose(1, 0, 2).reshape(depth, full)
    early = gather_frame(
        jnp.concatenate([s_out, pad(temporal_qkv.reshape(depth, -1))], axis=1)
    )
    stream = spread(row_copies)
    s_qkv = gather_frame(spatial_qkv.reshape(depth, -1))

    attended, late = vmem_call(
        spatial_kernel,
        (array(heads_n, width, rows), array(depth, full + 2 * (units + -units % LANES))),
        [HERE] * 3 + [THERE] * 2,
        (bf16(full, rows), bf16(depth, units), bf16(depth, units), sems(2)),
    )(stream, s_qkv, mod, mlp_up, mlp_down.T)
    late = gather_frame(late)

    mixed, stream = vmem_call(
        spatial_end_kernel,
        (array(frames_n, 112, LANES), array(full, rows)),
        [HERE, HERE, THERE, HERE],
        (f32(full, rows), bf16(full, rows), bf16(*early.shape), sems(full // BLOCK + 1)),
        46,
    )(spread(attended), stream, early, mod)
    attended = vmem_call(temporal_kernel, array(frames_n, 48, LANES), [HERE])(swap(mixed))
    attended = vmem_call(copies_kernel, array(heads_n, width, rows), [HERE])(swap(attended))

    partial, share = vmem_call(
        mlp_kernel,
        (array(heads_n, width, rows), array(width, rows, dtype=jnp.float32)),
        [SCALAR, HERE, HERE, THERE, HERE],
        (
            bf16(full, rows), f32(full, rows), bf16(full, rows), bf16(units, rows),
            bf16(*late.shape), sems(full // BLOCK + 2),
        ),
        46,
    )(mine, spread(attended), stream, late, mod)
    result = vmem_call(closing_kernel, array(width, rows), [SCALAR, HERE, HERE, HERE])(
        mine, spread(partial), share, mod
    )
    return result.T.reshape(1, rows, width)


def solution(mesh):
    placed = (
        P(("dp", "frame"), None, "head"),
        P("dp", None),
        P("frame", None, "head"),
        P("head", "frame"),
        P("frame", None, "head"),
        P("head", "frame"),
        P("frame", "head"),
        P("head", "frame"),
    )
    return jax.shard_map(
        per_device,
        mesh=mesh,
        in_specs=placed,
        out_specs=P(("dp", "frame"), None, "head"),
        check_vma=False,
    )
```

time: 223 us -> 190 us (0.85)
  waiting for transfers between devices: 67.7 us -> 21.6 us
  blocking collectives: 70.9 us -> 113 us
  Pallas kernels: 0 us -> 22.3 us
  starting transfers between devices: 29 us -> 13.5 us
  matrix products: 15 us -> 0 us
  local copies, waits for them, and re-layouts: 15 us -> 4.41 us
  other arithmetic: 10.9 us -> 0.73 us
    all_to_all x2 -> x4, blocking collectives: 34.8 us -> 81.2 us  [the longest x2 41.7 us: per_device(): spread = lambda copies: lax.all_to_all(copies, 'head', 0, 0, tiled=True)]
    all_to_all x7 -> x3, waiting for transfers between devices: 67.7 us -> 21.5 us  [per_device(): spread = lambda copies: lax.all_to_all(copies, 'head', 0, 0, tiled=True)]
    pallas_call x0 -> x8, Pallas kernels: none -> 22.3 us  [the longest x1 7.35 us: per_device(): vmem_call(mlp_kernel, (array(heads_n, width, rows), array(width, rows, dt...]
    all_to_all x7 -> x3, starting transfers between devices: 28.9 us -> 13.4 us  [per_device(): spread = lambda copies: lax.all_to_all(copies, 'head', 0, 0, tiled=True)]
    dot_general x9 -> x0, matrix products: 15 us -> none  [the longest x1 5.09 us: per_device(): jnp.dot(w_down, active, preferred_element_type=jnp.float32)]
    all_to_all x6 -> x0, other arithmetic: 7.32 us -> none  [swap_frames(): moved = lax.all_to_all(cut, 'frame', 0, 0, tiled=True)]
    broadcast_in_dim x7 -> x0, local copies, waits for them, and re-layouts: 4.47 us -> none  [gather_head(): copies = jnp.broadcast_to(block[None], (count,) + block.shape)]
    all_gather x1, blocking collectives: 36.1 us -> 32.2 us  [per_device(): lax.all_gather(packed, 'frame', axis=0, tiled=True)]
  transfers between devices with their start and end apart: 8 -> 5, of which waited for: 6 -> 2; matrix products, arithmetic and copies ran while one was open for 8% -> 1% of each run, Pallas kernels for 0% -> 7%
where the time goes in v2:
time: 190 us
  blocking collectives  113 us (59%)
  Pallas kernels  22.3 us (12%)
  waiting for transfers between devices  21.6 us (11%)
  between operations  13.6 us (7%)
  starting transfers between devices  13.5 us (7%)
  local copies, waits for them, and re-layouts  4.41 us (2%)
    all_to_all x2, blocking collectives, per_device(): spread = lambda copies: lax.all_to_all(copies, 'head', 0, 0, tiled=True)  41.7 us
    all_to_all x2, blocking collectives, per_device(): swap = lambda chunks: lax.all_to_all(chunks, 'frame', 0, 0, tiled=True)  39.6 us
    all_gather x1, blocking collectives, per_device(): lax.all_gather(packed, 'frame', axis=0, tiled=True)  32.2 us
    all_to_all x3, waiting for transfers between devices, per_device(): spread = lambda copies: lax.all_to_all(copies, 'head', 0, 0, tiled=True)  21.5 us
    all_to_all x3, starting transfers between devices, per_device(): spread = lambda copies: lax.all_to_all(copies, 'head', 0, 0, tiled=True)  13.4 us
    pallas_call x1, Pallas kernels, per_device(): vmem_call(mlp_kernel, (array(heads_n, width, rows), array(width, rows, dt...  7.35 us
    pallas_call x1, Pallas kernels, per_device(): vmem_call(spatial_end_kernel, (array(frames_n, 112, LANES), array(full, r...  6.11 us
    unnamed x24, local copies, waits for them, and re-layouts  3.86 us
  transfers between devices with their start and end apart: 5, of which 2 were waited for; matrix products, arithmetic and copies ran while one was open for 1% of the time, Pallas kernels for 7%

profile of v2, /device:TPU:1, one launch (start us, length us, event | category | flops | bytes accessed | tf_op | source)
XLA Modules:
  0.0 189.5 jit_solution(7993689159586487737)
XLA Ops:
  6.5 0.8 copy-done.8
  7.3 0.8 shard_map.84
  8.1 5.9 %all-to-all-start.2 = ((bf16[8,72,144]{2,1,0:T(8,128)(2,1)}), bf16[8,72,144]{2,1,0:T(8,128)(2,1)S(1)}, u32[]{:S(2)}, u32[]{:S(2)}) async-start(bf16[8,72,144]{2,1,0:T(8,128)(2,1)} %shard_map.84), calls=%async_computation.2 | async-start | bytes 589824 | tf_op jit(solution)/shard_map/all_to_all | solution.py:269
  14.0 0.0 all-gather.3.cloned.1.call-start
  14.0 1.1 copy.15
  15.1 0.1 copy.16
  15.2 5.0 %all-to-all-done.2 = bf16[8,72,144]{2,1,0:T(8,128)(2,1)S(1)} async-done(((bf16[8,72,144]{2,1,0:T(8,128)(2,1)}), bf16[8,72,144]{2,1,0:T(8,128)(2,1)S(1)}, u32[]{:S(2)}, u32[]{:S(2)}) %all-to-all-start.2) | async-done | bytes 165920 | tf_op jit(solution)/shard_map/all_to_all | solution.py:269
  20.3 0.1 copy.14
  20.3 0.3 reshape.21
  20.6 0.7 fusion.1
  21.3 0.0 all-gather.3.cloned.1.call-update
  21.4 1.4 shard_map.82
  22.8 3.7 %all-to-all-start = ((bf16[8,144,640]{2,1,0:T(8,128)(2,1)}), bf16[8,144,640]{2,1,0:T(8,128)(2,1)S(1)}, u32[]{:S(2)}, u32[]{:S(2)}) async-start(bf16[8,144,640]{2,1,0:T(8,128)(2,1)} %get-tuple-element.13), calls=%async_computation | async-start | bytes 2949120 | tf_op jit(solution)/shard_map/all_to_all | solution.py:269
  26.5 0.0 all-gather.5.cloned.1.call-start
  26.6 0.2 copy.12
  26.7 0.1 copy.13
  26.8 32.2 %all_gather.9.weight_ref = bf16[1152,432]{1,0:T(8,128)(2,1)S(1)} all-gather(bf16[72,432]{1,0:T(8,128)(2,1)S(1)} %copy.13), channel_id=1, replica_groups=mesh['frame'=16,'head'=8,'dp'=4] {'frame'}, dimensions={0}, use_global_device_ids=true | all-gather | bytes 1057536 | tf_op jit(solution)/shard_map/all_gather | solution.py:273
  59.1 2.9 %shard_map.83 = (bf16[8,144,512]{2,1,0:T(8,128)(2,1)S(1)}, bf16[72,2432]{1,0:T(8,128)(2,1)S(1)}) custom-call(bf16[8,144,640]{2,1,0:T(8,128)(2,1)S(1)} %all-to-all-done.rows_ref, bf16[1152,432]{1,0:T(8,128)(2,1)S(1)} %all_gather.9.weight_ref, f32[1152,9]{1,0:T(8,128)S(1)} %get-tuple-element.14.mod_ref, bf16[72,576]{1,0:T(8,128)(2,1)S(1)} %copy-done.5, ...), custom_call_target="tpu_custom_call" | custom-call | tf_op jit(solution)/shard_map/pallas_call | solution.py:292
  62.0 1.0 copy-done.2
  63.0 0.8 copy-done.3
  63.8 0.0 all-gather.5.cloned.1.call-update
  63.8 22.0 %all_to_all.35.gathered_ref = bf16[8,144,512]{2,1,0:T(8,128)(2,1)S(1)} all-to-all(bf16[8,144,512]{2,1,0:T(8,128)(2,1)} %copy-done.2), channel_id=1, replica_groups=mesh['frame'=16,'head'=8,'dp'=4] {'head'}, dimensions={0} | all-to-all | bytes 2359296 | tf_op jit(solution)/shard_map/all_to_all | solution.py:269
  85.8 6.1 %shard_map.85 = (bf16[16,112,128]{2,1,0:T(8,128)(2,1)S(1)}, bf16[1152,512]{1,0:T(8,128)(2,1)S(1)}) custom-call(bf16[8,144,512]{2,1,0:T(8,128)(2,1)S(1)} %all_to_all.35.gathered_ref, bf16[8,144,640]{2,1,0:T(8,128)(2,1)S(1)} %all-to-all-done.rows_ref, bf16[1152,1664]{1,0:T(8,128)(2,1)} %all-gather.3.cloned.1.call-done.weight_ref, ...), custom_call_target="tpu_custom_call" | custom-call | tf_op jit(solution)/shard_map/pallas_call | solution.py:300
  91.9 25.3 %all_to_all.36.moved_ref = bf16[16,112,128]{2,1,0:T(8,128)(2,1)S(1)} all-to-all(bf16[16,112,128]{2,1,0:T(8,128)(2,1)S(1)} %get-tuple-element.16), channel_id=1, replica_groups=mesh['frame'=16,'head'=8,'dp'=4] {'frame'}, dimensions={0} | all-to-all | bytes 917504 | tf_op jit(solution)/shard_map/all_to_all | solution.py:270
  117.2 1.7 shard_map.86
  118.9 14.3 %all_to_all.37.moved_ref = bf16[16,48,128]{2,1,0:T(8,128)(2,1)S(1)} all-to-all(bf16[16,48,128]{2,1,0:T(8,128)(2,1)S(1)} %shard_map.86), channel_id=1, replica_groups=mesh['frame'=16,'head'=8,'dp'=4] {'frame'}, dimensions={0} | all-to-all | bytes 393216 | tf_op jit(solution)/shard_map/all_to_all | solution.py:270
  133.2 1.2 shard_map.87
  134.4 3.9 %all-to-all-start.5 = ((bf16[8,144,512]{2,1,0:T(8,128)(2,1)}), bf16[8,144,512]{2,1,0:T(8,128)(2,1)S(1)}, u32[]{:S(2)}, u32[]{:S(2)}) async-start(bf16[8,144,512]{2,1,0:T(8,128)(2,1)} %shard_map.87), calls=%async_computation.5 | async-start | bytes 2359296 | tf_op jit(solution)/shard_map/all_to_all | solution.py:269
  138.3 16.5 %all-to-all-done.5.gathered_ref = bf16[8,144,512]{2,1,0:T(8,128)(2,1)S(1)} async-done(((bf16[8,144,512]{2,1,0:T(8,128)(2,1)}), bf16[8,144,512]{2,1,0:T(8,128)(2,1)S(1)}, u32[]{:S(2)}, u32[]{:S(2)}) %all-to-all-start.5) | async-done | bytes 1179680 | tf_op jit(solution)/shard_map/all_to_all | solution.py:269
  154.8 7.3 %shard_map.88 = (bf16[8,144,512]{2,1,0:T(8,128)(2,1)S(1)}, f32[144,512]{1,0:T(8,128)S(1)}) custom-call(s32[1]{0:T(128)} %bitcast.mine_ref, bf16[8,144,512]{2,1,0:T(8,128)(2,1)S(1)} %all-to-all-done.5.gathered_ref, bf16[1152,512]{1,0:T(8,128)(2,1)S(1)} %copy-done.1, bf16[1152,2432]{1,0:T(8,128)(2,1)} %all-gather.5.cloned.1.call-done.weight_ref, ...), custom_call_target="tpu_custom_call" | custom-call | tf_op jit(solution)/shard_map/pallas_call | solution.py:310
  162.2 19.7 %all_to_all.38.partial_ref = bf16[8,144,512]{2,1,0:T(8,128)(2,1)S(1)} all-to-all(bf16[8,144,512]{2,1,0:T(8,128)(2,1)S(1)} %get-tuple-element.19), channel_id=1, replica_groups=mesh['frame'=16,'head'=8,'dp'=4] {'head'}, dimensions={0} | all-to-all | bytes 2359296 | tf_op jit(solution)/shard_map/all_to_all | solution.py:269
  181.9 0.8 shard_map.89
  (22 shorter events, 0.1 us)
Async XLA Ops:
  6.5 0.8 copy-start.8
  8.1 12.2 %all-to-all-start.2 = ((bf16[8,72,144]{2,1,0:T(8,128)(2,1)}), bf16[8,72,144]{2,1,0:T(8,128)(2,1)S(1)}, u32[]{:S(2)}, u32[]{:S(2)}) async-start(bf16[8,72,144]{2,1,0:T(8,128)(2,1)} %shard_map.84), calls=%async_computation.2 | async-start | bytes 589824 | tf_op jit(solution)/shard_map/all_to_all | solution.py:269
  14.0 7.4 %copy-start.4 = (bf16[1,512,144]{1,2,0:T(8,128)(2,1)S(1)}, bf16[1,512,144]{1,2,0:T(8,128)(2,1)}, u32[]{:S(2)}) copy-start(bf16[1,512,144]{1,2,0:T(8,128)(2,1)} %param.8) | copy-start | bytes 442372
  14.0 7.4 %copy-start.7 = (f32[9,1152]{1,0:T(8,128)S(1)}, f32[9,1152]{1,0:T(8,128)}, u32[]{:S(2)}) copy-start(f32[9,1152]{1,0:T(8,128)} %mod_ref.1) | copy-start | bytes 124420
  14.0 7.4 %copy-start.9 = (bf16[144,72]{1,0:T(8,128)(2,1)S(1)}, bf16[144,72]{1,0:T(8,128)(2,1)}, u32[]{:S(2)}) copy-start(bf16[144,72]{1,0:T(8,128)(2,1)} %late_ref.1) | copy-start | bytes 62212
  14.0 71.8 %all-gather.3.cloned.1.call-start = ((), (), s32[]{:S(2)}) async-start(), calls=%async_computation.7 | async-start | bytes 4073472 | tf_op jit(solution)/shard_map/all_gather | solution.py:273
  22.8 3.8 %copy-start.10 = (bf16[72,3,144]{2,0,1:T(8,128)(2,1)S(1)}, bf16[72,3,144]{2,0,1:T(8,128)(2,1)}, u32[]{:S(2)}) copy-start(bf16[72,3,144]{2,0,1:T(8,128)(2,1)} %param.10) | copy-start | bytes 186628
  22.8 36.3 %all-to-all-start = ((bf16[8,144,640]{2,1,0:T(8,128)(2,1)}), bf16[8,144,640]{2,1,0:T(8,128)(2,1)S(1)}, u32[]{:S(2)}, u32[]{:S(2)}) async-start(bf16[8,144,640]{2,1,0:T(8,128)(2,1)} %get-tuple-element.13), calls=%async_computation | async-start | bytes 2949120 | tf_op jit(solution)/shard_map/all_to_all | solution.py:269
  26.5 32.6 %copy-start.5 = (bf16[72,576]{1,0:T(8,128)(2,1)S(1)}, bf16[72,576]{1,0:T(8,128)(2,1)}, u32[]{:S(2)}) copy-start(bf16[72,576]{1,0:T(8,128)(2,1)} %up_ref.1) | copy-start | bytes 248836
  26.5 32.6 %copy-start.6 = (bf16[576,72]{0,1:T(8,128)(2,1)S(1)}, bf16[576,72]{0,1:T(8,128)(2,1)}, u32[]{:S(2)}) copy-start(bf16[576,72]{0,1:T(8,128)(2,1)} %param.15) | copy-start | bytes 248836
  26.5 128.3 %all-gather.5.cloned.1.call-start = ((), (), s32[]{:S(2)}) async-start(), calls=%async_computation.8 | async-start | bytes 5953536 | tf_op jit(solution)/shard_map/all_gather | solution.py:273
  62.0 1.1 copy-start.2
  63.0 0.8 copy-start.3
  91.9 27.0 %copy-start = (bf16[1152,512]{1,0:T(8,128)(2,1)}, bf16[1152,512]{1,0:T(8,128)(2,1)S(1)}, u32[]{:S(2)}) copy-start(bf16[1152,512]{1,0:T(8,128)(2,1)S(1)} %get-tuple-element.17.before_ref) | copy-start | bytes 3538948
  134.4 20.4 %copy-start.1 = (bf16[1152,512]{1,0:T(8,128)(2,1)S(1)}, bf16[1152,512]{1,0:T(8,128)(2,1)}, u32[]{:S(2)}) copy-start(bf16[1152,512]{1,0:T(8,128)(2,1)} %copy-done) | copy-start | bytes 3538948
  134.4 20.4 %all-to-all-start.5 = ((bf16[8,144,512]{2,1,0:T(8,128)(2,1)}), bf16[8,144,512]{2,1,0:T(8,128)(2,1)S(1)}, u32[]{:S(2)}, u32[]{:S(2)}) async-start(bf16[8,144,512]{2,1,0:T(8,128)(2,1)} %shard_map.87), calls=%async_computation.5 | async-start | bytes 2359296 | tf_op jit(solution)/shard_map/all_to_all | solution.py:269
Sparse Core Ops, SparseCore 0:
  21.5 50.6 all-gather.2
  74.3 58.6 all-gather.4

commit v3 on v2

v3 whole, which is shorter than its diff:
```python
import math

import jax
import jax.numpy as jnp
from jax import lax
from jax.experimental import pallas as pl
from jax.experimental.pallas import tpu as pltpu
from jax.sharding import PartitionSpec as P

HEAD_DIM = 72
EPS = 1e-06
FACTOR = 1.0 / math.sqrt(HEAD_DIM)
LANES = 128
SHARES = 2
PLACE = 16
PARTS = LANES // PLACE
BLOCK = 144
FEATURES = 432


def project(weight, hidden):
    return lax.dot_general(
        weight, hidden, (((0,), (0,)), ((), ())), preferred_element_type=jnp.float32
    )


def exchange(pieces):
    part = lax.broadcasted_iota(jnp.int32, pieces[0].shape, 1) // PLACE
    step = 1
    while step < PARTS:
        held = list(pieces)
        high = (part // step) % 2 == 1
        for i in range(PARTS):
            if i & step:
                continue
            low_piece, high_piece = pieces[i], pieces[i + step]
            held[i] = jnp.where(high, pltpu.roll(high_piece, step * PLACE, 1), low_piece)
            held[i + step] = jnp.where(high, high_piece, pltpu.roll(low_piece, LANES - step * PLACE, 1))
        pieces, step = held, 2 * step
    return pieces


def pack(block, out_ref, group):
    features, rows = block.shape
    if features < PARTS * group:
        block = jnp.concatenate([block, jnp.zeros((PARTS * group - features, rows), block.dtype)], 0)
    for tile in range(rows // LANES):
        cut = block[:, tile * LANES : (tile + 1) * LANES]
        pieces = [cut[at : at + group] for at in range(0, PARTS * group, group)]
        for spot, piece in enumerate(exchange(pieces)):
            out_ref[tile * PARTS + spot] = piece.astype(out_ref.dtype)


def unpack(in_ref, features):
    tiles = []
    for tile in range(in_ref.shape[0] // PARTS):
        held = [in_ref[tile * PARTS + spot].astype(jnp.float32) for spot in range(PARTS)]
        tiles.append(jnp.concatenate(exchange(held), 0)[:features])
    return jnp.concatenate(tiles, 1)


def norm_heads(mixed):
    features, rows = mixed.shape
    parts = mixed.reshape(features // HEAD_DIM, HEAD_DIM, rows)
    scale = lax.rsqrt(jnp.mean(parts * parts, axis=1, keepdims=True) + EPS)
    normed = (parts * scale).reshape(features, rows)
    pairs = 2 * features // 3
    return jnp.concatenate([normed[:pairs], mixed[pairs:]], 0)


def attend(mixed, same=None):
    third = mixed.shape[0] // 3
    outs = []
    for at in range(0, third, HEAD_DIM):
        query, key, value = (mixed[at + i * third : at + i * third + HEAD_DIM] for i in range(3))
        weights = jnp.exp(project(key, query) * FACTOR)
        if same is not None:
            weights = jnp.where(same, weights, 0.0)
        weights = (weights / jnp.sum(weights, axis=0, keepdims=True)).astype(jnp.bfloat16)
        outs.append(jnp.dot(value, weights, preferred_element_type=jnp.float32))
    return jnp.concatenate(outs, 0)


def norm_rows(read, full, shift, scale, hidden_ref):
    steps = range(0, full, BLOCK)
    mean = sum(jnp.sum(read(at), axis=0, keepdims=True) for at in steps) / full
    spread = 0.0
    for at in steps:
        center = read(at) - mean
        spread += jnp.sum(center * center, axis=0, keepdims=True)
    inverse = lax.rsqrt(spread / full + EPS)
    for at in steps:
        spot = slice(at, at + BLOCK)
        normal = (read(at) - mean) * inverse
        hidden_ref[spot] = (normal * (1.0 + scale[spot]) + shift[spot]).astype(jnp.bfloat16)


def add_branch(weight, hidden, stream, gate, out_ref, whole_ref):
    for at in range(0, hidden.shape[0], BLOCK):
        spot = slice(at, at + BLOCK)
        branch = jnp.dot(weight(at), hidden, preferred_element_type=jnp.float32)
        total = (stream(at).astype(jnp.float32) + gate[spot] * branch).astype(jnp.bfloat16)
        out_ref[spot] = total
        whole_ref[spot] = total.astype(jnp.float32)


def start_copies(pairs, sems):
    copies = [pltpu.make_async_copy(a, b, sems.at[i]) for i, (a, b) in enumerate(pairs)]
    for copy in copies:
        copy.start()
    return copies


def blocks(weight_ref, held):
    full, cols = held.shape
    spots = [pl.ds(at, BLOCK) for at in range(0, full, BLOCK)]
    return [(weight_ref.at[spot, pl.ds(0, cols)], held.at[spot]) for spot in spots]


def turned_copies_kernel(in_ref, out_ref):
    turned = in_ref[...].T
    for at in range(out_ref.shape[0]):
        out_ref[at] = turned


def side_by_side_kernel(*refs):
    out_ref, at = refs[-1], 0
    for ref in refs[:-1]:
        out_ref[:, at : at + ref.shape[1]] = ref[...]
        at += ref.shape[1]


def opening_kernel(own_ref, late_ref, mod_ref, rows_ref, mod_out_ref):
    rows, cols = own_ref.shape[1], late_ref.shape[1]
    for at in range(rows_ref.shape[0]):
        rows_ref[at, :, :rows] = own_ref[...]
        rows_ref[at, :, rows : rows + cols] = late_ref[...]
    mod_out_ref[...] = mod_ref[...].T


def spatial_kernel(rows_ref, weight_ref, mod_ref, mlp_ref, others_ref, out_ref, late_ref, hidden):
    full, rows = hidden.shape
    depth, units = late_ref.shape[0], mlp_ref.shape[1] // 2
    late_ref[:, :full] = jnp.concatenate(
        [rows_ref[at, :, rows : rows + depth].T for at in range(rows_ref.shape[0])], 1
    )
    for i in range(2):
        for j, ref in enumerate((mlp_ref, others_ref)):
            at = full + (SHARES * i + j) * units
            late_ref[:, at : at + units] = ref[:, i * units : (i + 1) * units]
    read = lambda at: rows_ref[at // BLOCK, :, :rows].astype(jnp.float32)
    norm_rows(read, full, mod_ref[:, 0:1], mod_ref[:, 1:2], hidden)
    mixed = norm_heads(project(weight_ref[...], hidden[...])).astype(jnp.bfloat16)
    block = attend(mixed).astype(out_ref.dtype)
    share = rows // SHARES
    for at in range(out_ref.shape[0]):
        first = at % SHARES * share
        out_ref[at] = block[:, first : first + share]


def spatial_end_kernel(
    spot_ref, gathered_ref, rows_ref, weight_ref, mod_ref, mixed_ref, stream_ref, whole, hidden, held, qkv, sems
):
    full, share = stream_ref.shape
    pairs = blocks(weight_ref, held) + [(weight_ref.at[:, pl.ds(full, qkv.shape[1])], qkv)]
    copies = start_copies(pairs, sems)
    mine = pl.ds(pl.multiple_of(spot_ref[1] * share, share), share)

    def weight(at):
        copies[at // BLOCK].wait()
        return held[at : at + BLOCK]

    add_branch(
        weight,
        gathered_ref[...].reshape(full, share),
        lambda at: rows_ref[at // BLOCK, :, mine],
        mod_ref[:, 2:3],
        stream_ref,
        whole,
    )
    norm_rows(lambda at: whole[at : at + BLOCK], full, mod_ref[:, 3:4], mod_ref[:, 4:5], hidden)
    copies[-1].wait()
    mixed = project(qkv[:, : SHARES * FEATURES], hidden[...])
    mixed = [norm_heads(mixed[at : at + FEATURES]) for at in range(0, SHARES * FEATURES, FEATURES)]
    pack(jnp.concatenate(mixed, 0), mixed_ref, mixed_ref.shape[1])


def temporal_kernel(moved_ref, out_ref):
    mixed = unpack(moved_ref, SHARES * FEATURES).astype(jnp.bfloat16)
    rows = mixed.shape[1]
    spot = lax.broadcasted_iota(jnp.int32, (rows, rows), 0) % PLACE
    spot_q = lax.broadcasted_iota(jnp.int32, (rows, rows), 1) % PLACE
    same = spot == spot_q
    outs = [attend(mixed[at : at + FEATURES], same) for at in range(0, SHARES * FEATURES, FEATURES)]
    pack(jnp.concatenate(outs, 0), out_ref, out_ref.shape[1])


def copies_kernel(spot_ref, moved_ref, out_ref):
    block = unpack(moved_ref, SHARES * BLOCK).astype(out_ref.dtype)
    own = pl.ds(pl.multiple_of(spot_ref[1] * BLOCK, BLOCK), BLOCK)
    other = pl.ds(pl.multiple_of((1 - spot_ref[1]) * BLOCK, BLOCK), BLOCK)
    for at in range(out_ref.shape[0]):
        out_ref[at, own, :] = block[:BLOCK]
        out_ref[at, other, :] = block[BLOCK:]


def mlp_kernel(
    spot_ref, gathered_ref, before_ref, weight_ref, mod_ref, partial_ref, stream, whole, hidden, active,
    held, up, down, sems,
):
    full, rows = stream.shape
    pairs = blocks(weight_ref, held)
    for i, ref in enumerate((up, down)):
        pairs.append((weight_ref.at[:, pl.ds(full + i * up.shape[1], up.shape[1])], ref))
    copies = start_copies(pairs, sems)

    def weight(at):
        copies[at // BLOCK].wait()
        return held[at : at + BLOCK]

    add_branch(
        weight,
        gathered_ref[...].reshape(full, rows),
        lambda at: before_ref[at : at + BLOCK],
        mod_ref[:, 5:6],
        stream,
        whole,
    )
    norm_rows(lambda at: whole[at : at + BLOCK], full, mod_ref[:, 6:7], mod_ref[:, 7:8], hidden)
    copies[-2].wait()
    raised = project(up[...], hidden[...])
    active[...] = jax.nn.gelu(raised, approximate=True).astype(jnp.bfloat16)
    copies[-1].wait()
    for i in range(full // BLOCK):
        spot = slice(i * BLOCK, (i + 1) * BLOCK)
        lowered = jnp.dot(down[spot], active[...], preferred_element_type=jnp.float32)
        carried = jnp.where(spot_ref[0] == i // SHARES, whole[spot], 0.0)
        partial_ref[i] = (carried + mod_ref[spot, 8:9] * lowered).astype(jnp.bfloat16)


def closing_kernel(partial_ref, out_ref):
    count = partial_ref.shape[0]
    for i in range(SHARES):
        share = sum(partial_ref[at].astype(jnp.float32) for at in range(i, count, SHARES))
        out_ref[:, i * share.shape[1] : (i + 1) * share.shape[1]] = share.astype(out_ref.dtype)


HERE = pl.BlockSpec(memory_space=pltpu.VMEM)
THERE = pl.BlockSpec(memory_space=pltpu.HBM)
SCALAR = pl.BlockSpec(memory_space=pltpu.SMEM)


def vmem_call(kernel, out_shape, in_specs, scratch=(), limit=32):
    return pl.pallas_call(
        kernel,
        out_shape=out_shape,
        in_specs=in_specs,
        scratch_shapes=list(scratch),
        compiler_params=pltpu.CompilerParams(vmem_limit_bytes=limit * 2**20),
    )


def per_device(
    latents, modulation, spatial_qkv, spatial_out, temporal_qkv, temporal_out, mlp_up, mlp_down
):
    rows, width = latents.shape[1], latents.shape[2]
    heads_n, frames_n = lax.axis_size("head"), lax.axis_size("frame")
    full = width * heads_n
    depth = spatial_qkv.shape[0]
    units = mlp_up.shape[1]
    lines = heads_n // SHARES
    share = rows // SHARES
    place = lax.axis_index("head").astype(jnp.int32)
    spot = jnp.stack([place // SHARES, place % SHARES])
    array = lambda *shape, dtype=jnp.bfloat16: jax.ShapeDtypeStruct(shape, dtype)
    bf16 = lambda *shape: pltpu.VMEM(shape, jnp.bfloat16)
    f32 = lambda *shape: pltpu.VMEM(shape, jnp.float32)
    sems = lambda count: pltpu.SemaphoreType.DMA((count,))
    spread = lambda copies: lax.all_to_all(copies, "head", 0, 0, tiled=True)
    swap = lambda chunks: lax.all_to_all(chunks, "frame", 0, 0, tiled=True)
    gather_frame = lambda packed: lax.all_gather(packed, "frame", axis=0, tiled=True)
    along_x = [[x * SHARES + y for x in range(lines)] for y in range(SHARES)]
    across_y = [(x * SHARES + y, x * SHARES + 1 - y) for x in range(lines) for y in range(SHARES)]
    wide_qkv = SHARES * 3 * width + -SHARES * 3 * width % LANES

    others_qkv = lax.ppermute(temporal_qkv, "head", across_y)
    out_copies = vmem_call(turned_copies_kernel, array(heads_n, depth, width), [HERE])(spatial_out)
    mlp = vmem_call(side_by_side_kernel, array(depth, 2 * units), [HERE] * 2)(mlp_up, mlp_down.T)
    others = lax.ppermute(mlp, "head", across_y)
    row_copies, mod = vmem_call(
        opening_kernel,
        (
            array(heads_n, width, rows + LANES),
            array(full, modulation.shape[0], dtype=jnp.float32),
        ),
        [HERE] * 3,
    )(latents.reshape(rows, width).T, temporal_out, modulation)

    s_out, row_copies = lax.optimization_barrier((spread(out_copies), row_copies))
    pieces = [
        s_out.transpose(1, 0, 2).reshape(depth, full),
        temporal_qkv.reshape(depth, -1),
        others_qkv.reshape(depth, -1),
        jnp.zeros((depth, -SHARES * 3 * width % LANES), jnp.bfloat16),
    ]
    early = gather_frame(jnp.concatenate(pieces, axis=1))
    stream = spread(row_copies)
    s_qkv = gather_frame(spatial_qkv.reshape(depth, -1))

    attended, late = vmem_call(
        spatial_kernel,
        (array(heads_n, width, share), array(depth, full + 2 * SHARES * units)),
        [HERE] * 5,
        (bf16(full, rows),),
    )(stream, s_qkv, mod, mlp, others)
    late = gather_frame(late)

    mixed, stream = vmem_call(
        spatial_end_kernel,
        (array(frames_n, 112, LANES), array(full, share)),
        [SCALAR, HERE, HERE, THERE, HERE],
        (
            f32(full, share), bf16(full, share), bf16(full, full), bf16(full, wide_qkv),
            sems(full // BLOCK + 1),
        ),
        46,
    )(spot, spread(attended), stream, early, mod)
    attended = vmem_call(temporal_kernel, array(frames_n, 48, LANES), [HERE])(swap(mixed))
    attended = vmem_call(copies_kernel, array(lines, SHARES * width, share), [SCALAR, HERE])(
        spot, swap(attended)
    )
    attended = lax.all_to_all(attended, "head", 0, 0, axis_index_groups=along_x, tiled=True)

    partial = vmem_call(
        mlp_kernel,
        array(heads_n, width, share),
        [SCALAR, HERE, HERE, THERE, HERE],
        (
            bf16(full, share), f32(full, share), bf16(full, share), bf16(SHARES * units, share),
            bf16(full, full), bf16(full, SHARES * units), bf16(full, SHARES * units),
            sems(full // BLOCK + 2),
        ),
        46,
    )(spot, attended, stream, late, mod)
    result = vmem_call(closing_kernel, array(width, rows), [HERE])(spread(partial))
    return result.T.reshape(1, rows, width)


def solution(mesh):
    placed = (
        P(("dp", "frame"), None, "head"),
        P("dp", None),
        P("frame", None, "head"),
        P("head", "frame"),
        P("frame", None, "head"),
        P("head", "frame"),
        P("frame", "head"),
        P("head", "frame"),
    )
    return jax.shard_map(
        per_device,
        mesh=mesh,
        in_specs=placed,
        out_specs=P(("dp", "frame"), None, "head"),
        check_vma=False,
    )
```

time: 190 us -> 181 us (0.953)
  blocking collectives: 113 us -> 102 us
  waiting for transfers between devices: 21.6 us -> 11.9 us
  starting transfers between devices: 13.5 us -> 21.1 us
  local copies, waits for them, and re-layouts: 4.41 us -> 7.85 us
    all_to_all x2 -> x1, blocking collectives: 41.7 us -> 15 us  [per_device(): spread = lambda copies: lax.all_to_all(copies, 'head', 0, 0, tiled=True)]
    all_to_all x0 -> x1, blocking collectives: none -> 12.8 us  [per_device(): lax.all_to_all(attended, 'head', 0, 0, axis_index_groups=along_x, tiled=T...]
    all_to_all x3, waiting for transfers between devices: 21.5 us -> 10.1 us  [per_device(): spread = lambda copies: lax.all_to_all(copies, 'head', 0, 0, tiled=True)]
    ppermute x0 -> x2, starting transfers between devices: none -> 6.64 us  [the longest x1 3.32 us: per_device(): others = lax.ppermute(mlp, 'head', across_y)]
    unnamed x24 -> x20, local copies, waits for them, and re-layouts: 3.86 us -> 6.19 us
    all_to_all x2, blocking collectives: 39.6 us -> 41.7 us  [per_device(): swap = lambda chunks: lax.all_to_all(chunks, 'frame', 0, 0, tiled=True)]
    pallas_call x5 -> x6, Pallas kernels: 18.4 us -> 19.6 us  [the longest x1 8.16 us: per_device(): vmem_call(mlp_kernel, array(heads_n, width, share), [SCALAR, HERE, HERE,...]
  transfers between devices with their start and end apart: 5 -> 7, of which waited for: 2 -> 2; matrix products, arithmetic and copies ran while one was open for 1% -> 1% of each run, Pallas kernels for 7% -> 8%
where the time goes in v3:
time: 181 us; the launch traced here: 180 us
  blocking collectives  102 us (56%)
  Pallas kernels  23.4 us (13%)
  starting transfers between devices  21.1 us (12%)
  between operations  13.6 us (8%)
  waiting for transfers between devices  11.9 us (7%)
  local copies, waits for them, and re-layouts  7.85 us (4%)
    all_to_all x2, blocking collectives, per_device(): swap = lambda chunks: lax.all_to_all(chunks, 'frame', 0, 0, tiled=True)  41.7 us
    all_gather x1, blocking collectives, per_device(): lax.all_gather(packed, 'frame', axis=0, tiled=True)  32.7 us
    all_to_all x1, blocking collectives, per_device(): spread = lambda copies: lax.all_to_all(copies, 'head', 0, 0, tiled=True)  15 us
    all_to_all x3, starting transfers between devices, per_device(): spread = lambda copies: lax.all_to_all(copies, 'head', 0, 0, tiled=True)  14.4 us
    all_to_all x1, blocking collectives, per_device(): lax.all_to_all(attended, 'head', 0, 0, axis_index_groups=along_x, tiled=T...  12.8 us
    all_to_all x3, waiting for transfers between devices, per_device(): spread = lambda copies: lax.all_to_all(copies, 'head', 0, 0, tiled=True)  10.1 us
    pallas_call x1, Pallas kernels, per_device(): vmem_call(mlp_kernel, array(heads_n, width, share), [SCALAR, HERE, HERE,...  8.16 us
    unnamed x20, local copies, waits for them, and re-layouts  6.19 us
  transfers between devices with their start and end apart: 7, of which 2 were waited for; matrix products, arithmetic and copies ran while one was open for 1% of the time, Pallas kernels for 8%

profile of v3, /device:TPU:1, one launch (start us, length us, event | category | flops | bytes accessed | tf_op | source)
XLA Modules:
  0.0 180.1 jit_solution(18066029369168591204)
XLA Ops:
  6.5 0.8 copy-done.6
  7.3 0.8 shard_map.82
  8.1 5.9 %all-to-all-start = ((bf16[8,72,144]{2,1,0:T(8,128)(2,1)}), bf16[8,72,144]{2,1,0:T(8,128)(2,1)S(1)}, u32[]{:S(2)}, u32[]{:S(2)}) async-start(bf16[8,72,144]{2,1,0:T(8,128)(2,1)} %shard_map.82), calls=%async_computation | async-start | bytes 589824 | tf_op jit(solution)/shard_map/all_to_all | solution.py:279
  14.0 3.3 %collective-permute-start.1 = (bf16[72,3,144]{2,0,1:T(8,128)(2,1)}, bf16[72,3,144]{2,0,1:T(8,128)(2,1)S(1)}, u32[]{:S(2)}, u32[]{:S(2)}) collective-permute-start(bf16[72,3,144]{2,0,1:T(8,128)(2,1)} %param.12), channel_id=1, source_target_pairs={{0,4},{4,0},{8,12},{12,8},{16,20},{20,16},{24,28},{28,24},{1,5},{5... | collective-permute-start | bytes 186632 | tf_op jit(solution)/shard_map/ppermute | solution.py:286
  17.3 1.1 copy.16
  18.4 0.1 copy.18
  18.5 0.9 copy-done.2
  19.4 0.9 copy-done.5
  20.3 0.8 copy-done.7
  21.1 1.4 shard_map.83
  22.5 0.2 copy.17
  22.8 0.3 reshape.20
  23.1 0.8 concatenate.3
  24.0 4.1 %all-to-all-start.1 = ((bf16[8,144,640]{2,1,0:T(8,128)(2,1)}), bf16[8,144,640]{2,1,0:T(8,128)(2,1)S(1)}, u32[]{:S(2)}, u32[]{:S(2)}) async-start(bf16[8,144,640]{2,1,0:T(8,128)(2,1)} %get-tuple-element.14), calls=%async_computation.1 | async-start | bytes 2949120 | tf_op jit(solution)/shard_map/all_to_all | solution.py:279
  28.3 3.3 %collective-permute-start = (bf16[72,1152]{1,0:T(8,128)(2,1)S(1)}, bf16[72,1152]{1,0:T(8,128)(2,1)}, u32[]{:S(2)}, u32[]{:S(2)}) collective-permute-start(bf16[72,1152]{1,0:T(8,128)(2,1)S(1)} %shard_map.84.mlp_ref), channel_id=1, source_target_pairs={{0,4},{4,0},{8,12},{12,8},{16,20},{20,16},{24,28},{28,24},{1,5},{5... | collective-permute-start | bytes 497672 | tf_op jit(solution)/shard_map/ppermute | solution.py:289
  31.6 0.2 copy.13
  31.9 32.7 %all_gather.9.weight_ref = bf16[1152,432]{1,0:T(8,128)(2,1)S(1)} all-gather(bf16[72,432]{1,0:T(8,128)(2,1)S(1)} %copy.14), channel_id=1, replica_groups=mesh['frame'=16,'head'=8,'dp'=4] {'frame'}, dimensions={0}, use_global_device_ids=true | all-gather | bytes 1057536 | tf_op jit(solution)/shard_map/all_gather | solution.py:281
  64.6 3.6 %shard_map.85 = (bf16[8,144,256]{2,1,0:T(8,128)(2,1)S(1)}, bf16[72,3456]{1,0:T(8,128)(2,1)S(1)}) custom-call(bf16[8,144,640]{2,1,0:T(8,128)(2,1)S(1)} %all-to-all-done.1.rows_ref, bf16[1152,432]{1,0:T(8,128)(2,1)S(1)} %all_gather.9.weight_ref, f32[1152,9]{1,0:T(8,128)S(1)} %get-tuple-element.15.mod_ref, bf16[72,1152]{1,0:T(8,128)(2,1)S(1)} %shard_map.84.mlp_ref, ...), custom_call_target="tpu_custom_call" | custom-call | tf_op jit(solution)/shard_map/pallas_call | solution.py:310
  68.2 0.9 copy-done
  69.0 0.8 copy-done.1
  69.8 4.5 %all-to-all-start.2 = ((bf16[8,144,256]{2,1,0:T(8,128)(2,1)}), bf16[8,144,256]{2,1,0:T(8,128)(2,1)S(1)}, u32[]{:S(2)}, u32[]{:S(2)}) async-start(bf16[8,144,256]{2,1,0:T(8,128)(2,1)} %copy-done), calls=%async_computation.2 | async-start | bytes 1179648 | tf_op jit(solution)/shard_map/all_to_all | solution.py:279
  74.4 10.1 %all-to-all-done.2.gathered_ref = bf16[8,144,256]{2,1,0:T(8,128)(2,1)S(1)} async-done(((bf16[8,144,256]{2,1,0:T(8,128)(2,1)}), bf16[8,144,256]{2,1,0:T(8,128)(2,1)S(1)}, u32[]{:S(2)}, u32[]{:S(2)}) %all-to-all-start.2) | async-done | bytes 589856 | tf_op jit(solution)/shard_map/all_to_all | solution.py:279
  84.4 6.1 %shard_map.86 = (bf16[16,112,128]{2,1,0:T(8,128)(2,1)S(1)}, bf16[1152,256]{1,0:T(8,128)(2,1)S(1)}) custom-call(s32[2]{0:T(128)S(1)} %pad_add_fusion.spot_ref, bf16[8,144,256]{2,1,0:T(8,128)(2,1)S(1)} %all-to-all-done.2.gathered_ref, bf16[8,144,640]{2,1,0:T(8,128)(2,1)S(1)} %all-to-all-done.1.rows_ref, ...), custom_call_target="tpu_custom_call" | custom-call | tf_op jit(solution)/shard_map/pallas_call | solution.py:318
  90.5 25.6 %all_to_all.35.moved_ref = bf16[16,112,128]{2,1,0:T(8,128)(2,1)S(1)} all-to-all(bf16[16,112,128]{2,1,0:T(8,128)(2,1)S(1)} %get-tuple-element.18), channel_id=1, replica_groups=mesh['frame'=16,'head'=8,'dp'=4] {'frame'}, dimensions={0} | all-to-all | bytes 917504 | tf_op jit(solution)/shard_map/all_to_all | solution.py:280
  116.2 1.7 shard_map.87
  117.8 16.0 %all_to_all.36.moved_ref = bf16[16,48,128]{2,1,0:T(8,128)(2,1)S(1)} all-to-all(bf16[16,48,128]{2,1,0:T(8,128)(2,1)S(1)} %shard_map.87), channel_id=1, replica_groups=mesh['frame'=16,'head'=8,'dp'=4] {'frame'}, dimensions={0} | all-to-all | bytes 393216 | tf_op jit(solution)/shard_map/all_to_all | solution.py:280
  133.9 0.9 shard_map.88
  134.8 12.8 %all_to_all.37.gathered_ref = bf16[4,288,256]{2,1,0:T(8,128)(2,1)S(1)} all-to-all(bf16[4,288,256]{2,1,0:T(8,128)(2,1)S(1)} %shard_map.88), channel_id=1, replica_groups={{0,8,16,24},{4,12,20,28},{1,9,17,25},{5,13,21,29},{2,10,18,26},{6,14,22..., dimensions={0} | all-to-all | bytes 1179648 | tf_op jit(solution)/shard_map/all_to_all | solution.py:332
  147.5 1.8 all-gather.5.cloned.1.call-done.weight_ref
  149.3 8.2 %shard_map.89 = bf16[8,144,256]{2,1,0:T(8,128)(2,1)S(1)} custom-call(s32[2]{0:T(128)S(1)} %pad_add_fusion.spot_ref, bf16[4,288,256]{2,1,0:T(8,128)(2,1)S(1)} %all_to_all.37.gathered_ref, bf16[1152,256]{1,0:T(8,128)(2,1)S(1)} %get-tuple-element.19.before_ref, bf16[1152,3456]{1,0:T(8,128)(2,1)} %all-gather.5.cloned.1.call-done.weight_ref, ...), custom_call_target="tpu_custom_call" | custom-call | tf_op jit(solution)/shard_map/pallas_call | solution.py:334
  157.5 15.0 %all_to_all.38.partial_ref = bf16[8,144,256]{2,1,0:T(8,128)(2,1)S(1)} all-to-all(bf16[8,144,256]{2,1,0:T(8,128)(2,1)S(1)} %shard_map.89), channel_id=1, replica_groups=mesh['frame'=16,'head'=8,'dp'=4] {'head'}, dimensions={0} | all-to-all | bytes 1179648 | tf_op jit(solution)/shard_map/all_to_all | solution.py:279
  172.5 0.7 shard_map.90
  (27 shorter events, 0.6 us)
Async XLA Ops:
  6.5 0.8 copy-start.6
  8.1 14.7 %all-to-all-start = ((bf16[8,72,144]{2,1,0:T(8,128)(2,1)}), bf16[8,72,144]{2,1,0:T(8,128)(2,1)S(1)}, u32[]{:S(2)}, u32[]{:S(2)}) async-start(bf16[8,72,144]{2,1,0:T(8,128)(2,1)} %shard_map.82), calls=%async_computation | async-start | bytes 589824 | tf_op jit(solution)/shard_map/all_to_all | solution.py:279
  13.9 70.5 %all-gather.3.cloned.1.call-start = ((), (), s32[]{:S(2)}) async-start(), calls=%async_computation.7 | async-start | bytes 5013504 | tf_op jit(solution)/shard_map/all_gather | solution.py:281
  14.0 8.5 %collective-permute-start.1 = (bf16[72,3,144]{2,0,1:T(8,128)(2,1)}, bf16[72,3,144]{2,0,1:T(8,128)(2,1)S(1)}, u32[]{:S(2)}, u32[]{:S(2)}) collective-permute-start(bf16[72,3,144]{2,0,1:T(8,128)(2,1)} %param.12), channel_id=1, source_target_pairs={{0,4},{4,0},{8,12},{12,8},{16,20},{20,16},{24,28},{28,24},{1,5},{5... | collective-permute-start | bytes 186632 | tf_op jit(solution)/shard_map/ppermute | solution.py:286
  18.5 0.9 copy-start.2
  19.4 0.9 copy-start.5
  20.3 0.8 copy-start.7
  23.9 4.2 %copy-start.3 = (bf16[72,576]{1,0:T(8,128)(2,1)S(1)}, bf16[72,576]{1,0:T(8,128)(2,1)}, u32[]{:S(2)}) copy-start(bf16[72,576]{1,0:T(8,128)(2,1)} %refs_0_.1) | copy-start | bytes 248836
  24.0 4.2 %copy-start.4 = (bf16[576,72]{0,1:T(8,128)(2,1)S(1)}, bf16[576,72]{0,1:T(8,128)(2,1)}, u32[]{:S(2)}) copy-start(bf16[576,72]{0,1:T(8,128)(2,1)} %param.15) | copy-start | bytes 248836
  24.0 7.6 %copy-start.8 = (bf16[72,3,144]{2,0,1:T(8,128)(2,1)S(1)}, bf16[72,3,144]{2,0,1:T(8,128)(2,1)}, u32[]{:S(2)}) copy-start(bf16[72,3,144]{2,0,1:T(8,128)(2,1)} %param.10) | copy-start | bytes 186628
  24.0 40.6 %all-to-all-start.1 = ((bf16[8,144,640]{2,1,0:T(8,128)(2,1)}), bf16[8,144,640]{2,1,0:T(8,128)(2,1)S(1)}, u32[]{:S(2)}, u32[]{:S(2)}) async-start(bf16[8,144,640]{2,1,0:T(8,128)(2,1)} %get-tuple-element.14), calls=%async_computation.1 | async-start | bytes 2949120 | tf_op jit(solution)/shard_map/all_to_all | solution.py:279
  28.1 121.2 %all-gather.5.cloned.1.call-start = ((), (), s32[]{:S(2)}) async-start(), calls=%async_computation.8 | async-start | bytes 8460288 | tf_op jit(solution)/shard_map/all_gather | solution.py:281
  28.3 36.3 %collective-permute-start = (bf16[72,1152]{1,0:T(8,128)(2,1)S(1)}, bf16[72,1152]{1,0:T(8,128)(2,1)}, u32[]{:S(2)}, u32[]{:S(2)}) collective-permute-start(bf16[72,1152]{1,0:T(8,128)(2,1)S(1)} %shard_map.84.mlp_ref), channel_id=1, source_target_pairs={{0,4},{4,0},{8,12},{12,8},{16,20},{20,16},{24,28},{28,24},{1,5},{5... | collective-permute-start | bytes 497672 | tf_op jit(solution)/shard_map/ppermute | solution.py:289
  68.1 0.9 copy-start
  69.0 0.8 copy-start.1
  69.8 14.6 %all-to-all-start.2 = ((bf16[8,144,256]{2,1,0:T(8,128)(2,1)}), bf16[8,144,256]{2,1,0:T(8,128)(2,1)S(1)}, u32[]{:S(2)}, u32[]{:S(2)}) async-start(bf16[8,144,256]{2,1,0:T(8,128)(2,1)} %copy-done), calls=%async_computation.2 | async-start | bytes 1179648 | tf_op jit(solution)/shard_map/all_to_all | solution.py:279
Sparse Core Ops, SparseCore 0:
  24.1 53.7 all-gather.2
  80.0 69.2 all-gather.4

commit v4 on v3

--- a/solution.py
+++ b/solution.py
@@ -15,6 +15,7 @@
 PLACE = 16
 PARTS = LANES // PLACE
 BLOCK = 144
+STEP = 576
 FEATURES = 432
 
 
@@ -96,12 +97,14 @@
 
 
 def add_branch(weight, hidden, stream, gate, out_ref, whole_ref):
-    for at in range(0, hidden.shape[0], BLOCK):
-        spot = slice(at, at + BLOCK)
+    for at in range(0, hidden.shape[0], STEP):
         branch = jnp.dot(weight(at), hidden, preferred_element_type=jnp.float32)
-        total = (stream(at).astype(jnp.float32) + gate[spot] * branch).astype(jnp.bfloat16)
-        out_ref[spot] = total
-        whole_ref[spot] = total.astype(jnp.float32)
+        for inner in range(0, STEP, BLOCK):
+            spot = slice(at + inner, at + inner + BLOCK)
+            gated = gate[spot] * branch[inner : inner + BLOCK]
+            total = (stream(at + inner).astype(jnp.float32) + gated).astype(jnp.bfloat16)
+            out_ref[spot] = total
+            whole_ref[spot] = total.astype(jnp.float32)
 
 
 def start_copies(pairs, sems):
@@ -113,7 +116,7 @@
 
 def blocks(weight_ref, held):
     full, cols = held.shape
-    spots = [pl.ds(at, BLOCK) for at in range(0, full, BLOCK)]
+    spots = [pl.ds(at, STEP) for at in range(0, full, STEP)]
     return [(weight_ref.at[spot, pl.ds(0, cols)], held.at[spot]) for spot in spots]
 
 
@@ -144,10 +147,9 @@
     late_ref[:, :full] = jnp.concatenate(
         [rows_ref[at, :, rows : rows + depth].T for at in range(rows_ref.shape[0])], 1
     )
-    for i in range(2):
-        for j, ref in enumerate((mlp_ref, others_ref)):
-            at = full + (SHARES * i + j) * units
-            late_ref[:, at : at + units] = ref[:, i * units : (i + 1) * units]
+    late_ref[:, full : full + units] = mlp_ref[:, units:]
+    late_ref[:, full + units : full + 2 * units] = others_ref[:, units:]
+    late_ref[:, full + 2 * units : full + 3 * units] = others_ref[:, :units]
     read = lambda at: rows_ref[at // BLOCK, :, :rows].astype(jnp.float32)
     norm_rows(read, full, mod_ref[:, 0:1], mod_ref[:, 1:2], hidden)
     mixed = norm_heads(project(weight_ref[...], hidden[...])).astype(jnp.bfloat16)
@@ -167,8 +169,8 @@
     mine = pl.ds(pl.multiple_of(spot_ref[1] * share, share), share)
 
     def weight(at):
-        copies[at // BLOCK].wait()
-        return held[at : at + BLOCK]
+        copies[at // STEP].wait()
+        return held[at : at + STEP]
 
     add_branch(
         weight,
@@ -205,18 +207,24 @@
 
 
 def mlp_kernel(
-    spot_ref, gathered_ref, before_ref, weight_ref, mod_ref, partial_ref, stream, whole, hidden, active,
-    held, up, down, sems,
+    spot_ref, gathered_ref, before_ref, weight_ref, early_ref, mod_ref, partial_ref, stream, whole, hidden,
+    active, held, up, down, sems,
 ):
     full, rows = stream.shape
+    units = active.shape[0] // SHARES
     pairs = blocks(weight_ref, held)
-    for i, ref in enumerate((up, down)):
-        pairs.append((weight_ref.at[:, pl.ds(full + i * up.shape[1], up.shape[1])], ref))
+    pairs.append((early_ref.at[:, pl.ds(early_ref.shape[1] - up.shape[2], up.shape[2])], up.at[0]))
+    wide = weight_ref.shape[1] - full - SHARES * units
+    pairs.append((weight_ref.at[:, pl.ds(full + SHARES * units, wide)], up.at[1, :, pl.ds(0, wide)]))
+    for at in range(0, full, STEP):
+        rows_at = pl.ds(at, STEP)
+        pairs.append((weight_ref.at[rows_at, pl.ds(full, SHARES * units)], down.at[rows_at]))
     copies = start_copies(pairs, sems)
+    first = full // STEP
 
     def weight(at):
-        copies[at // BLOCK].wait()
-        return held[at : at + BLOCK]
+        copies[at // STEP].wait()
+        return held[at : at + STEP]
 
     add_branch(
         weight,
@@ -227,15 +235,19 @@
         whole,
     )
     norm_rows(lambda at: whole[at : at + BLOCK], full, mod_ref[:, 6:7], mod_ref[:, 7:8], hidden)
-    copies[-2].wait()
-    raised = project(up[...], hidden[...])
-    active[...] = jax.nn.gelu(raised, approximate=True).astype(jnp.bfloat16)
-    copies[-1].wait()
-    for i in range(full // BLOCK):
-        spot = slice(i * BLOCK, (i + 1) * BLOCK)
-        lowered = jnp.dot(down[spot], active[...], preferred_element_type=jnp.float32)
-        carried = jnp.where(spot_ref[0] == i // SHARES, whole[spot], 0.0)
-        partial_ref[i] = (carried + mod_ref[spot, 8:9] * lowered).astype(jnp.bfloat16)
+    for i in range(SHARES):
+        copies[first + i].wait()
+        raised = project(up[i, :, :units], hidden[...])
+        active[i * units : (i + 1) * units] = jax.nn.gelu(raised, approximate=True).astype(jnp.bfloat16)
+    for i, at in enumerate(range(0, full, STEP)):
+        copies[first + SHARES + i].wait()
+        lowered = jnp.dot(down[at : at + STEP], active[...], preferred_element_type=jnp.float32)
+        for inner in range(0, STEP, BLOCK):
+            spot = slice(at + inner, at + inner + BLOCK)
+            place = (at + inner) // BLOCK
+            carried = jnp.where(spot_ref[0] == place // SHARES, whole[spot], 0.0)
+            gated = mod_ref[spot, 8:9] * lowered[inner : inner + BLOCK]
+            partial_ref[place] = (carried + gated).astype(jnp.bfloat16)
 
 
 def closing_kernel(partial_ref, out_ref):
@@ -281,6 +293,7 @@
     gather_frame = lambda packed: lax.all_gather(packed, "frame", axis=0, tiled=True)
     along_x = [[x * SHARES + y for x in range(lines)] for y in range(SHARES)]
     across_y = [(x * SHARES + y, x * SHARES + 1 - y) for x in range(lines) for y in range(SHARES)]
+    pad = lambda a: jnp.pad(a, ((0, 0), (0, -a.shape[1] % LANES)))
     wide_qkv = SHARES * 3 * width + -SHARES * 3 * width % LANES
 
     others_qkv = lax.ppermute(temporal_qkv, "head", across_y)
@@ -294,14 +307,15 @@
             array(full, modulation.shape[0], dtype=jnp.float32),
         ),
         [HERE] * 3,
+        limit=60,
     )(latents.reshape(rows, width).T, temporal_out, modulation)
 
-    s_out, row_copies = lax.optimization_barrier((spread(out_copies), row_copies))
     pieces = [
-        s_out.transpose(1, 0, 2).reshape(depth, full),
+        spread(out_copies).transpose(1, 0, 2).reshape(depth, full),
         temporal_qkv.reshape(depth, -1),
         others_qkv.reshape(depth, -1),
         jnp.zeros((depth, -SHARES * 3 * width % LANES), jnp.bfloat16),
+        pad(mlp_up),
     ]
     early = gather_frame(jnp.concatenate(pieces, axis=1))
     stream = spread(row_copies)
@@ -309,7 +323,7 @@
 
     attended, late = vmem_call(
         spatial_kernel,
-        (array(heads_n, width, share), array(depth, full + 2 * SHARES * units)),
+        (array(heads_n, width, share), array(depth, full + 3 * units + -units % LANES)),
         [HERE] * 5,
         (bf16(full, rows),),
     )(stream, s_qkv, mod, mlp, others)
@@ -321,7 +335,7 @@
         [SCALAR, HERE, HERE, THERE, HERE],
         (
             f32(full, share), bf16(full, share), bf16(full, full), bf16(full, wide_qkv),
-            sems(full // BLOCK + 1),
+            sems(full // STEP + 1),
         ),
         46,
     )(spot, spread(attended), stream, early, mod)
@@ -334,14 +348,14 @@
     partial = vmem_call(
         mlp_kernel,
         array(heads_n, width, share),
-        [SCALAR, HERE, HERE, THERE, HERE],
+        [SCALAR, HERE, HERE, THERE, THERE, HERE],
         (
             bf16(full, share), f32(full, share), bf16(full, share), bf16(SHARES * units, share),
-            bf16(full, full), bf16(full, SHARES * units), bf16(full, SHARES * units),
-            sems(full // BLOCK + 2),
+            bf16(full, full), bf16(SHARES, full, units + -units % LANES), bf16(full, SHARES * units),
+            sems(2 * full // STEP + 2),
         ),
         46,
-    )(spot, attended, stream, late, mod)
+    )(spot, attended, stream, late, early, mod)
     result = vmem_call(closing_kernel, array(width, rows), [HERE])(spread(partial))
     return result.T.reshape(1, rows, width)
 

time: 181 us -> 178 us (0.983)
  blocking collectives: 102 us -> 100 us
    all_to_all x1, blocking collectives: 15 us -> 12.2 us  [per_device(): spread = lambda copies: lax.all_to_all(copies, 'head', 0, 0, tiled=True)]
    unnamed x20 -> x16, local copies, waits for them, and re-layouts: 6.19 us -> 3.6 us
  transfers between devices with their start and end apart: 7 -> 7, of which waited for: 2 -> 3; matrix products, arithmetic and copies ran while one was open for 1% -> 2% of each run, Pallas kernels for 8% -> 8%
where the time goes in v4:
time: 178 us; the launch traced here: 177 us
  blocking collectives  100 us (56%)
  Pallas kernels  23.6 us (13%)
  starting transfers between devices  22.4 us (13%)
  between operations  13.6 us (8%)
  waiting for transfers between devices  10.7 us (6%)
  local copies, waits for them, and re-layouts  6.18 us (3%)
    all_to_all x2, blocking collectives, per_device(): swap = lambda chunks: lax.all_to_all(chunks, 'frame', 0, 0, tiled=True)  41.2 us
    all_gather x1, blocking collectives, per_device(): lax.all_gather(packed, 'frame', axis=0, tiled=True)  34.4 us
    all_to_all x3, starting transfers between devices, per_device(): spread = lambda copies: lax.all_to_all(copies, 'head', 0, 0, tiled=True)  15.6 us
    all_to_all x1, blocking collectives, per_device(): lax.all_to_all(attended, 'head', 0, 0, axis_index_groups=along_x, tiled=T...  12.7 us
    all_to_all x1, blocking collectives, per_device(): spread = lambda copies: lax.all_to_all(copies, 'head', 0, 0, tiled=True)  12.2 us
    all_to_all x3, waiting for transfers between devices, per_device(): spread = lambda copies: lax.all_to_all(copies, 'head', 0, 0, tiled=True)  10.4 us
    pallas_call x1, Pallas kernels, per_device(): vmem_call(mlp_kernel, array(heads_n, width, share), [SCALAR, HERE, HERE,...  7.86 us
    pallas_call x1, Pallas kernels, per_device(): vmem_call(spatial_end_kernel, (array(frames_n, 112, LANES), array(full, s...  5.47 us
  transfers between devices with their start and end apart: 7, of which 3 were waited for; matrix products, arithmetic and copies ran while one was open for 2% of the time, Pallas kernels for 8%

profile of v4, /device:TPU:1, one launch (start us, length us, event | category | flops | bytes accessed | tf_op | source)
XLA Modules:
  0.0 177.0 jit_solution(6765226242279580673)
XLA Ops:
  6.5 0.8 copy-done.5
  7.3 0.8 shard_map.85
  8.1 5.9 %all-to-all-start.2 = ((bf16[8,72,144]{2,1,0:T(8,128)(2,1)}), bf16[8,72,144]{2,1,0:T(8,128)(2,1)S(1)}, u32[]{:S(2)}, u32[]{:S(2)}) async-start(bf16[8,72,144]{2,1,0:T(8,128)(2,1)} %shard_map.85), calls=%async_computation.2 | async-start | bytes 589824 | tf_op jit(solution)/shard_map/all_to_all | solution.py:291
  14.0 3.3 %collective-permute-start.1 = (bf16[72,3,144]{2,0,1:T(8,128)(2,1)}, bf16[72,3,144]{2,0,1:T(8,128)(2,1)S(1)}, u32[]{:S(2)}, u32[]{:S(2)}) collective-permute-start(bf16[72,3,144]{2,0,1:T(8,128)(2,1)} %param.12), channel_id=1, source_target_pairs={{0,4},{4,0},{8,12},{12,8},{16,20},{20,16},{24,28},{28,24},{1,5},{5... | collective-permute-start | bytes 186632 | tf_op jit(solution)/shard_map/ppermute | solution.py:299
  17.3 1.1 copy.16
  18.4 0.1 copy.18
  18.5 0.9 pad.4
  19.4 0.3 collective-permute-done.1
  19.7 0.2 copy.17
  20.0 0.3 all-to-all-done.2
  20.3 0.3 reshape.20
  20.6 0.9 concatenate.3
  21.5 2.5 %shard_map.82 = (bf16[8,144,640]{2,1,0:T(8,128)(2,1)}, f32[1152,9]{1,0:T(8,128)}) custom-call(bf16[144,512]{1,0:T(8,128)(2,1)} %bitcast.18, bf16[144,72]{1,0:T(8,128)(2,1)} %late_ref.1, f32[9,1152]{1,0:T(8,128)} %mod_ref.1), custom_call_target="tpu_custom_call" | custom-call | tf_op jit(solution)/shard_map/pallas_call | solution.py:303
  24.1 5.0 %all-to-all-start = ((bf16[8,144,640]{2,1,0:T(8,128)(2,1)}), bf16[8,144,640]{2,1,0:T(8,128)(2,1)S(1)}, u32[]{:S(2)}, u32[]{:S(2)}) async-start(bf16[8,144,640]{2,1,0:T(8,128)(2,1)} %get-tuple-element.11), calls=%async_computation | async-start | bytes 2949120 | tf_op jit(solution)/shard_map/all_to_all | solution.py:291
  29.2 3.4 %collective-permute-start = (bf16[72,1152]{1,0:T(8,128)(2,1)S(1)}, bf16[72,1152]{1,0:T(8,128)(2,1)}, u32[]{:S(2)}, u32[]{:S(2)}) collective-permute-start(bf16[72,1152]{1,0:T(8,128)(2,1)S(1)} %shard_map.83.mlp_ref), channel_id=1, source_target_pairs={{0,4},{4,0},{8,12},{12,8},{16,20},{20,16},{24,28},{28,24},{1,5},{5... | collective-permute-start | bytes 497672 | tf_op jit(solution)/shard_map/ppermute | solution.py:302
  32.7 0.2 copy.13
  32.8 0.1 copy.14
  32.9 34.4 %all_gather.9.weight_ref = bf16[1152,432]{1,0:T(8,128)(2,1)S(1)} all-gather(bf16[72,432]{1,0:T(8,128)(2,1)S(1)} %copy.14), channel_id=1, replica_groups=mesh['frame'=16,'head'=8,'dp'=4] {'frame'}, dimensions={0}, use_global_device_ids=true | all-gather | bytes 1057536 | tf_op jit(solution)/shard_map/all_gather | solution.py:293
  67.3 3.6 %shard_map.84 = (bf16[8,144,256]{2,1,0:T(8,128)(2,1)S(1)}, bf16[72,2944]{1,0:T(8,128)(2,1)S(1)}) custom-call(bf16[8,144,640]{2,1,0:T(8,128)(2,1)S(1)} %all-to-all-done.rows_ref, bf16[1152,432]{1,0:T(8,128)(2,1)S(1)} %all_gather.9.weight_ref, f32[1152,9]{1,0:T(8,128)S(1)} %copy-done, bf16[72,1152]{1,0:T(8,128)(2,1)S(1)} %shard_map.83.mlp_ref, ...), custom_call_target="tpu_custom_call" | custom-call | tf_op jit(solution)/shard_map/pallas_call | solution.py:324
  70.9 0.8 copy-done.1
  71.7 0.8 copy-done.2
  72.5 4.7 %all-to-all-start.1 = ((bf16[8,144,256]{2,1,0:T(8,128)(2,1)}), bf16[8,144,256]{2,1,0:T(8,128)(2,1)S(1)}, u32[]{:S(2)}, u32[]{:S(2)}) async-start(bf16[8,144,256]{2,1,0:T(8,128)(2,1)} %copy-done.1), calls=%async_computation.1 | async-start | bytes 1179648 | tf_op jit(solution)/shard_map/all_to_all | solution.py:291
  77.3 10.1 %all-to-all-done.1.gathered_ref = bf16[8,144,256]{2,1,0:T(8,128)(2,1)S(1)} async-done(((bf16[8,144,256]{2,1,0:T(8,128)(2,1)}), bf16[8,144,256]{2,1,0:T(8,128)(2,1)S(1)}, u32[]{:S(2)}, u32[]{:S(2)}) %all-to-all-start.1) | async-done | bytes 589856 | tf_op jit(solution)/shard_map/all_to_all | solution.py:291
  87.4 5.5 %shard_map.86 = (bf16[16,112,128]{2,1,0:T(8,128)(2,1)S(1)}, bf16[1152,256]{1,0:T(8,128)(2,1)S(1)}) custom-call(s32[2]{0:T(128)S(1)} %pad_add_fusion.spot_ref, bf16[8,144,256]{2,1,0:T(8,128)(2,1)S(1)} %all-to-all-done.1.gathered_ref, bf16[8,144,640]{2,1,0:T(8,128)(2,1)S(1)} %all-to-all-done.rows_ref, ...), custom_call_target="tpu_custom_call" | custom-call | tf_op jit(solution)/shard_map/pallas_call | solution.py:332
  92.9 25.2 %all_to_all.35.moved_ref = bf16[16,112,128]{2,1,0:T(8,128)(2,1)S(1)} all-to-all(bf16[16,112,128]{2,1,0:T(8,128)(2,1)S(1)} %get-tuple-element.14), channel_id=1, replica_groups=mesh['frame'=16,'head'=8,'dp'=4] {'frame'}, dimensions={0} | all-to-all | bytes 917504 | tf_op jit(solution)/shard_map/all_to_all | solution.py:292
  118.2 1.7 shard_map.87
  119.8 16.0 %all_to_all.36.moved_ref = bf16[16,48,128]{2,1,0:T(8,128)(2,1)S(1)} all-to-all(bf16[16,48,128]{2,1,0:T(8,128)(2,1)S(1)} %shard_map.87), channel_id=1, replica_groups=mesh['frame'=16,'head'=8,'dp'=4] {'frame'}, dimensions={0} | all-to-all | bytes 393216 | tf_op jit(solution)/shard_map/all_to_all | solution.py:292
  135.8 0.9 shard_map.88
  136.7 12.7 %all_to_all.37.gathered_ref = bf16[4,288,256]{2,1,0:T(8,128)(2,1)S(1)} all-to-all(bf16[4,288,256]{2,1,0:T(8,128)(2,1)S(1)} %shard_map.88), channel_id=1, replica_groups={{0,8,16,24},{4,12,20,28},{1,9,17,25},{5,13,21,29},{2,10,18,26},{6,14,22..., dimensions={0} | all-to-all | bytes 1179648 | tf_op jit(solution)/shard_map/all_to_all | solution.py:346
  149.4 7.9 %shard_map.89 = bf16[8,144,256]{2,1,0:T(8,128)(2,1)S(1)} custom-call(s32[2]{0:T(128)S(1)} %pad_add_fusion.spot_ref, bf16[4,288,256]{2,1,0:T(8,128)(2,1)S(1)} %all_to_all.37.gathered_ref, bf16[1152,256]{1,0:T(8,128)(2,1)S(1)} %get-tuple-element.15.before_ref, bf16[1152,2944]{1,0:T(8,128)(2,1)} %all-gather.5.cloned.1.call-done.weight_ref, ...), custom_call_target="tpu_custom_call" | custom-call | tf_op jit(solution)/shard_map/pallas_call | solution.py:348
  157.3 12.2 %all_to_all.38.partial_ref = bf16[8,144,256]{2,1,0:T(8,128)(2,1)S(1)} all-to-all(bf16[8,144,256]{2,1,0:T(8,128)(2,1)S(1)} %shard_map.89), channel_id=1, replica_groups=mesh['frame'=16,'head'=8,'dp'=4] {'head'}, dimensions={0} | all-to-all | bytes 1179648 | tf_op jit(solution)/shard_map/all_to_all | solution.py:291
  169.4 0.7 shard_map.90
  (24 shorter events, 0.5 us)
Async XLA Ops:
  6.5 0.8 copy-start.5
  8.1 12.2 %all-to-all-start.2 = ((bf16[8,72,144]{2,1,0:T(8,128)(2,1)}), bf16[8,72,144]{2,1,0:T(8,128)(2,1)S(1)}, u32[]{:S(2)}, u32[]{:S(2)}) async-start(bf16[8,72,144]{2,1,0:T(8,128)(2,1)} %shard_map.85), calls=%async_computation.2 | async-start | bytes 589824 | tf_op jit(solution)/shard_map/all_to_all | solution.py:291
  14.0 73.5 %all-gather.3.cloned.1.call-start = ((), (), s32[]{:S(2)}) async-start(), calls=%async_computation.7 | async-start | bytes 6580224 | tf_op jit(solution)/shard_map/all_gather | solution.py:293
  14.0 5.7 %collective-permute-start.1 = (bf16[72,3,144]{2,0,1:T(8,128)(2,1)}, bf16[72,3,144]{2,0,1:T(8,128)(2,1)S(1)}, u32[]{:S(2)}, u32[]{:S(2)}) collective-permute-start(bf16[72,3,144]{2,0,1:T(8,128)(2,1)} %param.12), channel_id=1, source_target_pairs={{0,4},{4,0},{8,12},{12,8},{16,20},{20,16},{24,28},{28,24},{1,5},{5... | collective-permute-start | bytes 186632 | tf_op jit(solution)/shard_map/ppermute | solution.py:299
  24.0 5.0 %copy-start.3 = (bf16[72,576]{1,0:T(8,128)(2,1)S(1)}, bf16[72,576]{1,0:T(8,128)(2,1)}, u32[]{:S(2)}) copy-start(bf16[72,576]{1,0:T(8,128)(2,1)} %refs_0_.1) | copy-start | bytes 248836
  24.0 5.0 %copy-start.4 = (bf16[576,72]{0,1:T(8,128)(2,1)S(1)}, bf16[576,72]{0,1:T(8,128)(2,1)}, u32[]{:S(2)}) copy-start(bf16[576,72]{0,1:T(8,128)(2,1)} %param.15) | copy-start | bytes 248836
  24.0 8.6 %copy-start.6 = (bf16[72,3,144]{2,0,1:T(8,128)(2,1)S(1)}, bf16[72,3,144]{2,0,1:T(8,128)(2,1)}, u32[]{:S(2)}) copy-start(bf16[72,3,144]{2,0,1:T(8,128)(2,1)} %param.10) | copy-start | bytes 186628
  24.1 43.3 %all-to-all-start = ((bf16[8,144,640]{2,1,0:T(8,128)(2,1)}), bf16[8,144,640]{2,1,0:T(8,128)(2,1)S(1)}, u32[]{:S(2)}, u32[]{:S(2)}) async-start(bf16[8,144,640]{2,1,0:T(8,128)(2,1)} %get-tuple-element.11), calls=%async_computation | async-start | bytes 2949120 | tf_op jit(solution)/shard_map/all_to_all | solution.py:291
  29.0 38.3 %copy-start = (f32[1152,9]{1,0:T(8,128)S(1)}, f32[1152,9]{1,0:T(8,128)}, u32[]{:S(2)}) copy-start(f32[1152,9]{1,0:T(8,128)} %get-tuple-element.12.mod_ref) | copy-start | bytes 124420
  29.0 120.4 %all-gather.5.cloned.1.call-start = ((), (), s32[]{:S(2)}) async-start(), calls=%async_computation.8 | async-start | bytes 7206912 | tf_op jit(solution)/shard_map/all_gather | solution.py:293
  29.2 38.1 %collective-permute-start = (bf16[72,1152]{1,0:T(8,128)(2,1)S(1)}, bf16[72,1152]{1,0:T(8,128)(2,1)}, u32[]{:S(2)}, u32[]{:S(2)}) collective-permute-start(bf16[72,1152]{1,0:T(8,128)(2,1)S(1)} %shard_map.83.mlp_ref), channel_id=1, source_target_pairs={{0,4},{4,0},{8,12},{12,8},{16,20},{20,16},{24,28},{28,24},{1,5},{5... | collective-permute-start | bytes 497672 | tf_op jit(solution)/shard_map/ppermute | solution.py:302
  70.9 0.8 copy-start.1
  71.7 0.8 copy-start.2
  72.5 14.9 %all-to-all-start.1 = ((bf16[8,144,256]{2,1,0:T(8,128)(2,1)}), bf16[8,144,256]{2,1,0:T(8,128)(2,1)S(1)}, u32[]{:S(2)}, u32[]{:S(2)}) async-start(bf16[8,144,256]{2,1,0:T(8,128)(2,1)} %copy-done.1), calls=%async_computation.1 | async-start | bytes 1179648 | tf_op jit(solution)/shard_map/all_to_all | solution.py:291
Sparse Core Ops, SparseCore 0:
  21.6 61.5 all-gather.2
  85.4 62.7 all-gather.4

commit v5 on v4

--- a/solution.py
+++ b/solution.py
@@ -16,6 +16,7 @@
 PARTS = LANES // PLACE
 BLOCK = 144
 STEP = 576
+UNITS = 512
 FEATURES = 432
 
 
@@ -141,15 +142,15 @@
     mod_out_ref[...] = mod_ref[...].T
 
 
-def spatial_kernel(rows_ref, weight_ref, mod_ref, mlp_ref, others_ref, out_ref, late_ref, hidden):
+def late_weights_kernel(rows_ref, mlp_ref, others_ref, out_ref):
+    depth, units = mlp_ref.shape[0], mlp_ref.shape[1] // 2
+    turned = [rows_ref[at, :, :depth].T for at in range(rows_ref.shape[0])]
+    pieces = turned + [mlp_ref[:, units:], others_ref[:, units:], mlp_ref[:, UNITS:units], others_ref[:, :units]]
+    out_ref[...] = jnp.concatenate(pieces, 1)
+
+
+def spatial_kernel(rows_ref, weight_ref, mod_ref, out_ref, hidden):
     full, rows = hidden.shape
-    depth, units = late_ref.shape[0], mlp_ref.shape[1] // 2
-    late_ref[:, :full] = jnp.concatenate(
-        [rows_ref[at, :, rows : rows + depth].T for at in range(rows_ref.shape[0])], 1
-    )
-    late_ref[:, full : full + units] = mlp_ref[:, units:]
-    late_ref[:, full + units : full + 2 * units] = others_ref[:, units:]
-    late_ref[:, full + 2 * units : full + 3 * units] = others_ref[:, :units]
     read = lambda at: rows_ref[at // BLOCK, :, :rows].astype(jnp.float32)
     norm_rows(read, full, mod_ref[:, 0:1], mod_ref[:, 1:2], hidden)
     mixed = norm_heads(project(weight_ref[...], hidden[...])).astype(jnp.bfloat16)
@@ -211,14 +212,15 @@
     active, held, up, down, sems,
 ):
     full, rows = stream.shape
-    units = active.shape[0] // SHARES
+    units = active.shape[0]
+    cuts = [(0, UNITS), (UNITS, units - UNITS)]
     pairs = blocks(weight_ref, held)
-    pairs.append((early_ref.at[:, pl.ds(early_ref.shape[1] - up.shape[2], up.shape[2])], up.at[0]))
-    wide = weight_ref.shape[1] - full - SHARES * units
-    pairs.append((weight_ref.at[:, pl.ds(full + SHARES * units, wide)], up.at[1, :, pl.ds(0, wide)]))
+    pairs.append((early_ref.at[:, pl.ds(early_ref.shape[1] - UNITS, UNITS)], up.at[:, pl.ds(0, UNITS)]))
+    rest = units - UNITS
+    pairs.append((weight_ref.at[:, pl.ds(full + units, rest)], up.at[:, pl.ds(UNITS, rest)]))
     for at in range(0, full, STEP):
         rows_at = pl.ds(at, STEP)
-        pairs.append((weight_ref.at[rows_at, pl.ds(full, SHARES * units)], down.at[rows_at]))
+        pairs.append((weight_ref.at[rows_at, pl.ds(full, units)], down.at[rows_at]))
     copies = start_copies(pairs, sems)
     first = full // STEP
 
@@ -235,12 +237,12 @@
         whole,
     )
     norm_rows(lambda at: whole[at : at + BLOCK], full, mod_ref[:, 6:7], mod_ref[:, 7:8], hidden)
-    for i in range(SHARES):
+    for i, (at, count) in enumerate(cuts):
         copies[first + i].wait()
-        raised = project(up[i, :, :units], hidden[...])
-        active[i * units : (i + 1) * units] = jax.nn.gelu(raised, approximate=True).astype(jnp.bfloat16)
+        raised = project(up[:, at : at + count], hidden[...])
+        active[at : at + count] = jax.nn.gelu(raised, approximate=True).astype(jnp.bfloat16)
     for i, at in enumerate(range(0, full, STEP)):
-        copies[first + SHARES + i].wait()
+        copies[first + len(cuts) + i].wait()
         lowered = jnp.dot(down[at : at + STEP], active[...], preferred_element_type=jnp.float32)
         for inner in range(0, STEP, BLOCK):
             spot = slice(at + inner, at + inner + BLOCK)
@@ -293,7 +295,6 @@
     gather_frame = lambda packed: lax.all_gather(packed, "frame", axis=0, tiled=True)
     along_x = [[x * SHARES + y for x in range(lines)] for y in range(SHARES)]
     across_y = [(x * SHARES + y, x * SHARES + 1 - y) for x in range(lines) for y in range(SHARES)]
-    pad = lambda a: jnp.pad(a, ((0, 0), (0, -a.shape[1] % LANES)))
     wide_qkv = SHARES * 3 * width + -SHARES * 3 * width % LANES
 
     others_qkv = lax.ppermute(temporal_qkv, "head", across_y)
@@ -307,7 +308,6 @@
             array(full, modulation.shape[0], dtype=jnp.float32),
         ),
         [HERE] * 3,
-        limit=60,
     )(latents.reshape(rows, width).T, temporal_out, modulation)
 
     pieces = [
@@ -315,18 +315,19 @@
         temporal_qkv.reshape(depth, -1),
         others_qkv.reshape(depth, -1),
         jnp.zeros((depth, -SHARES * 3 * width % LANES), jnp.bfloat16),
-        pad(mlp_up),
+        mlp_up[:, :UNITS],
     ]
     early = gather_frame(jnp.concatenate(pieces, axis=1))
     stream = spread(row_copies)
     s_qkv = gather_frame(spatial_qkv.reshape(depth, -1))
 
-    attended, late = vmem_call(
-        spatial_kernel,
-        (array(heads_n, width, share), array(depth, full + 3 * units + -units % LANES)),
-        [HERE] * 5,
-        (bf16(full, rows),),
-    )(stream, s_qkv, mod, mlp, others)
+    attended = vmem_call(
+        spatial_kernel, array(heads_n, width, share), [HERE] * 3, (bf16(full, rows),)
+    )(stream, s_qkv, mod)
+    t_out, attended = lax.optimization_barrier((stream[:, :, rows:], attended))
+    late = vmem_call(
+        late_weights_kernel, array(depth, full + 2 * SHARES * units - UNITS), [HERE] * 3
+    )(t_out, mlp, others)
     late = gather_frame(late)
 
     mixed, stream = vmem_call(
@@ -351,10 +352,10 @@
         [SCALAR, HERE, HERE, THERE, THERE, HERE],
         (
             bf16(full, share), f32(full, share), bf16(full, share), bf16(SHARES * units, share),
-            bf16(full, full), bf16(SHARES, full, units + -units % LANES), bf16(full, SHARES * units),
+            bf16(full, full), bf16(full, SHARES * units), bf16(full, SHARES * units),
             sems(2 * full // STEP + 2),
         ),
-        46,
+        50,
     )(spot, attended, stream, late, early, mod)
     result = vmem_call(closing_kernel, array(width, rows), [HERE])(spread(partial))
     return result.T.reshape(1, rows, width)

time: 178 us -> 178 us (level)
    pallas_call x1 -> x2, Pallas kernels: 3.55 us -> 4.57 us  [the longest x1 2.59 us: per_device(): vmem_call(spatial_kernel, array(heads_n, width, share), [HERE] * 3, (bf16...]
    unnamed x16 -> x18, local copies, waits for them, and re-layouts: 3.6 us -> 2.91 us
  transfers between devices with their start and end apart: 7 -> 7, of which waited for: 3 -> 3; matrix products, arithmetic and copies ran while one was open for 2% -> 1% of each run, Pallas kernels for 8% -> 8%
where the time goes in v5:
time: 178 us; the launch traced here: 176 us
  blocking collectives  100 us (56%)
  Pallas kernels  23.4 us (13%)
  starting transfers between devices  22.6 us (13%)
  between operations  13.6 us (8%)
  waiting for transfers between devices  11.6 us (7%)
  local copies, waits for them, and re-layouts  4.63 us (3%)
    all_to_all x2, blocking collectives, per_device(): swap = lambda chunks: lax.all_to_all(chunks, 'frame', 0, 0, tiled=True)  41.1 us
    all_gather x1, blocking collectives, per_device(): lax.all_gather(packed, 'frame', axis=0, tiled=True)  34.7 us
    all_to_all x3, starting transfers between devices, per_device(): spread = lambda copies: lax.all_to_all(copies, 'head', 0, 0, tiled=True)  15.9 us
    all_to_all x1, blocking collectives, per_device(): lax.all_to_all(attended, 'head', 0, 0, axis_index_groups=along_x, tiled=T...  12.4 us
    all_to_all x1, blocking collectives, per_device(): spread = lambda copies: lax.all_to_all(copies, 'head', 0, 0, tiled=True)  12.1 us
    all_to_all x3, waiting for transfers between devices, per_device(): spread = lambda copies: lax.all_to_all(copies, 'head', 0, 0, tiled=True)  10.4 us
    pallas_call x1, Pallas kernels, per_device(): vmem_call(mlp_kernel, array(heads_n, width, share), [SCALAR, HERE, HERE,...  7.77 us
    pallas_call x1, Pallas kernels, per_device(): vmem_call(spatial_end_kernel, (array(frames_n, 112, LANES), array(full, s...  5.47 us
  transfers between devices with their start and end apart: 7, of which 3 were waited for; matrix products, arithmetic and copies ran while one was open for 1% of the time, Pallas kernels for 8%

profile of v5, /device:TPU:1, one launch (start us, length us, event | category | flops | bytes accessed | tf_op | source)
XLA Modules:
  0.0 176.2 jit_solution(13293238773799503347)
XLA Ops:
  6.5 0.8 copy-done.5
  7.3 0.8 shard_map.84
  8.1 5.9 %all-to-all-start.2 = ((bf16[8,72,144]{2,1,0:T(8,128)(2,1)}), bf16[8,72,144]{2,1,0:T(8,128)(2,1)S(1)}, u32[]{:S(2)}, u32[]{:S(2)}) async-start(bf16[8,72,144]{2,1,0:T(8,128)(2,1)} %shard_map.84), calls=%async_computation.2 | async-start | bytes 589824 | tf_op jit(solution)/shard_map/all_to_all | solution.py:293
  14.0 3.3 %collective-permute-start = (bf16[72,3,144]{2,0,1:T(8,128)(2,1)}, bf16[72,3,144]{2,0,1:T(8,128)(2,1)S(1)}, u32[]{:S(2)}, u32[]{:S(2)}) collective-permute-start(bf16[72,3,144]{2,0,1:T(8,128)(2,1)} %param.12), channel_id=1, source_target_pairs={{0,4},{4,0},{8,12},{12,8},{16,20},{20,16},{24,28},{28,24},{1,5},{5... | collective-permute-start | bytes 186632 | tf_op jit(solution)/shard_map/ppermute | solution.py:300
  17.4 1.1 copy.16
  18.4 0.1 copy.18
  18.6 1.2 collective-permute-done
  19.7 0.2 copy.17
  19.9 0.1 copy.19
  20.0 0.3 all-to-all-done.2
  20.3 0.3 reshape.20
  20.6 0.9 concatenate.3
  21.6 1.4 shard_map.82
  23.0 5.0 %all-to-all-start = ((bf16[8,144,640]{2,1,0:T(8,128)(2,1)}), bf16[8,144,640]{2,1,0:T(8,128)(2,1)S(1)}, u32[]{:S(2)}, u32[]{:S(2)}) async-start(bf16[8,144,640]{2,1,0:T(8,128)(2,1)} %get-tuple-element.11), calls=%async_computation | async-start | bytes 2949120 | tf_op jit(solution)/shard_map/all_to_all | solution.py:293
  28.1 3.3 %collective-permute-start.1 = (bf16[72,1152]{1,0:T(8,128)(2,1)S(1)}, bf16[72,1152]{1,0:T(8,128)(2,1)}, u32[]{:S(2)}, u32[]{:S(2)}) collective-permute-start(bf16[72,1152]{1,0:T(8,128)(2,1)S(1)} %shard_map.88.mlp_ref), channel_id=1, source_target_pairs={{0,4},{4,0},{8,12},{12,8},{16,20},{20,16},{24,28},{28,24},{1,5},{5... | collective-permute-start | bytes 497672 | tf_op jit(solution)/shard_map/ppermute | solution.py:303
  31.4 0.2 copy.13
  31.6 0.1 copy.14
  31.7 34.7 %all_gather.9.weight_ref = bf16[1152,432]{1,0:T(8,128)(2,1)S(1)} all-gather(bf16[72,432]{1,0:T(8,128)(2,1)S(1)} %copy.14), channel_id=1, replica_groups=mesh['frame'=16,'head'=8,'dp'=4] {'frame'}, dimensions={0}, use_global_device_ids=true | all-gather | bytes 1057536 | tf_op jit(solution)/shard_map/all_gather | solution.py:295
  66.4 2.6 %shard_map.83 = bf16[8,144,256]{2,1,0:T(8,128)(2,1)S(1)} custom-call(bf16[8,144,640]{2,1,0:T(8,128)(2,1)S(1)} %all-to-all-done.rows_ref, bf16[1152,432]{1,0:T(8,128)(2,1)S(1)} %all_gather.9.weight_ref, f32[1152,9]{1,0:T(8,128)S(1)} %get-tuple-element.12.mod_ref), custom_call_target="tpu_custom_call" | custom-call | tf_op jit(solution)/shard_map/pallas_call | solution.py:324
  69.0 0.9 copy-done
  69.9 2.0 %shard_map.89 = bf16[72,2944]{1,0:T(8,128)(2,1)} custom-call(bf16[8,144,128]{2,1,0:T(8,128)(2,1)S(1)} %slice.8.rows_ref, bf16[72,1152]{1,0:T(8,128)(2,1)S(1)} %shard_map.88.mlp_ref, bf16[72,1152]{1,0:T(8,128)(2,1)} %collective-permute-done.1.others_ref), custom_call_target="tpu_custom_call" | custom-call | tf_op jit(solution)/shard_map/pallas_call | solution.py:328
  71.9 5.1 %all-to-all-start.1 = ((bf16[8,144,256]{2,1,0:T(8,128)(2,1)}), bf16[8,144,256]{2,1,0:T(8,128)(2,1)S(1)}, u32[]{:S(2)}, u32[]{:S(2)}) async-start(bf16[8,144,256]{2,1,0:T(8,128)(2,1)} %copy-done), calls=%async_computation.1 | async-start | bytes 1179648 | tf_op jit(solution)/shard_map/all_to_all | solution.py:293
  77.0 10.1 %all-to-all-done.1.gathered_ref = bf16[8,144,256]{2,1,0:T(8,128)(2,1)S(1)} async-done(((bf16[8,144,256]{2,1,0:T(8,128)(2,1)}), bf16[8,144,256]{2,1,0:T(8,128)(2,1)S(1)}, u32[]{:S(2)}, u32[]{:S(2)}) %all-to-all-start.1) | async-done | bytes 589856 | tf_op jit(solution)/shard_map/all_to_all | solution.py:293
  87.1 5.5 %shard_map.85 = (bf16[16,112,128]{2,1,0:T(8,128)(2,1)S(1)}, bf16[1152,256]{1,0:T(8,128)(2,1)S(1)}) custom-call(s32[2]{0:T(128)S(1)} %pad_add_fusion.spot_ref, bf16[8,144,256]{2,1,0:T(8,128)(2,1)S(1)} %all-to-all-done.1.gathered_ref, bf16[8,144,640]{2,1,0:T(8,128)(2,1)S(1)} %all-to-all-done.rows_ref, ...), custom_call_target="tpu_custom_call" | custom-call | tf_op jit(solution)/shard_map/pallas_call | solution.py:333
  92.6 25.1 %all_to_all.35.moved_ref = bf16[16,112,128]{2,1,0:T(8,128)(2,1)S(1)} all-to-all(bf16[16,112,128]{2,1,0:T(8,128)(2,1)S(1)} %get-tuple-element.14), channel_id=1, replica_groups=mesh['frame'=16,'head'=8,'dp'=4] {'frame'}, dimensions={0} | all-to-all | bytes 917504 | tf_op jit(solution)/shard_map/all_to_all | solution.py:294
  117.7 1.7 shard_map.86
  119.4 16.0 %all_to_all.36.moved_ref = bf16[16,48,128]{2,1,0:T(8,128)(2,1)S(1)} all-to-all(bf16[16,48,128]{2,1,0:T(8,128)(2,1)S(1)} %shard_map.86), channel_id=1, replica_groups=mesh['frame'=16,'head'=8,'dp'=4] {'frame'}, dimensions={0} | all-to-all | bytes 393216 | tf_op jit(solution)/shard_map/all_to_all | solution.py:294
  135.4 0.9 shard_map.87
  136.3 12.4 %all_to_all.37.gathered_ref = bf16[4,288,256]{2,1,0:T(8,128)(2,1)S(1)} all-to-all(bf16[4,288,256]{2,1,0:T(8,128)(2,1)S(1)} %shard_map.87), channel_id=1, replica_groups={{0,8,16,24},{4,12,20,28},{1,9,17,25},{5,13,21,29},{2,10,18,26},{6,14,22..., dimensions={0} | all-to-all | bytes 1179648 | tf_op jit(solution)/shard_map/all_to_all | solution.py:347
  148.7 7.8 %shard_map.90 = bf16[8,144,256]{2,1,0:T(8,128)(2,1)S(1)} custom-call(s32[2]{0:T(128)S(1)} %pad_add_fusion.spot_ref, bf16[4,288,256]{2,1,0:T(8,128)(2,1)S(1)} %all_to_all.37.gathered_ref, bf16[1152,256]{1,0:T(8,128)(2,1)S(1)} %get-tuple-element.15.before_ref, bf16[1152,2944]{1,0:T(8,128)(2,1)} %all-gather.5.cloned.1.call-done.weight_ref, ...), custom_call_target="tpu_custom_call" | custom-call | tf_op jit(solution)/shard_map/pallas_call | solution.py:349
  156.5 12.1 %all_to_all.38.partial_ref = bf16[8,144,256]{2,1,0:T(8,128)(2,1)S(1)} all-to-all(bf16[8,144,256]{2,1,0:T(8,128)(2,1)S(1)} %shard_map.90), channel_id=1, replica_groups=mesh['frame'=16,'head'=8,'dp'=4] {'head'}, dimensions={0} | all-to-all | bytes 1179648 | tf_op jit(solution)/shard_map/all_to_all | solution.py:293
  168.6 0.7 shard_map.91
  (29 shorter events, 0.4 us)
Async XLA Ops:
  6.5 14.1 %slice-start = ((bf16[72,576]{1,0:T(8,128)(2,1)}), bf16[72,512]{1,0:T(8,128)(2,1)S(1)}, s32[]{:S(2)}) async-start(bf16[72,576]{1,0:T(8,128)(2,1)} %refs_0_.1), calls=%async_computation.9 | async-start | bytes 147456 | tf_op jit(solution)/shard_map/slice | solution.py:318
  6.5 0.8 copy-start.5
  8.1 12.2 %all-to-all-start.2 = ((bf16[8,72,144]{2,1,0:T(8,128)(2,1)}), bf16[8,72,144]{2,1,0:T(8,128)(2,1)S(1)}, u32[]{:S(2)}, u32[]{:S(2)}) async-start(bf16[8,72,144]{2,1,0:T(8,128)(2,1)} %shard_map.84), calls=%async_computation.2 | async-start | bytes 589824 | tf_op jit(solution)/shard_map/all_to_all | solution.py:293
  14.0 73.1 %all-gather.3.cloned.1.call-start = ((), (), s32[]{:S(2)}) async-start(), calls=%async_computation.7 | async-start | bytes 6266880 | tf_op jit(solution)/shard_map/all_gather | solution.py:295
  14.0 5.7 %collective-permute-start = (bf16[72,3,144]{2,0,1:T(8,128)(2,1)}, bf16[72,3,144]{2,0,1:T(8,128)(2,1)S(1)}, u32[]{:S(2)}, u32[]{:S(2)}) collective-permute-start(bf16[72,3,144]{2,0,1:T(8,128)(2,1)} %param.12), channel_id=1, source_target_pairs={{0,4},{4,0},{8,12},{12,8},{16,20},{20,16},{24,28},{28,24},{1,5},{5... | collective-permute-start | bytes 186632 | tf_op jit(solution)/shard_map/ppermute | solution.py:300
  18.4 3.1 %copy-start.2 = (bf16[1,512,144]{1,2,0:T(8,128)(2,1)S(1)}, bf16[1,512,144]{1,2,0:T(8,128)(2,1)}, u32[]{:S(2)}) copy-start(bf16[1,512,144]{1,2,0:T(8,128)(2,1)} %param.8) | copy-start | bytes 442372
  18.4 3.1 %copy-start.4 = (f32[9,1152]{1,0:T(8,128)S(1)}, f32[9,1152]{1,0:T(8,128)}, u32[]{:S(2)}) copy-start(f32[9,1152]{1,0:T(8,128)} %mod_ref.1) | copy-start | bytes 124420
  18.4 3.1 %copy-start.6 = (bf16[144,72]{1,0:T(8,128)(2,1)S(1)}, bf16[144,72]{1,0:T(8,128)(2,1)}, u32[]{:S(2)}) copy-start(bf16[144,72]{1,0:T(8,128)(2,1)} %late_ref.1) | copy-start | bytes 62212
  23.0 5.0 %copy-start.1 = (bf16[72,576]{1,0:T(8,128)(2,1)S(1)}, bf16[72,576]{1,0:T(8,128)(2,1)}, u32[]{:S(2)}) copy-start(bf16[72,576]{1,0:T(8,128)(2,1)} %refs_0_.1) | copy-start | bytes 248836
  23.0 5.0 %copy-start.3 = (bf16[576,72]{0,1:T(8,128)(2,1)S(1)}, bf16[576,72]{0,1:T(8,128)(2,1)}, u32[]{:S(2)}) copy-start(bf16[576,72]{0,1:T(8,128)(2,1)} %param.15) | copy-start | bytes 248836
  23.0 8.5 %copy-start.7 = (bf16[72,3,144]{2,0,1:T(8,128)(2,1)S(1)}, bf16[72,3,144]{2,0,1:T(8,128)(2,1)}, u32[]{:S(2)}) copy-start(bf16[72,3,144]{2,0,1:T(8,128)(2,1)} %param.10) | copy-start | bytes 186628
  23.0 43.4 %all-to-all-start = ((bf16[8,144,640]{2,1,0:T(8,128)(2,1)}), bf16[8,144,640]{2,1,0:T(8,128)(2,1)S(1)}, u32[]{:S(2)}, u32[]{:S(2)}) async-start(bf16[8,144,640]{2,1,0:T(8,128)(2,1)} %get-tuple-element.11), calls=%async_computation | async-start | bytes 2949120 | tf_op jit(solution)/shard_map/all_to_all | solution.py:293
  27.9 120.8 %all-gather.5.cloned.1.call-start = ((), (), s32[]{:S(2)}) async-start(), calls=%async_computation.8 | async-start | bytes 7206912 | tf_op jit(solution)/shard_map/all_gather | solution.py:295
  28.1 41.8 %collective-permute-start.1 = (bf16[72,1152]{1,0:T(8,128)(2,1)S(1)}, bf16[72,1152]{1,0:T(8,128)(2,1)}, u32[]{:S(2)}, u32[]{:S(2)}) collective-permute-start(bf16[72,1152]{1,0:T(8,128)(2,1)S(1)} %shard_map.88.mlp_ref), channel_id=1, source_target_pairs={{0,4},{4,0},{8,12},{12,8},{16,20},{20,16},{24,28},{28,24},{1,5},{5... | collective-permute-start | bytes 497672 | tf_op jit(solution)/shard_map/ppermute | solution.py:303
  69.0 0.9 copy-start
  71.9 15.2 %all-to-all-start.1 = ((bf16[8,144,256]{2,1,0:T(8,128)(2,1)}), bf16[8,144,256]{2,1,0:T(8,128)(2,1)S(1)}, u32[]{:S(2)}, u32[]{:S(2)}) async-start(bf16[8,144,256]{2,1,0:T(8,128)(2,1)} %copy-done), calls=%async_computation.1 | async-start | bytes 1179648 | tf_op jit(solution)/shard_map/all_to_all | solution.py:293
Sparse Core Ops, SparseCore 0:
  21.7 59.6 all-gather.2
  83.5 63.0 all-gather.4

commit v6 on v5

--- a/solution.py
+++ b/solution.py
@@ -16,6 +16,7 @@
 PARTS = LANES // PLACE
 BLOCK = 144
 STEP = 576
+LONG = 1152
 UNITS = 512
 FEATURES = 432
 
@@ -97,10 +98,10 @@
         hidden_ref[spot] = (normal * (1.0 + scale[spot]) + shift[spot]).astype(jnp.bfloat16)
 
 
-def add_branch(weight, hidden, stream, gate, out_ref, whole_ref):
-    for at in range(0, hidden.shape[0], STEP):
+def add_branch(weight, hidden, stream, gate, out_ref, whole_ref, step=STEP):
+    for at in range(0, hidden.shape[0], step):
         branch = jnp.dot(weight(at), hidden, preferred_element_type=jnp.float32)
-        for inner in range(0, STEP, BLOCK):
+        for inner in range(0, step, BLOCK):
             spot = slice(at + inner, at + inner + BLOCK)
             gated = gate[spot] * branch[inner : inner + BLOCK]
             total = (stream(at + inner).astype(jnp.float32) + gated).astype(jnp.bfloat16)
@@ -115,9 +116,9 @@
     return copies
 
 
-def blocks(weight_ref, held):
+def blocks(weight_ref, held, step=STEP):
     full, cols = held.shape
-    spots = [pl.ds(at, STEP) for at in range(0, full, STEP)]
+    spots = [pl.ds(at, step) for at in range(0, full, step)]
     return [(weight_ref.at[spot, pl.ds(0, cols)], held.at[spot]) for spot in spots]
 
 
@@ -214,19 +215,19 @@
     full, rows = stream.shape
     units = active.shape[0]
     cuts = [(0, UNITS), (UNITS, units - UNITS)]
-    pairs = blocks(weight_ref, held)
+    pairs = blocks(weight_ref, held, LONG)
     pairs.append((early_ref.at[:, pl.ds(early_ref.shape[1] - UNITS, UNITS)], up.at[:, pl.ds(0, UNITS)]))
     rest = units - UNITS
     pairs.append((weight_ref.at[:, pl.ds(full + units, rest)], up.at[:, pl.ds(UNITS, rest)]))
-    for at in range(0, full, STEP):
-        rows_at = pl.ds(at, STEP)
+    for at in range(0, full, LONG):
+        rows_at = pl.ds(at, LONG)
         pairs.append((weight_ref.at[rows_at, pl.ds(full, units)], down.at[rows_at]))
     copies = start_copies(pairs, sems)
-    first = full // STEP
+    first = full // LONG
 
     def weight(at):
-        copies[at // STEP].wait()
-        return held[at : at + STEP]
+        copies[at // LONG].wait()
+        return held[at : at + LONG]
 
     add_branch(
         weight,
@@ -235,16 +236,17 @@
         mod_ref[:, 5:6],
         stream,
         whole,
+        LONG,
     )
     norm_rows(lambda at: whole[at : at + BLOCK], full, mod_ref[:, 6:7], mod_ref[:, 7:8], hidden)
     for i, (at, count) in enumerate(cuts):
         copies[first + i].wait()
         raised = project(up[:, at : at + count], hidden[...])
         active[at : at + count] = jax.nn.gelu(raised, approximate=True).astype(jnp.bfloat16)
-    for i, at in enumerate(range(0, full, STEP)):
+    for i, at in enumerate(range(0, full, LONG)):
         copies[first + len(cuts) + i].wait()
-        lowered = jnp.dot(down[at : at + STEP], active[...], preferred_element_type=jnp.float32)
-        for inner in range(0, STEP, BLOCK):
+        lowered = jnp.dot(down[at : at + LONG], active[...], preferred_element_type=jnp.float32)
+        for inner in range(0, LONG, BLOCK):
             spot = slice(at + inner, at + inner + BLOCK)
             place = (at + inner) // BLOCK
             carried = jnp.where(spot_ref[0] == place // SHARES, whole[spot], 0.0)
@@ -353,7 +355,7 @@
         (
             bf16(full, share), f32(full, share), bf16(full, share), bf16(SHARES * units, share),
             bf16(full, full), bf16(full, SHARES * units), bf16(full, SHARES * units),
-            sems(2 * full // STEP + 2),
+            sems(2 * full // LONG + 2),
         ),
         50,
     )(spot, attended, stream, late, early, mod)

time: 178 us -> 177 us (level)
  no operation moved by 1% of the time
where the time goes in v6:
time: 177 us; the launch traced here: 176 us
  blocking collectives  100 us (56%)
  Pallas kernels  22.8 us (13%)
  starting transfers between devices  22.6 us (13%)
  between operations  13.6 us (8%)
  waiting for transfers between devices  11.6 us (7%)
  local copies, waits for them, and re-layouts  4.63 us (3%)
    all_to_all x2, blocking collectives, per_device(): swap = lambda chunks: lax.all_to_all(chunks, 'frame', 0, 0, tiled=True)  41.1 us
    all_gather x1, blocking collectives, per_device(): lax.all_gather(packed, 'frame', axis=0, tiled=True)  34.7 us
    all_to_all x3, starting transfers between devices, per_device(): spread = lambda copies: lax.all_to_all(copies, 'head', 0, 0, tiled=True)  15.9 us
    all_to_all x1, blocking collectives, per_device(): lax.all_to_all(attended, 'head', 0, 0, axis_index_groups=along_x, tiled=T...  12.4 us
    all_to_all x1, blocking collectives, per_device(): spread = lambda copies: lax.all_to_all(copies, 'head', 0, 0, tiled=True)  12.1 us
    all_to_all x3, waiting for transfers between devices, per_device(): spread = lambda copies: lax.all_to_all(copies, 'head', 0, 0, tiled=True)  10.4 us
    pallas_call x1, Pallas kernels, per_device(): vmem_call(mlp_kernel, array(heads_n, width, share), [SCALAR, HERE, HERE,...  7.24 us
    pallas_call x1, Pallas kernels, per_device(): vmem_call(spatial_end_kernel, (array(frames_n, 112, LANES), array(full, s...  5.47 us
  transfers between devices with their start and end apart: 7, of which 3 were waited for; matrix products, arithmetic and copies ran while one was open for 1% of the time, Pallas kernels for 8%

profile of v6, /device:TPU:1, one launch (start us, length us, event | category | flops | bytes accessed | tf_op | source)
XLA Modules:
  0.0 175.7 jit_solution(11827084066601882540)
XLA Ops:
  6.5 0.8 copy-done.5
  7.3 0.8 shard_map.84
  8.1 5.9 %all-to-all-start.2 = ((bf16[8,72,144]{2,1,0:T(8,128)(2,1)}), bf16[8,72,144]{2,1,0:T(8,128)(2,1)S(1)}, u32[]{:S(2)}, u32[]{:S(2)}) async-start(bf16[8,72,144]{2,1,0:T(8,128)(2,1)} %shard_map.84), calls=%async_computation.2 | async-start | bytes 589824 | tf_op jit(solution)/shard_map/all_to_all | solution.py:295
  14.0 3.3 %collective-permute-start = (bf16[72,3,144]{2,0,1:T(8,128)(2,1)}, bf16[72,3,144]{2,0,1:T(8,128)(2,1)S(1)}, u32[]{:S(2)}, u32[]{:S(2)}) collective-permute-start(bf16[72,3,144]{2,0,1:T(8,128)(2,1)} %param.12), channel_id=1, source_target_pairs={{0,4},{4,0},{8,12},{12,8},{16,20},{20,16},{24,28},{28,24},{1,5},{5... | collective-permute-start | bytes 186632 | tf_op jit(solution)/shard_map/ppermute | solution.py:302
  17.4 1.1 copy.16
  18.4 0.1 copy.18
  18.6 1.2 collective-permute-done
  19.7 0.2 copy.17
  19.9 0.1 copy.19
  20.0 0.3 all-to-all-done.2
  20.3 0.3 reshape.20
  20.6 0.9 concatenate.3
  21.6 1.4 shard_map.82
  23.0 5.0 %all-to-all-start = ((bf16[8,144,640]{2,1,0:T(8,128)(2,1)}), bf16[8,144,640]{2,1,0:T(8,128)(2,1)S(1)}, u32[]{:S(2)}, u32[]{:S(2)}) async-start(bf16[8,144,640]{2,1,0:T(8,128)(2,1)} %get-tuple-element.11), calls=%async_computation | async-start | bytes 2949120 | tf_op jit(solution)/shard_map/all_to_all | solution.py:295
  28.1 3.3 %collective-permute-start.1 = (bf16[72,1152]{1,0:T(8,128)(2,1)S(1)}, bf16[72,1152]{1,0:T(8,128)(2,1)}, u32[]{:S(2)}, u32[]{:S(2)}) collective-permute-start(bf16[72,1152]{1,0:T(8,128)(2,1)S(1)} %shard_map.88.mlp_ref), channel_id=1, source_target_pairs={{0,4},{4,0},{8,12},{12,8},{16,20},{20,16},{24,28},{28,24},{1,5},{5... | collective-permute-start | bytes 497672 | tf_op jit(solution)/shard_map/ppermute | solution.py:305
  31.4 0.2 copy.13
  31.6 0.1 copy.14
  31.7 34.7 %all_gather.9.weight_ref = bf16[1152,432]{1,0:T(8,128)(2,1)S(1)} all-gather(bf16[72,432]{1,0:T(8,128)(2,1)S(1)} %copy.14), channel_id=1, replica_groups=mesh['frame'=16,'head'=8,'dp'=4] {'frame'}, dimensions={0}, use_global_device_ids=true | all-gather | bytes 1057536 | tf_op jit(solution)/shard_map/all_gather | solution.py:297
  66.4 2.6 %shard_map.83 = bf16[8,144,256]{2,1,0:T(8,128)(2,1)S(1)} custom-call(bf16[8,144,640]{2,1,0:T(8,128)(2,1)S(1)} %all-to-all-done.rows_ref, bf16[1152,432]{1,0:T(8,128)(2,1)S(1)} %all_gather.9.weight_ref, f32[1152,9]{1,0:T(8,128)S(1)} %get-tuple-element.12.mod_ref), custom_call_target="tpu_custom_call" | custom-call | tf_op jit(solution)/shard_map/pallas_call | solution.py:326
  69.0 0.9 copy-done
  69.9 2.0 %shard_map.89 = bf16[72,2944]{1,0:T(8,128)(2,1)} custom-call(bf16[8,144,128]{2,1,0:T(8,128)(2,1)S(1)} %slice.8.rows_ref, bf16[72,1152]{1,0:T(8,128)(2,1)S(1)} %shard_map.88.mlp_ref, bf16[72,1152]{1,0:T(8,128)(2,1)} %collective-permute-done.1.others_ref), custom_call_target="tpu_custom_call" | custom-call | tf_op jit(solution)/shard_map/pallas_call | solution.py:330
  71.9 5.1 %all-to-all-start.1 = ((bf16[8,144,256]{2,1,0:T(8,128)(2,1)}), bf16[8,144,256]{2,1,0:T(8,128)(2,1)S(1)}, u32[]{:S(2)}, u32[]{:S(2)}) async-start(bf16[8,144,256]{2,1,0:T(8,128)(2,1)} %copy-done), calls=%async_computation.1 | async-start | bytes 1179648 | tf_op jit(solution)/shard_map/all_to_all | solution.py:295
  77.0 10.1 %all-to-all-done.1.gathered_ref = bf16[8,144,256]{2,1,0:T(8,128)(2,1)S(1)} async-done(((bf16[8,144,256]{2,1,0:T(8,128)(2,1)}), bf16[8,144,256]{2,1,0:T(8,128)(2,1)S(1)}, u32[]{:S(2)}, u32[]{:S(2)}) %all-to-all-start.1) | async-done | bytes 589856 | tf_op jit(solution)/shard_map/all_to_all | solution.py:295
  87.1 5.5 %shard_map.85 = (bf16[16,112,128]{2,1,0:T(8,128)(2,1)S(1)}, bf16[1152,256]{1,0:T(8,128)(2,1)S(1)}) custom-call(s32[2]{0:T(128)S(1)} %pad_add_fusion.spot_ref, bf16[8,144,256]{2,1,0:T(8,128)(2,1)S(1)} %all-to-all-done.1.gathered_ref, bf16[8,144,640]{2,1,0:T(8,128)(2,1)S(1)} %all-to-all-done.rows_ref, ...), custom_call_target="tpu_custom_call" | custom-call | tf_op jit(solution)/shard_map/pallas_call | solution.py:335
  92.6 25.1 %all_to_all.35.moved_ref = bf16[16,112,128]{2,1,0:T(8,128)(2,1)S(1)} all-to-all(bf16[16,112,128]{2,1,0:T(8,128)(2,1)S(1)} %get-tuple-element.14), channel_id=1, replica_groups=mesh['frame'=16,'head'=8,'dp'=4] {'frame'}, dimensions={0} | all-to-all | bytes 917504 | tf_op jit(solution)/shard_map/all_to_all | solution.py:296
  117.7 1.7 shard_map.86
  119.4 16.0 %all_to_all.36.moved_ref = bf16[16,48,128]{2,1,0:T(8,128)(2,1)S(1)} all-to-all(bf16[16,48,128]{2,1,0:T(8,128)(2,1)S(1)} %shard_map.86), channel_id=1, replica_groups=mesh['frame'=16,'head'=8,'dp'=4] {'frame'}, dimensions={0} | all-to-all | bytes 393216 | tf_op jit(solution)/shard_map/all_to_all | solution.py:296
  135.4 0.9 shard_map.87
  136.3 12.4 %all_to_all.37.gathered_ref = bf16[4,288,256]{2,1,0:T(8,128)(2,1)S(1)} all-to-all(bf16[4,288,256]{2,1,0:T(8,128)(2,1)S(1)} %shard_map.87), channel_id=1, replica_groups={{0,8,16,24},{4,12,20,28},{1,9,17,25},{5,13,21,29},{2,10,18,26},{6,14,22..., dimensions={0} | all-to-all | bytes 1179648 | tf_op jit(solution)/shard_map/all_to_all | solution.py:349
  148.7 7.2 %shard_map.90 = bf16[8,144,256]{2,1,0:T(8,128)(2,1)S(1)} custom-call(s32[2]{0:T(128)S(1)} %pad_add_fusion.spot_ref, bf16[4,288,256]{2,1,0:T(8,128)(2,1)S(1)} %all_to_all.37.gathered_ref, bf16[1152,256]{1,0:T(8,128)(2,1)S(1)} %get-tuple-element.15.before_ref, bf16[1152,2944]{1,0:T(8,128)(2,1)} %all-gather.5.cloned.1.call-done.weight_ref, ...), custom_call_target="tpu_custom_call" | custom-call | tf_op jit(solution)/shard_map/pallas_call | solution.py:351
  155.9 12.1 %all_to_all.38.partial_ref = bf16[8,144,256]{2,1,0:T(8,128)(2,1)S(1)} all-to-all(bf16[8,144,256]{2,1,0:T(8,128)(2,1)S(1)} %shard_map.90), channel_id=1, replica_groups=mesh['frame'=16,'head'=8,'dp'=4] {'head'}, dimensions={0} | all-to-all | bytes 1179648 | tf_op jit(solution)/shard_map/all_to_all | solution.py:295
  168.1 0.7 shard_map.91
  (29 shorter events, 0.4 us)
Async XLA Ops:
  6.5 14.1 %slice-start = ((bf16[72,576]{1,0:T(8,128)(2,1)}), bf16[72,512]{1,0:T(8,128)(2,1)S(1)}, s32[]{:S(2)}) async-start(bf16[72,576]{1,0:T(8,128)(2,1)} %refs_0_.1), calls=%async_computation.9 | async-start | bytes 147456 | tf_op jit(solution)/shard_map/slice | solution.py:320
  6.5 0.8 copy-start.5
  8.1 12.2 %all-to-all-start.2 = ((bf16[8,72,144]{2,1,0:T(8,128)(2,1)}), bf16[8,72,144]{2,1,0:T(8,128)(2,1)S(1)}, u32[]{:S(2)}, u32[]{:S(2)}) async-start(bf16[8,72,144]{2,1,0:T(8,128)(2,1)} %shard_map.84), calls=%async_computation.2 | async-start | bytes 589824 | tf_op jit(solution)/shard_map/all_to_all | solution.py:295
  14.0 73.1 %all-gather.3.cloned.1.call-start = ((), (), s32[]{:S(2)}) async-start(), calls=%async_computation.7 | async-start | bytes 6266880 | tf_op jit(solution)/shard_map/all_gather | solution.py:297
  14.0 5.7 %collective-permute-start = (bf16[72,3,144]{2,0,1:T(8,128)(2,1)}, bf16[72,3,144]{2,0,1:T(8,128)(2,1)S(1)}, u32[]{:S(2)}, u32[]{:S(2)}) collective-permute-start(bf16[72,3,144]{2,0,1:T(8,128)(2,1)} %param.12), channel_id=1, source_target_pairs={{0,4},{4,0},{8,12},{12,8},{16,20},{20,16},{24,28},{28,24},{1,5},{5... | collective-permute-start | bytes 186632 | tf_op jit(solution)/shard_map/ppermute | solution.py:302
  18.4 3.1 %copy-start.2 = (bf16[1,512,144]{1,2,0:T(8,128)(2,1)S(1)}, bf16[1,512,144]{1,2,0:T(8,128)(2,1)}, u32[]{:S(2)}) copy-start(bf16[1,512,144]{1,2,0:T(8,128)(2,1)} %param.8) | copy-start | bytes 442372
  18.4 3.1 %copy-start.4 = (f32[9,1152]{1,0:T(8,128)S(1)}, f32[9,1152]{1,0:T(8,128)}, u32[]{:S(2)}) copy-start(f32[9,1152]{1,0:T(8,128)} %mod_ref.1) | copy-start | bytes 124420
  18.4 3.1 %copy-start.6 = (bf16[144,72]{1,0:T(8,128)(2,1)S(1)}, bf16[144,72]{1,0:T(8,128)(2,1)}, u32[]{:S(2)}) copy-start(bf16[144,72]{1,0:T(8,128)(2,1)} %late_ref.1) | copy-start | bytes 62212
  23.0 5.0 %copy-start.1 = (bf16[72,576]{1,0:T(8,128)(2,1)S(1)}, bf16[72,576]{1,0:T(8,128)(2,1)}, u32[]{:S(2)}) copy-start(bf16[72,576]{1,0:T(8,128)(2,1)} %refs_0_.1) | copy-start | bytes 248836
  23.0 5.0 %copy-start.3 = (bf16[576,72]{0,1:T(8,128)(2,1)S(1)}, bf16[576,72]{0,1:T(8,128)(2,1)}, u32[]{:S(2)}) copy-start(bf16[576,72]{0,1:T(8,128)(2,1)} %param.15) | copy-start | bytes 248836
  23.0 8.5 %copy-start.7 = (bf16[72,3,144]{2,0,1:T(8,128)(2,1)S(1)}, bf16[72,3,144]{2,0,1:T(8,128)(2,1)}, u32[]{:S(2)}) copy-start(bf16[72,3,144]{2,0,1:T(8,128)(2,1)} %param.10) | copy-start | bytes 186628
  23.0 43.4 %all-to-all-start = ((bf16[8,144,640]{2,1,0:T(8,128)(2,1)}), bf16[8,144,640]{2,1,0:T(8,128)(2,1)S(1)}, u32[]{:S(2)}, u32[]{:S(2)}) async-start(bf16[8,144,640]{2,1,0:T(8,128)(2,1)} %get-tuple-element.11), calls=%async_computation | async-start | bytes 2949120 | tf_op jit(solution)/shard_map/all_to_all | solution.py:295
  27.9 120.8 %all-gather.5.cloned.1.call-start = ((), (), s32[]{:S(2)}) async-start(), calls=%async_computation.8 | async-start | bytes 7206912 | tf_op jit(solution)/shard_map/all_gather | solution.py:297
  28.1 41.8 %collective-permute-start.1 = (bf16[72,1152]{1,0:T(8,128)(2,1)S(1)}, bf16[72,1152]{1,0:T(8,128)(2,1)}, u32[]{:S(2)}, u32[]{:S(2)}) collective-permute-start(bf16[72,1152]{1,0:T(8,128)(2,1)S(1)} %shard_map.88.mlp_ref), channel_id=1, source_target_pairs={{0,4},{4,0},{8,12},{12,8},{16,20},{20,16},{24,28},{28,24},{1,5},{5... | collective-permute-start | bytes 497672 | tf_op jit(solution)/shard_map/ppermute | solution.py:305
  69.0 0.9 copy-start
  71.9 15.2 %all-to-all-start.1 = ((bf16[8,144,256]{2,1,0:T(8,128)(2,1)}), bf16[8,144,256]{2,1,0:T(8,128)(2,1)S(1)}, u32[]{:S(2)}, u32[]{:S(2)}) async-start(bf16[8,144,256]{2,1,0:T(8,128)(2,1)} %copy-done), calls=%async_computation.1 | async-start | bytes 1179648 | tf_op jit(solution)/shard_map/all_to_all | solution.py:295
Sparse Core Ops, SparseCore 0:
  21.7 59.6 all-gather.2
  83.5 63.0 all-gather.4

commit v7 on v6

--- a/solution.py
+++ b/solution.py
@@ -143,15 +143,12 @@
     mod_out_ref[...] = mod_ref[...].T
 
 
-def late_weights_kernel(rows_ref, mlp_ref, others_ref, out_ref):
-    depth, units = mlp_ref.shape[0], mlp_ref.shape[1] // 2
-    turned = [rows_ref[at, :, :depth].T for at in range(rows_ref.shape[0])]
-    pieces = turned + [mlp_ref[:, units:], others_ref[:, units:], mlp_ref[:, UNITS:units], others_ref[:, :units]]
-    out_ref[...] = jnp.concatenate(pieces, 1)
-
-
-def spatial_kernel(rows_ref, weight_ref, mod_ref, out_ref, hidden):
+def spatial_kernel(rows_ref, weight_ref, mod_ref, out_ref, late_ref, hidden):
     full, rows = hidden.shape
+    depth = late_ref.shape[0]
+    late_ref[...] = jnp.concatenate(
+        [rows_ref[at, :, rows : rows + depth].T for at in range(rows_ref.shape[0])], 1
+    )
     read = lambda at: rows_ref[at // BLOCK, :, :rows].astype(jnp.float32)
     norm_rows(read, full, mod_ref[:, 0:1], mod_ref[:, 1:2], hidden)
     mixed = norm_heads(project(weight_ref[...], hidden[...])).astype(jnp.bfloat16)
@@ -242,7 +239,12 @@
     for i, (at, count) in enumerate(cuts):
         copies[first + i].wait()
         raised = project(up[:, at : at + count], hidden[...])
-        active[at : at + count] = jax.nn.gelu(raised, approximate=True).astype(jnp.bfloat16)
+        raised = jax.nn.gelu(raised, approximate=True).astype(jnp.bfloat16)
+        if at == 0:
+            active[:count] = raised
+        else:
+            active[units // SHARES :] = raised[: units // SHARES]
+            active[UNITS : units // SHARES] = raised[units // SHARES :]
     for i, at in enumerate(range(0, full, LONG)):
         copies[first + len(cuts) + i].wait()
         lowered = jnp.dot(down[at : at + LONG], active[...], preferred_element_type=jnp.float32)
@@ -301,8 +303,7 @@
 
     others_qkv = lax.ppermute(temporal_qkv, "head", across_y)
     out_copies = vmem_call(turned_copies_kernel, array(heads_n, depth, width), [HERE])(spatial_out)
-    mlp = vmem_call(side_by_side_kernel, array(depth, 2 * units), [HERE] * 2)(mlp_up, mlp_down.T)
-    others = lax.ppermute(mlp, "head", across_y)
+    mlp = vmem_call(side_by_side_kernel, array(depth, 2 * units), [HERE] * 2)(mlp_down.T, mlp_up)
     row_copies, mod = vmem_call(
         opening_kernel,
         (
@@ -323,14 +324,17 @@
     stream = spread(row_copies)
     s_qkv = gather_frame(spatial_qkv.reshape(depth, -1))
 
-    attended = vmem_call(
-        spatial_kernel, array(heads_n, width, share), [HERE] * 3, (bf16(full, rows),)
+    s_qkv, mlp = lax.optimization_barrier((s_qkv, mlp))
+    others = lax.ppermute(mlp, "head", across_y)
+
+    attended, t_out = vmem_call(
+        spatial_kernel,
+        (array(heads_n, width, share), array(depth, full)),
+        [HERE] * 3,
+        (bf16(full, rows),),
     )(stream, s_qkv, mod)
-    t_out, attended = lax.optimization_barrier((stream[:, :, rows:], attended))
-    late = vmem_call(
-        late_weights_kernel, array(depth, full + 2 * SHARES * units - UNITS), [HERE] * 3
-    )(t_out, mlp, others)
-    late = gather_frame(late)
+    late = [t_out, mlp[:, :units], others, mlp[:, units + UNITS :]]
+    late = gather_frame(jnp.concatenate(late, axis=1))
 
     mixed, stream = vmem_call(
         spatial_end_kernel,

time: 177 us -> 178 us (level)
  local copies, waits for them, and re-layouts: 4.63 us -> 7.22 us
  Pallas kernels: 22.8 us -> 20.9 us
    pallas_call x2 -> x1, Pallas kernels: 4.57 us -> 2.6 us  [per_device(): vmem_call(spatial_kernel, (array(heads_n, width, share), array(depth, ful...]
    concatenate x0 -> x1, local copies, waits for them, and re-layouts: none -> 1.92 us  [per_device(): late = gather_frame(jnp.concatenate(late, axis=1))]
  transfers between devices with their start and end apart: 7 -> 7, of which waited for: 3 -> 4; matrix products, arithmetic and copies ran while one was open for 1% -> 2% of each run, Pallas kernels for 8% -> 7%
where the time goes in v7:
time: 178 us; the launch traced here: 176 us
  blocking collectives  100 us (56%)
  starting transfers between devices  22.7 us (13%)
  Pallas kernels  20.9 us (12%)
  between operations  13.6 us (8%)
  waiting for transfers between devices  11.5 us (6%)
  local copies, waits for them, and re-layouts  7.22 us (4%)
    all_to_all x2, blocking collectives, per_device(): swap = lambda chunks: lax.all_to_all(chunks, 'frame', 0, 0, tiled=True)  42.2 us
    all_gather x1, blocking collectives, per_device(): lax.all_gather(packed, 'frame', axis=0, tiled=True)  34 us
    all_to_all x3, starting transfers between devices, per_device(): spread = lambda copies: lax.all_to_all(copies, 'head', 0, 0, tiled=True)  15.7 us
    all_to_all x1, blocking collectives, per_device(): spread = lambda copies: lax.all_to_all(copies, 'head', 0, 0, tiled=True)  12.1 us
    all_to_all x1, blocking collectives, per_device(): lax.all_to_all(attended, 'head', 0, 0, axis_index_groups=along_x, tiled=T...  12.1 us
    all_to_all x3, waiting for transfers between devices, per_device(): spread = lambda copies: lax.all_to_all(copies, 'head', 0, 0, tiled=True)  9.84 us
    pallas_call x1, Pallas kernels, per_device(): vmem_call(mlp_kernel, array(heads_n, width, share), [SCALAR, HERE, HERE,...  7.23 us
    pallas_call x1, Pallas kernels, per_device(): vmem_call(spatial_end_kernel, (array(frames_n, 112, LANES), array(full, s...  5.47 us
  transfers between devices with their start and end apart: 7, of which 4 were waited for; matrix products, arithmetic and copies ran while one was open for 2% of the time, Pallas kernels for 7%

profile of v7, /device:TPU:1, one launch (start us, length us, event | category | flops | bytes accessed | tf_op | source)
XLA Modules:
  0.0 176.4 jit_solution(16883827961132714684)
XLA Ops:
  6.5 0.8 copy-done.6
  7.3 0.8 shard_map.85
  8.1 5.9 %all-to-all-start.2 = ((bf16[8,72,144]{2,1,0:T(8,128)(2,1)}), bf16[8,72,144]{2,1,0:T(8,128)(2,1)S(1)}, u32[]{:S(2)}, u32[]{:S(2)}) async-start(bf16[8,72,144]{2,1,0:T(8,128)(2,1)} %shard_map.85), calls=%async_computation.2 | async-start | bytes 589824 | tf_op jit(solution)/shard_map/all_to_all | solution.py:297
  14.0 3.3 %collective-permute-start = (bf16[72,3,144]{2,0,1:T(8,128)(2,1)}, bf16[72,3,144]{2,0,1:T(8,128)(2,1)S(1)}, u32[]{:S(2)}, u32[]{:S(2)}) collective-permute-start(bf16[72,3,144]{2,0,1:T(8,128)(2,1)} %param.12), channel_id=1, source_target_pairs={{0,4},{4,0},{8,12},{12,8},{16,20},{20,16},{24,28},{28,24},{1,5},{5... | collective-permute-start | bytes 186632 | tf_op jit(solution)/shard_map/ppermute | solution.py:304
  17.4 1.1 copy.16
  18.6 1.2 collective-permute-done
  19.7 0.2 copy.17
  20.0 0.3 all-to-all-done.2
  20.4 0.3 reshape.20
  20.7 0.8 concatenate.6
  21.6 1.4 shard_map.82
  22.9 5.0 %all-to-all-start = ((bf16[8,144,640]{2,1,0:T(8,128)(2,1)}), bf16[8,144,640]{2,1,0:T(8,128)(2,1)S(1)}, u32[]{:S(2)}, u32[]{:S(2)}) async-start(bf16[8,144,640]{2,1,0:T(8,128)(2,1)} %get-tuple-element.13), calls=%async_computation | async-start | bytes 2949120 | tf_op jit(solution)/shard_map/all_to_all | solution.py:297
  27.9 0.2 copy.13
  28.1 0.1 copy.14
  28.3 34.0 %all_gather.9.weight_ref = bf16[1152,432]{1,0:T(8,128)(2,1)S(1)} all-gather(bf16[72,432]{1,0:T(8,128)(2,1)S(1)} %copy.14), channel_id=1, replica_groups=mesh['frame'=16,'head'=8,'dp'=4] {'frame'}, dimensions={0}, use_global_device_ids=true | all-gather | bytes 1057536 | tf_op jit(solution)/shard_map/all_gather | solution.py:299
  62.4 3.6 %collective-permute-start.1 = (bf16[72,1152]{1,0:T(8,128)(2,1)S(1)}, bf16[72,1152]{1,0:T(8,128)(2,1)}, u32[]{:S(2)}, u32[]{:S(2)}) collective-permute-start(bf16[72,1152]{1,0:T(8,128)(2,1)S(1)} %shard_map.83), channel_id=1, source_target_pairs={{0,4},{4,0},{8,12},{12,8},{16,20},{20,16},{24,28},{28,24},{1,5},{5... | collective-permute-start | bytes 497672 | tf_op jit(solution)/shard_map/ppermute | solution.py:328
  66.1 2.6 %shard_map.84 = (bf16[8,144,256]{2,1,0:T(8,128)(2,1)S(1)}, bf16[72,1152]{1,0:T(8,128)(2,1)S(1)}) custom-call(bf16[8,144,640]{2,1,0:T(8,128)(2,1)S(1)} %all-to-all-done.rows_ref, bf16[1152,432]{1,0:T(8,128)(2,1)S(1)} %all_gather.9.weight_ref, f32[1152,9]{1,0:T(8,128)S(1)} %get-tuple-element.15.mod_ref), custom_call_target="tpu_custom_call" | custom-call | tf_op jit(solution)/shard_map/pallas_call | solution.py:330
  68.7 0.8 copy-done
  69.5 0.7 copy-done.2
  70.2 0.4 collective-permute-done.1
  70.6 1.9 %concatenate.7 = bf16[72,2944]{1,0:T(8,128)(2,1)} concatenate(bf16[72,1152]{1,0:T(8,128)(2,1)} %copy-done.2, bf16[72,576]{1,0:T(8,128)(2,1)S(1)} %slice.10, bf16[72,1152]{1,0:T(8,128)(2,1)} %collective-permute-done.1, bf16[72,64]{1,0:T(8,128)(2,1)S(1)} %slice.11), dimensions={1} | concatenate | bytes 847872 | tf_op jit(solution)/shard_map/concatenate | solution.py:337
  72.6 4.9 %all-to-all-start.1 = ((bf16[8,144,256]{2,1,0:T(8,128)(2,1)}), bf16[8,144,256]{2,1,0:T(8,128)(2,1)S(1)}, u32[]{:S(2)}, u32[]{:S(2)}) async-start(bf16[8,144,256]{2,1,0:T(8,128)(2,1)} %copy-done), calls=%async_computation.1 | async-start | bytes 1179648 | tf_op jit(solution)/shard_map/all_to_all | solution.py:297
  77.5 9.6 %all-to-all-done.1.gathered_ref = bf16[8,144,256]{2,1,0:T(8,128)(2,1)S(1)} async-done(((bf16[8,144,256]{2,1,0:T(8,128)(2,1)}), bf16[8,144,256]{2,1,0:T(8,128)(2,1)S(1)}, u32[]{:S(2)}, u32[]{:S(2)}) %all-to-all-start.1) | async-done | bytes 589856 | tf_op jit(solution)/shard_map/all_to_all | solution.py:297
  87.1 5.5 %shard_map.86 = (bf16[16,112,128]{2,1,0:T(8,128)(2,1)S(1)}, bf16[1152,256]{1,0:T(8,128)(2,1)S(1)}) custom-call(s32[2]{0:T(128)S(1)} %pad_add_fusion.spot_ref, bf16[8,144,256]{2,1,0:T(8,128)(2,1)S(1)} %all-to-all-done.1.gathered_ref, bf16[8,144,640]{2,1,0:T(8,128)(2,1)S(1)} %all-to-all-done.rows_ref, ...), custom_call_target="tpu_custom_call" | custom-call | tf_op jit(solution)/shard_map/pallas_call | solution.py:339
  92.5 26.3 %all_to_all.35.moved_ref = bf16[16,112,128]{2,1,0:T(8,128)(2,1)S(1)} all-to-all(bf16[16,112,128]{2,1,0:T(8,128)(2,1)S(1)} %get-tuple-element.17), channel_id=1, replica_groups=mesh['frame'=16,'head'=8,'dp'=4] {'frame'}, dimensions={0} | all-to-all | bytes 917504 | tf_op jit(solution)/shard_map/all_to_all | solution.py:298
  118.9 1.7 shard_map.87
  120.5 15.9 %all_to_all.36.moved_ref = bf16[16,48,128]{2,1,0:T(8,128)(2,1)S(1)} all-to-all(bf16[16,48,128]{2,1,0:T(8,128)(2,1)S(1)} %shard_map.87), channel_id=1, replica_groups=mesh['frame'=16,'head'=8,'dp'=4] {'frame'}, dimensions={0} | all-to-all | bytes 393216 | tf_op jit(solution)/shard_map/all_to_all | solution.py:298
  136.5 0.9 shard_map.88
  137.4 12.1 %all_to_all.37.gathered_ref = bf16[4,288,256]{2,1,0:T(8,128)(2,1)S(1)} all-to-all(bf16[4,288,256]{2,1,0:T(8,128)(2,1)S(1)} %shard_map.88), channel_id=1, replica_groups={{0,8,16,24},{4,12,20,28},{1,9,17,25},{5,13,21,29},{2,10,18,26},{6,14,22..., dimensions={0} | all-to-all | bytes 1179648 | tf_op jit(solution)/shard_map/all_to_all | solution.py:353
  149.4 7.2 %shard_map.89 = bf16[8,144,256]{2,1,0:T(8,128)(2,1)S(1)} custom-call(s32[2]{0:T(128)S(1)} %pad_add_fusion.spot_ref, bf16[4,288,256]{2,1,0:T(8,128)(2,1)S(1)} %all_to_all.37.gathered_ref, bf16[1152,256]{1,0:T(8,128)(2,1)S(1)} %get-tuple-element.18.before_ref, bf16[1152,2944]{1,0:T(8,128)(2,1)} %all-gather.5.cloned.1.call-done.weight_ref, ...), custom_call_target="tpu_custom_call" | custom-call | tf_op jit(solution)/shard_map/pallas_call | solution.py:355
  156.7 12.1 %all_to_all.38.partial_ref = bf16[8,144,256]{2,1,0:T(8,128)(2,1)S(1)} all-to-all(bf16[8,144,256]{2,1,0:T(8,128)(2,1)S(1)} %shard_map.89), channel_id=1, replica_groups=mesh['frame'=16,'head'=8,'dp'=4] {'head'}, dimensions={0} | all-to-all | bytes 1179648 | tf_op jit(solution)/shard_map/all_to_all | solution.py:297
  168.8 0.7 shard_map.90
  (32 shorter events, 0.7 us)
Async XLA Ops:
  6.5 14.1 %slice-start = ((bf16[72,576]{1,0:T(8,128)(2,1)}), bf16[72,512]{1,0:T(8,128)(2,1)S(1)}, s32[]{:S(2)}) async-start(bf16[72,576]{1,0:T(8,128)(2,1)} %refs_1_.1), calls=%async_computation.9 | async-start | bytes 147456 | tf_op jit(solution)/shard_map/slice | solution.py:321
  6.5 0.8 copy-start.6
  8.1 12.2 %all-to-all-start.2 = ((bf16[8,72,144]{2,1,0:T(8,128)(2,1)}), bf16[8,72,144]{2,1,0:T(8,128)(2,1)S(1)}, u32[]{:S(2)}, u32[]{:S(2)}) async-start(bf16[8,72,144]{2,1,0:T(8,128)(2,1)} %shard_map.85), calls=%async_computation.2 | async-start | bytes 589824 | tf_op jit(solution)/shard_map/all_to_all | solution.py:297
  14.0 73.1 %all-gather.3.cloned.1.call-start = ((), (), s32[]{:S(2)}) async-start(), calls=%async_computation.7 | async-start | bytes 6266880 | tf_op jit(solution)/shard_map/all_gather | solution.py:299
  14.0 5.7 %collective-permute-start = (bf16[72,3,144]{2,0,1:T(8,128)(2,1)}, bf16[72,3,144]{2,0,1:T(8,128)(2,1)S(1)}, u32[]{:S(2)}, u32[]{:S(2)}) collective-permute-start(bf16[72,3,144]{2,0,1:T(8,128)(2,1)} %param.12), channel_id=1, source_target_pairs={{0,4},{4,0},{8,12},{12,8},{16,20},{20,16},{24,28},{28,24},{1,5},{5... | collective-permute-start | bytes 186632 | tf_op jit(solution)/shard_map/ppermute | solution.py:304
  18.4 3.1 %copy-start.3 = (bf16[1,512,144]{1,2,0:T(8,128)(2,1)S(1)}, bf16[1,512,144]{1,2,0:T(8,128)(2,1)}, u32[]{:S(2)}) copy-start(bf16[1,512,144]{1,2,0:T(8,128)(2,1)} %param.8) | copy-start | bytes 442372
  18.4 3.1 %copy-start.5 = (f32[9,1152]{1,0:T(8,128)S(1)}, f32[9,1152]{1,0:T(8,128)}, u32[]{:S(2)}) copy-start(f32[9,1152]{1,0:T(8,128)} %mod_ref.1) | copy-start | bytes 124420
  18.4 3.1 %copy-start.7 = (bf16[144,72]{1,0:T(8,128)(2,1)S(1)}, bf16[144,72]{1,0:T(8,128)(2,1)}, u32[]{:S(2)}) copy-start(bf16[144,72]{1,0:T(8,128)(2,1)} %late_ref.1) | copy-start | bytes 62212
  22.9 5.0 %copy-start.8 = (bf16[72,3,144]{2,0,1:T(8,128)(2,1)S(1)}, bf16[72,3,144]{2,0,1:T(8,128)(2,1)}, u32[]{:S(2)}) copy-start(bf16[72,3,144]{2,0,1:T(8,128)(2,1)} %param.10) | copy-start | bytes 186628
  22.9 5.3 %copy-start.1 = (bf16[72,576]{1,0:T(8,128)(2,1)S(1)}, bf16[72,576]{1,0:T(8,128)(2,1)}, u32[]{:S(2)}) copy-start(bf16[72,576]{1,0:T(8,128)(2,1)} %refs_1_.1) | copy-start | bytes 248836
  22.9 5.3 %copy-start.4 = (bf16[576,72]{0,1:T(8,128)(2,1)S(1)}, bf16[576,72]{0,1:T(8,128)(2,1)}, u32[]{:S(2)}) copy-start(bf16[576,72]{0,1:T(8,128)(2,1)} %param.15) | copy-start | bytes 248836
  22.9 43.1 %all-to-all-start = ((bf16[8,144,640]{2,1,0:T(8,128)(2,1)}), bf16[8,144,640]{2,1,0:T(8,128)(2,1)S(1)}, u32[]{:S(2)}, u32[]{:S(2)}) async-start(bf16[8,144,640]{2,1,0:T(8,128)(2,1)} %get-tuple-element.13), calls=%async_computation | async-start | bytes 2949120 | tf_op jit(solution)/shard_map/all_to_all | solution.py:297
  27.9 121.6 %all-gather.5.cloned.1.call-start = ((), (), s32[]{:S(2)}) async-start(), calls=%async_computation.8 | async-start | bytes 7206912 | tf_op jit(solution)/shard_map/all_gather | solution.py:299
  62.4 8.3 %collective-permute-start.1 = (bf16[72,1152]{1,0:T(8,128)(2,1)S(1)}, bf16[72,1152]{1,0:T(8,128)(2,1)}, u32[]{:S(2)}, u32[]{:S(2)}) collective-permute-start(bf16[72,1152]{1,0:T(8,128)(2,1)S(1)} %shard_map.83), channel_id=1, source_target_pairs={{0,4},{4,0},{8,12},{12,8},{16,20},{20,16},{24,28},{28,24},{1,5},{5... | collective-permute-start | bytes 497672 | tf_op jit(solution)/shard_map/ppermute | solution.py:328
  68.7 0.8 copy-start
  69.5 0.7 copy-start.2
  72.6 14.5 %all-to-all-start.1 = ((bf16[8,144,256]{2,1,0:T(8,128)(2,1)}), bf16[8,144,256]{2,1,0:T(8,128)(2,1)S(1)}, u32[]{:S(2)}, u32[]{:S(2)}) async-start(bf16[8,144,256]{2,1,0:T(8,128)(2,1)} %copy-done), calls=%async_computation.1 | async-start | bytes 1179648 | tf_op jit(solution)/shard_map/all_to_all | solution.py:297
Sparse Core Ops, SparseCore 0:
  21.6 57.8 all-gather.2
  81.6 63.7 all-gather.4

commit v8 on v6

--- a/solution.py
+++ b/solution.py
@@ -79,7 +79,8 @@
         weights = jnp.exp(project(key, query) * FACTOR)
         if same is not None:
             weights = jnp.where(same, weights, 0.0)
-        weights = (weights / jnp.sum(weights, axis=0, keepdims=True)).astype(jnp.bfloat16)
+        inverse = 1.0 / jnp.sum(weights, axis=0, keepdims=True)
+        weights = (weights * inverse).astype(jnp.bfloat16)
         outs.append(jnp.dot(value, weights, preferred_element_type=jnp.float32))
     return jnp.concatenate(outs, 0)
 
@@ -302,7 +303,6 @@
     others_qkv = lax.ppermute(temporal_qkv, "head", across_y)
     out_copies = vmem_call(turned_copies_kernel, array(heads_n, depth, width), [HERE])(spatial_out)
     mlp = vmem_call(side_by_side_kernel, array(depth, 2 * units), [HERE] * 2)(mlp_up, mlp_down.T)
-    others = lax.ppermute(mlp, "head", across_y)
     row_copies, mod = vmem_call(
         opening_kernel,
         (
@@ -322,6 +322,9 @@
     early = gather_frame(jnp.concatenate(pieces, axis=1))
     stream = spread(row_copies)
     s_qkv = gather_frame(spatial_qkv.reshape(depth, -1))
+
+    s_qkv, mlp = lax.optimization_barrier((s_qkv, mlp))
+    others = lax.ppermute(mlp, "head", across_y)
 
     attended = vmem_call(
         spatial_kernel, array(heads_n, width, share), [HERE] * 3, (bf16(full, rows),)

time: 177 us -> 178 us (level)
  transfers between devices with their start and end apart: 7 -> 7, of which waited for: 3 -> 4; matrix products, arithmetic and copies ran while one was open for 1% -> 1% of each run, Pallas kernels for 8% -> 8%
where the time goes in v8:
time: 178 us; the launch traced here: 176 us
  blocking collectives  101 us (57%)
  Pallas kernels  22.8 us (13%)
  starting transfers between devices  22.7 us (13%)
  between operations  13.6 us (8%)
  waiting for transfers between devices  12.1 us (7%)
  local copies, waits for them, and re-layouts  4.63 us (3%)
    all_to_all x2, blocking collectives, per_device(): swap = lambda chunks: lax.all_to_all(chunks, 'frame', 0, 0, tiled=True)  42.3 us
    all_gather x1, blocking collectives, per_device(): lax.all_gather(packed, 'frame', axis=0, tiled=True)  34 us
    all_to_all x3, starting transfers between devices, per_device(): spread = lambda copies: lax.all_to_all(copies, 'head', 0, 0, tiled=True)  15.7 us
    all_to_all x1, blocking collectives, per_device(): spread = lambda copies: lax.all_to_all(copies, 'head', 0, 0, tiled=True)  12.3 us
    all_to_all x1, blocking collectives, per_device(): lax.all_to_all(attended, 'head', 0, 0, axis_index_groups=along_x, tiled=T...  12 us
    all_to_all x3, waiting for transfers between devices, per_device(): spread = lambda copies: lax.all_to_all(copies, 'head', 0, 0, tiled=True)  9.79 us
    pallas_call x1, Pallas kernels, per_device(): vmem_call(mlp_kernel, array(heads_n, width, share), [SCALAR, HERE, HERE,...  7.23 us
    pallas_call x1, Pallas kernels, per_device(): vmem_call(spatial_end_kernel, (array(frames_n, 112, LANES), array(full, s...  5.47 us
  transfers between devices with their start and end apart: 7, of which 4 were waited for; matrix products, arithmetic and copies ran while one was open for 1% of the time, Pallas kernels for 8%

profile of v8, /device:TPU:1, one launch (start us, length us, event | category | flops | bytes accessed | tf_op | source)
XLA Modules:
  0.0 176.5 jit_solution(4419946060478191896)
XLA Ops:
  6.5 0.8 copy-done.5
  7.3 0.8 shard_map.85
  8.1 5.9 %all-to-all-start.2 = ((bf16[8,72,144]{2,1,0:T(8,128)(2,1)}), bf16[8,72,144]{2,1,0:T(8,128)(2,1)S(1)}, u32[]{:S(2)}, u32[]{:S(2)}) async-start(bf16[8,72,144]{2,1,0:T(8,128)(2,1)} %shard_map.85), calls=%async_computation.2 | async-start | bytes 589824 | tf_op jit(solution)/shard_map/all_to_all | solution.py:296
  14.0 3.3 %collective-permute-start = (bf16[72,3,144]{2,0,1:T(8,128)(2,1)}, bf16[72,3,144]{2,0,1:T(8,128)(2,1)S(1)}, u32[]{:S(2)}, u32[]{:S(2)}) collective-permute-start(bf16[72,3,144]{2,0,1:T(8,128)(2,1)} %param.12), channel_id=1, source_target_pairs={{0,4},{4,0},{8,12},{12,8},{16,20},{20,16},{24,28},{28,24},{1,5},{5... | collective-permute-start | bytes 186632 | tf_op jit(solution)/shard_map/ppermute | solution.py:303
  17.4 1.1 copy.16
  18.6 1.2 collective-permute-done
  19.7 0.2 copy.17
  19.9 0.1 copy.19
  20.0 0.3 all-to-all-done.2
  20.3 0.3 reshape.20
  20.6 0.9 concatenate.3
  21.6 1.4 shard_map.82
  23.0 5.0 %all-to-all-start = ((bf16[8,144,640]{2,1,0:T(8,128)(2,1)}), bf16[8,144,640]{2,1,0:T(8,128)(2,1)S(1)}, u32[]{:S(2)}, u32[]{:S(2)}) async-start(bf16[8,144,640]{2,1,0:T(8,128)(2,1)} %get-tuple-element.13), calls=%async_computation | async-start | bytes 2949120 | tf_op jit(solution)/shard_map/all_to_all | solution.py:296
  28.0 0.2 copy.13
  28.1 0.1 copy.14
  28.4 34.0 %all_gather.9.weight_ref = bf16[1152,432]{1,0:T(8,128)(2,1)S(1)} all-gather(bf16[72,432]{1,0:T(8,128)(2,1)S(1)} %copy.14), channel_id=1, replica_groups=mesh['frame'=16,'head'=8,'dp'=4] {'frame'}, dimensions={0}, use_global_device_ids=true | all-gather | bytes 1057536 | tf_op jit(solution)/shard_map/all_gather | solution.py:298
  62.4 3.6 %collective-permute-start.1 = (bf16[72,1152]{1,0:T(8,128)(2,1)S(1)}, bf16[72,1152]{1,0:T(8,128)(2,1)}, u32[]{:S(2)}, u32[]{:S(2)}) collective-permute-start(bf16[72,1152]{1,0:T(8,128)(2,1)S(1)} %shard_map.83.mlp_ref), channel_id=1, source_target_pairs={{0,4},{4,0},{8,12},{12,8},{16,20},{20,16},{24,28},{28,24},{1,5},{5... | collective-permute-start | bytes 497672 | tf_op jit(solution)/shard_map/ppermute | solution.py:327
  66.1 2.6 %shard_map.84 = bf16[8,144,256]{2,1,0:T(8,128)(2,1)S(1)} custom-call(bf16[8,144,640]{2,1,0:T(8,128)(2,1)S(1)} %all-to-all-done.rows_ref, bf16[1152,432]{1,0:T(8,128)(2,1)S(1)} %all_gather.9.weight_ref, f32[1152,9]{1,0:T(8,128)S(1)} %get-tuple-element.15.mod_ref), custom_call_target="tpu_custom_call" | custom-call | tf_op jit(solution)/shard_map/pallas_call | solution.py:329
  68.7 0.9 copy-done
  69.5 1.1 collective-permute-done.1.others_ref
  70.6 2.0 %shard_map.89 = bf16[72,2944]{1,0:T(8,128)(2,1)} custom-call(bf16[8,144,128]{2,1,0:T(8,128)(2,1)S(1)} %slice.8.rows_ref, bf16[72,1152]{1,0:T(8,128)(2,1)S(1)} %shard_map.83.mlp_ref, bf16[72,1152]{1,0:T(8,128)(2,1)} %collective-permute-done.1.others_ref), custom_call_target="tpu_custom_call" | custom-call | tf_op jit(solution)/shard_map/pallas_call | solution.py:333
  72.6 4.8 %all-to-all-start.1 = ((bf16[8,144,256]{2,1,0:T(8,128)(2,1)}), bf16[8,144,256]{2,1,0:T(8,128)(2,1)S(1)}, u32[]{:S(2)}, u32[]{:S(2)}) async-start(bf16[8,144,256]{2,1,0:T(8,128)(2,1)} %copy-done), calls=%async_computation.1 | async-start | bytes 1179648 | tf_op jit(solution)/shard_map/all_to_all | solution.py:296
  77.5 9.5 %all-to-all-done.1.gathered_ref = bf16[8,144,256]{2,1,0:T(8,128)(2,1)S(1)} async-done(((bf16[8,144,256]{2,1,0:T(8,128)(2,1)}), bf16[8,144,256]{2,1,0:T(8,128)(2,1)S(1)}, u32[]{:S(2)}, u32[]{:S(2)}) %all-to-all-start.1) | async-done | bytes 589856 | tf_op jit(solution)/shard_map/all_to_all | solution.py:296
  87.1 5.5 %shard_map.86 = (bf16[16,112,128]{2,1,0:T(8,128)(2,1)S(1)}, bf16[1152,256]{1,0:T(8,128)(2,1)S(1)}) custom-call(s32[2]{0:T(128)S(1)} %pad_add_fusion.spot_ref, bf16[8,144,256]{2,1,0:T(8,128)(2,1)S(1)} %all-to-all-done.1.gathered_ref, bf16[8,144,640]{2,1,0:T(8,128)(2,1)S(1)} %all-to-all-done.rows_ref, ...), custom_call_target="tpu_custom_call" | custom-call | tf_op jit(solution)/shard_map/pallas_call | solution.py:338
  92.5 26.3 %all_to_all.35.moved_ref = bf16[16,112,128]{2,1,0:T(8,128)(2,1)S(1)} all-to-all(bf16[16,112,128]{2,1,0:T(8,128)(2,1)S(1)} %get-tuple-element.17), channel_id=1, replica_groups=mesh['frame'=16,'head'=8,'dp'=4] {'frame'}, dimensions={0} | all-to-all | bytes 917504 | tf_op jit(solution)/shard_map/all_to_all | solution.py:297
  118.9 1.7 shard_map.87
  120.6 15.9 %all_to_all.36.moved_ref = bf16[16,48,128]{2,1,0:T(8,128)(2,1)S(1)} all-to-all(bf16[16,48,128]{2,1,0:T(8,128)(2,1)S(1)} %shard_map.87), channel_id=1, replica_groups=mesh['frame'=16,'head'=8,'dp'=4] {'frame'}, dimensions={0} | all-to-all | bytes 393216 | tf_op jit(solution)/shard_map/all_to_all | solution.py:297
  136.5 0.9 shard_map.88
  137.4 12.0 %all_to_all.37.gathered_ref = bf16[4,288,256]{2,1,0:T(8,128)(2,1)S(1)} all-to-all(bf16[4,288,256]{2,1,0:T(8,128)(2,1)S(1)} %shard_map.88), channel_id=1, replica_groups={{0,8,16,24},{4,12,20,28},{1,9,17,25},{5,13,21,29},{2,10,18,26},{6,14,22..., dimensions={0} | all-to-all | bytes 1179648 | tf_op jit(solution)/shard_map/all_to_all | solution.py:352
  149.4 7.2 %shard_map.90 = bf16[8,144,256]{2,1,0:T(8,128)(2,1)S(1)} custom-call(s32[2]{0:T(128)S(1)} %pad_add_fusion.spot_ref, bf16[4,288,256]{2,1,0:T(8,128)(2,1)S(1)} %all_to_all.37.gathered_ref, bf16[1152,256]{1,0:T(8,128)(2,1)S(1)} %get-tuple-element.18.before_ref, bf16[1152,2944]{1,0:T(8,128)(2,1)} %all-gather.5.cloned.1.call-done.weight_ref, ...), custom_call_target="tpu_custom_call" | custom-call | tf_op jit(solution)/shard_map/pallas_call | solution.py:354
  156.6 12.3 %all_to_all.38.partial_ref = bf16[8,144,256]{2,1,0:T(8,128)(2,1)S(1)} all-to-all(bf16[8,144,256]{2,1,0:T(8,128)(2,1)S(1)} %shard_map.90), channel_id=1, replica_groups=mesh['frame'=16,'head'=8,'dp'=4] {'head'}, dimensions={0} | all-to-all | bytes 1179648 | tf_op jit(solution)/shard_map/all_to_all | solution.py:296
  168.9 0.7 shard_map.91
  (29 shorter events, 0.5 us)
Async XLA Ops:
  6.5 14.1 %slice-start = ((bf16[72,576]{1,0:T(8,128)(2,1)}), bf16[72,512]{1,0:T(8,128)(2,1)S(1)}, s32[]{:S(2)}) async-start(bf16[72,576]{1,0:T(8,128)(2,1)} %refs_0_.1), calls=%async_computation.9 | async-start | bytes 147456 | tf_op jit(solution)/shard_map/slice | solution.py:320
  6.5 0.8 copy-start.5
  8.1 12.2 %all-to-all-start.2 = ((bf16[8,72,144]{2,1,0:T(8,128)(2,1)}), bf16[8,72,144]{2,1,0:T(8,128)(2,1)S(1)}, u32[]{:S(2)}, u32[]{:S(2)}) async-start(bf16[8,72,144]{2,1,0:T(8,128)(2,1)} %shard_map.85), calls=%async_computation.2 | async-start | bytes 589824 | tf_op jit(solution)/shard_map/all_to_all | solution.py:296
  14.0 73.1 %all-gather.3.cloned.1.call-start = ((), (), s32[]{:S(2)}) async-start(), calls=%async_computation.7 | async-start | bytes 6266880 | tf_op jit(solution)/shard_map/all_gather | solution.py:298
  14.0 5.7 %collective-permute-start = (bf16[72,3,144]{2,0,1:T(8,128)(2,1)}, bf16[72,3,144]{2,0,1:T(8,128)(2,1)S(1)}, u32[]{:S(2)}, u32[]{:S(2)}) collective-permute-start(bf16[72,3,144]{2,0,1:T(8,128)(2,1)} %param.12), channel_id=1, source_target_pairs={{0,4},{4,0},{8,12},{12,8},{16,20},{20,16},{24,28},{28,24},{1,5},{5... | collective-permute-start | bytes 186632 | tf_op jit(solution)/shard_map/ppermute | solution.py:303
  18.4 3.1 %copy-start.2 = (bf16[1,512,144]{1,2,0:T(8,128)(2,1)S(1)}, bf16[1,512,144]{1,2,0:T(8,128)(2,1)}, u32[]{:S(2)}) copy-start(bf16[1,512,144]{1,2,0:T(8,128)(2,1)} %param.8) | copy-start | bytes 442372
  18.4 3.1 %copy-start.4 = (f32[9,1152]{1,0:T(8,128)S(1)}, f32[9,1152]{1,0:T(8,128)}, u32[]{:S(2)}) copy-start(f32[9,1152]{1,0:T(8,128)} %mod_ref.1) | copy-start | bytes 124420
  18.4 3.1 %copy-start.6 = (bf16[144,72]{1,0:T(8,128)(2,1)S(1)}, bf16[144,72]{1,0:T(8,128)(2,1)}, u32[]{:S(2)}) copy-start(bf16[144,72]{1,0:T(8,128)(2,1)} %late_ref.1) | copy-start | bytes 62212
  23.0 5.0 %copy-start.7 = (bf16[72,3,144]{2,0,1:T(8,128)(2,1)S(1)}, bf16[72,3,144]{2,0,1:T(8,128)(2,1)}, u32[]{:S(2)}) copy-start(bf16[72,3,144]{2,0,1:T(8,128)(2,1)} %param.10) | copy-start | bytes 186628
  23.0 5.3 %copy-start.1 = (bf16[72,576]{1,0:T(8,128)(2,1)S(1)}, bf16[72,576]{1,0:T(8,128)(2,1)}, u32[]{:S(2)}) copy-start(bf16[72,576]{1,0:T(8,128)(2,1)} %refs_0_.1) | copy-start | bytes 248836
  23.0 5.3 %copy-start.3 = (bf16[576,72]{0,1:T(8,128)(2,1)S(1)}, bf16[576,72]{0,1:T(8,128)(2,1)}, u32[]{:S(2)}) copy-start(bf16[576,72]{0,1:T(8,128)(2,1)} %param.15) | copy-start | bytes 248836
  23.0 43.0 %all-to-all-start = ((bf16[8,144,640]{2,1,0:T(8,128)(2,1)}), bf16[8,144,640]{2,1,0:T(8,128)(2,1)S(1)}, u32[]{:S(2)}, u32[]{:S(2)}) async-start(bf16[8,144,640]{2,1,0:T(8,128)(2,1)} %get-tuple-element.13), calls=%async_computation | async-start | bytes 2949120 | tf_op jit(solution)/shard_map/all_to_all | solution.py:296
  27.9 121.5 %all-gather.5.cloned.1.call-start = ((), (), s32[]{:S(2)}) async-start(), calls=%async_computation.8 | async-start | bytes 7206912 | tf_op jit(solution)/shard_map/all_gather | solution.py:298
  62.4 8.3 %collective-permute-start.1 = (bf16[72,1152]{1,0:T(8,128)(2,1)S(1)}, bf16[72,1152]{1,0:T(8,128)(2,1)}, u32[]{:S(2)}, u32[]{:S(2)}) collective-permute-start(bf16[72,1152]{1,0:T(8,128)(2,1)S(1)} %shard_map.83.mlp_ref), channel_id=1, source_target_pairs={{0,4},{4,0},{8,12},{12,8},{16,20},{20,16},{24,28},{28,24},{1,5},{5... | collective-permute-start | bytes 497672 | tf_op jit(solution)/shard_map/ppermute | solution.py:327
  68.7 0.9 copy-start
  72.6 14.4 %all-to-all-start.1 = ((bf16[8,144,256]{2,1,0:T(8,128)(2,1)}), bf16[8,144,256]{2,1,0:T(8,128)(2,1)S(1)}, u32[]{:S(2)}, u32[]{:S(2)}) async-start(bf16[8,144,256]{2,1,0:T(8,128)(2,1)} %copy-done), calls=%async_computation.1 | async-start | bytes 1179648 | tf_op jit(solution)/shard_map/all_to_all | solution.py:296
Sparse Core Ops, SparseCore 0:
  21.7 57.8 all-gather.2
  81.6 63.5 all-gather.4

commit v9 on v8

--- a/solution.py
+++ b/solution.py
@@ -303,6 +303,7 @@
     others_qkv = lax.ppermute(temporal_qkv, "head", across_y)
     out_copies = vmem_call(turned_copies_kernel, array(heads_n, depth, width), [HERE])(spatial_out)
     mlp = vmem_call(side_by_side_kernel, array(depth, 2 * units), [HERE] * 2)(mlp_up, mlp_down.T)
+    others = lax.ppermute(mlp, "head", across_y)
     row_copies, mod = vmem_call(
         opening_kernel,
         (
@@ -322,9 +323,6 @@
     early = gather_frame(jnp.concatenate(pieces, axis=1))
     stream = spread(row_copies)
     s_qkv = gather_frame(spatial_qkv.reshape(depth, -1))
-
-    s_qkv, mlp = lax.optimization_barrier((s_qkv, mlp))
-    others = lax.ppermute(mlp, "head", across_y)
 
     attended = vmem_call(
         spatial_kernel, array(heads_n, width, share), [HERE] * 3, (bf16(full, rows),)

time: 178 us -> 177 us (level)
  transfers between devices with their start and end apart: 7 -> 7, of which waited for: 4 -> 3; matrix products, arithmetic and copies ran while one was open for 1% -> 1% of each run, Pallas kernels for 8% -> 8%
where the time goes in v9:
time: 177 us; the launch traced here: 176 us
  blocking collectives  100 us (56%)
  Pallas kernels  22.8 us (13%)
  starting transfers between devices  22.6 us (13%)
  between operations  13.6 us (8%)
  waiting for transfers between devices  11.6 us (7%)
  local copies, waits for them, and re-layouts  4.63 us (3%)
    all_to_all x2, blocking collectives, per_device(): swap = lambda chunks: lax.all_to_all(chunks, 'frame', 0, 0, tiled=True)  41.1 us
    all_gather x1, blocking collectives, per_device(): lax.all_gather(packed, 'frame', axis=0, tiled=True)  34.7 us
    all_to_all x3, starting transfers between devices, per_device(): spread = lambda copies: lax.all_to_all(copies, 'head', 0, 0, tiled=True)  15.9 us
    all_to_all x1, blocking collectives, per_device(): lax.all_to_all(attended, 'head', 0, 0, axis_index_groups=along_x, tiled=T...  12.4 us
    all_to_all x1, blocking collectives, per_device(): spread = lambda copies: lax.all_to_all(copies, 'head', 0, 0, tiled=True)  12.1 us
    all_to_all x3, waiting for transfers between devices, per_device(): spread = lambda copies: lax.all_to_all(copies, 'head', 0, 0, tiled=True)  10.4 us
    pallas_call x1, Pallas kernels, per_device(): vmem_call(mlp_kernel, array(heads_n, width, share), [SCALAR, HERE, HERE,...  7.24 us
    pallas_call x1, Pallas kernels, per_device(): vmem_call(spatial_end_kernel, (array(frames_n, 112, LANES), array(full, s...  5.47 us
  transfers between devices with their start and end apart: 7, of which 3 were waited for; matrix products, arithmetic and copies ran while one was open for 1% of the time, Pallas kernels for 8%

profile of v9, /device:TPU:1, one launch (start us, length us, event | category | flops | bytes accessed | tf_op | source)
XLA Modules:
  0.0 175.7 jit_solution(11827084066601882540)
XLA Ops:
  6.5 0.8 copy-done.5
  7.3 0.8 shard_map.84
  8.1 5.9 %all-to-all-start.2 = ((bf16[8,72,144]{2,1,0:T(8,128)(2,1)}), bf16[8,72,144]{2,1,0:T(8,128)(2,1)S(1)}, u32[]{:S(2)}, u32[]{:S(2)}) async-start(bf16[8,72,144]{2,1,0:T(8,128)(2,1)} %shard_map.84), calls=%async_computation.2 | async-start | bytes 589824 | tf_op jit(solution)/shard_map/all_to_all | solution.py:296
  14.0 3.3 %collective-permute-start = (bf16[72,3,144]{2,0,1:T(8,128)(2,1)}, bf16[72,3,144]{2,0,1:T(8,128)(2,1)S(1)}, u32[]{:S(2)}, u32[]{:S(2)}) collective-permute-start(bf16[72,3,144]{2,0,1:T(8,128)(2,1)} %param.12), channel_id=1, source_target_pairs={{0,4},{4,0},{8,12},{12,8},{16,20},{20,16},{24,28},{28,24},{1,5},{5... | collective-permute-start | bytes 186632 | tf_op jit(solution)/shard_map/ppermute | solution.py:303
  17.4 1.1 copy.16
  18.4 0.1 copy.18
  18.6 1.2 collective-permute-done
  19.7 0.2 copy.17
  19.9 0.1 copy.19
  20.0 0.3 all-to-all-done.2
  20.3 0.3 reshape.20
  20.6 0.9 concatenate.3
  21.6 1.4 shard_map.82
  23.0 5.0 %all-to-all-start = ((bf16[8,144,640]{2,1,0:T(8,128)(2,1)}), bf16[8,144,640]{2,1,0:T(8,128)(2,1)S(1)}, u32[]{:S(2)}, u32[]{:S(2)}) async-start(bf16[8,144,640]{2,1,0:T(8,128)(2,1)} %get-tuple-element.11), calls=%async_computation | async-start | bytes 2949120 | tf_op jit(solution)/shard_map/all_to_all | solution.py:296
  28.1 3.3 %collective-permute-start.1 = (bf16[72,1152]{1,0:T(8,128)(2,1)S(1)}, bf16[72,1152]{1,0:T(8,128)(2,1)}, u32[]{:S(2)}, u32[]{:S(2)}) collective-permute-start(bf16[72,1152]{1,0:T(8,128)(2,1)S(1)} %shard_map.88.mlp_ref), channel_id=1, source_target_pairs={{0,4},{4,0},{8,12},{12,8},{16,20},{20,16},{24,28},{28,24},{1,5},{5... | collective-permute-start | bytes 497672 | tf_op jit(solution)/shard_map/ppermute | solution.py:306
  31.4 0.2 copy.13
  31.6 0.1 copy.14
  31.7 34.7 %all_gather.9.weight_ref = bf16[1152,432]{1,0:T(8,128)(2,1)S(1)} all-gather(bf16[72,432]{1,0:T(8,128)(2,1)S(1)} %copy.14), channel_id=1, replica_groups=mesh['frame'=16,'head'=8,'dp'=4] {'frame'}, dimensions={0}, use_global_device_ids=true | all-gather | bytes 1057536 | tf_op jit(solution)/shard_map/all_gather | solution.py:298
  66.4 2.6 %shard_map.83 = bf16[8,144,256]{2,1,0:T(8,128)(2,1)S(1)} custom-call(bf16[8,144,640]{2,1,0:T(8,128)(2,1)S(1)} %all-to-all-done.rows_ref, bf16[1152,432]{1,0:T(8,128)(2,1)S(1)} %all_gather.9.weight_ref, f32[1152,9]{1,0:T(8,128)S(1)} %get-tuple-element.12.mod_ref), custom_call_target="tpu_custom_call" | custom-call | tf_op jit(solution)/shard_map/pallas_call | solution.py:327
  69.0 0.9 copy-done
  69.9 2.0 %shard_map.89 = bf16[72,2944]{1,0:T(8,128)(2,1)} custom-call(bf16[8,144,128]{2,1,0:T(8,128)(2,1)S(1)} %slice.8.rows_ref, bf16[72,1152]{1,0:T(8,128)(2,1)S(1)} %shard_map.88.mlp_ref, bf16[72,1152]{1,0:T(8,128)(2,1)} %collective-permute-done.1.others_ref), custom_call_target="tpu_custom_call" | custom-call | tf_op jit(solution)/shard_map/pallas_call | solution.py:331
  71.9 5.1 %all-to-all-start.1 = ((bf16[8,144,256]{2,1,0:T(8,128)(2,1)}), bf16[8,144,256]{2,1,0:T(8,128)(2,1)S(1)}, u32[]{:S(2)}, u32[]{:S(2)}) async-start(bf16[8,144,256]{2,1,0:T(8,128)(2,1)} %copy-done), calls=%async_computation.1 | async-start | bytes 1179648 | tf_op jit(solution)/shard_map/all_to_all | solution.py:296
  77.0 10.1 %all-to-all-done.1.gathered_ref = bf16[8,144,256]{2,1,0:T(8,128)(2,1)S(1)} async-done(((bf16[8,144,256]{2,1,0:T(8,128)(2,1)}), bf16[8,144,256]{2,1,0:T(8,128)(2,1)S(1)}, u32[]{:S(2)}, u32[]{:S(2)}) %all-to-all-start.1) | async-done | bytes 589856 | tf_op jit(solution)/shard_map/all_to_all | solution.py:296
  87.1 5.5 %shard_map.85 = (bf16[16,112,128]{2,1,0:T(8,128)(2,1)S(1)}, bf16[1152,256]{1,0:T(8,128)(2,1)S(1)}) custom-call(s32[2]{0:T(128)S(1)} %pad_add_fusion.spot_ref, bf16[8,144,256]{2,1,0:T(8,128)(2,1)S(1)} %all-to-all-done.1.gathered_ref, bf16[8,144,640]{2,1,0:T(8,128)(2,1)S(1)} %all-to-all-done.rows_ref, ...), custom_call_target="tpu_custom_call" | custom-call | tf_op jit(solution)/shard_map/pallas_call | solution.py:336
  92.6 25.1 %all_to_all.35.moved_ref = bf16[16,112,128]{2,1,0:T(8,128)(2,1)S(1)} all-to-all(bf16[16,112,128]{2,1,0:T(8,128)(2,1)S(1)} %get-tuple-element.14), channel_id=1, replica_groups=mesh['frame'=16,'head'=8,'dp'=4] {'frame'}, dimensions={0} | all-to-all | bytes 917504 | tf_op jit(solution)/shard_map/all_to_all | solution.py:297
  117.7 1.7 shard_map.86
  119.4 16.0 %all_to_all.36.moved_ref = bf16[16,48,128]{2,1,0:T(8,128)(2,1)S(1)} all-to-all(bf16[16,48,128]{2,1,0:T(8,128)(2,1)S(1)} %shard_map.86), channel_id=1, replica_groups=mesh['frame'=16,'head'=8,'dp'=4] {'frame'}, dimensions={0} | all-to-all | bytes 393216 | tf_op jit(solution)/shard_map/all_to_all | solution.py:297
  135.4 0.9 shard_map.87
  136.3 12.4 %all_to_all.37.gathered_ref = bf16[4,288,256]{2,1,0:T(8,128)(2,1)S(1)} all-to-all(bf16[4,288,256]{2,1,0:T(8,128)(2,1)S(1)} %shard_map.87), channel_id=1, replica_groups={{0,8,16,24},{4,12,20,28},{1,9,17,25},{5,13,21,29},{2,10,18,26},{6,14,22..., dimensions={0} | all-to-all | bytes 1179648 | tf_op jit(solution)/shard_map/all_to_all | solution.py:350
  148.7 7.2 %shard_map.90 = bf16[8,144,256]{2,1,0:T(8,128)(2,1)S(1)} custom-call(s32[2]{0:T(128)S(1)} %pad_add_fusion.spot_ref, bf16[4,288,256]{2,1,0:T(8,128)(2,1)S(1)} %all_to_all.37.gathered_ref, bf16[1152,256]{1,0:T(8,128)(2,1)S(1)} %get-tuple-element.15.before_ref, bf16[1152,2944]{1,0:T(8,128)(2,1)} %all-gather.5.cloned.1.call-done.weight_ref, ...), custom_call_target="tpu_custom_call" | custom-call | tf_op jit(solution)/shard_map/pallas_call | solution.py:352
  155.9 12.1 %all_to_all.38.partial_ref = bf16[8,144,256]{2,1,0:T(8,128)(2,1)S(1)} all-to-all(bf16[8,144,256]{2,1,0:T(8,128)(2,1)S(1)} %shard_map.90), channel_id=1, replica_groups=mesh['frame'=16,'head'=8,'dp'=4] {'head'}, dimensions={0} | all-to-all | bytes 1179648 | tf_op jit(solution)/shard_map/all_to_all | solution.py:296
  168.1 0.7 shard_map.91
  (29 shorter events, 0.4 us)
Async XLA Ops:
  6.5 14.1 %slice-start = ((bf16[72,576]{1,0:T(8,128)(2,1)}), bf16[72,512]{1,0:T(8,128)(2,1)S(1)}, s32[]{:S(2)}) async-start(bf16[72,576]{1,0:T(8,128)(2,1)} %refs_0_.1), calls=%async_computation.9 | async-start | bytes 147456 | tf_op jit(solution)/shard_map/slice | solution.py:321
  6.5 0.8 copy-start.5
  8.1 12.2 %all-to-all-start.2 = ((bf16[8,72,144]{2,1,0:T(8,128)(2,1)}), bf16[8,72,144]{2,1,0:T(8,128)(2,1)S(1)}, u32[]{:S(2)}, u32[]{:S(2)}) async-start(bf16[8,72,144]{2,1,0:T(8,128)(2,1)} %shard_map.84), calls=%async_computation.2 | async-start | bytes 589824 | tf_op jit(solution)/shard_map/all_to_all | solution.py:296
  14.0 73.1 %all-gather.3.cloned.1.call-start = ((), (), s32[]{:S(2)}) async-start(), calls=%async_computation.7 | async-start | bytes 6266880 | tf_op jit(solution)/shard_map/all_gather | solution.py:298
  14.0 5.7 %collective-permute-start = (bf16[72,3,144]{2,0,1:T(8,128)(2,1)}, bf16[72,3,144]{2,0,1:T(8,128)(2,1)S(1)}, u32[]{:S(2)}, u32[]{:S(2)}) collective-permute-start(bf16[72,3,144]{2,0,1:T(8,128)(2,1)} %param.12), channel_id=1, source_target_pairs={{0,4},{4,0},{8,12},{12,8},{16,20},{20,16},{24,28},{28,24},{1,5},{5... | collective-permute-start | bytes 186632 | tf_op jit(solution)/shard_map/ppermute | solution.py:303
  18.4 3.1 %copy-start.2 = (bf16[1,512,144]{1,2,0:T(8,128)(2,1)S(1)}, bf16[1,512,144]{1,2,0:T(8,128)(2,1)}, u32[]{:S(2)}) copy-start(bf16[1,512,144]{1,2,0:T(8,128)(2,1)} %param.8) | copy-start | bytes 442372
  18.4 3.1 %copy-start.4 = (f32[9,1152]{1,0:T(8,128)S(1)}, f32[9,1152]{1,0:T(8,128)}, u32[]{:S(2)}) copy-start(f32[9,1152]{1,0:T(8,128)} %mod_ref.1) | copy-start | bytes 124420
  18.4 3.1 %copy-start.6 = (bf16[144,72]{1,0:T(8,128)(2,1)S(1)}, bf16[144,72]{1,0:T(8,128)(2,1)}, u32[]{:S(2)}) copy-start(bf16[144,72]{1,0:T(8,128)(2,1)} %late_ref.1) | copy-start | bytes 62212
  23.0 5.0 %copy-start.1 = (bf16[72,576]{1,0:T(8,128)(2,1)S(1)}, bf16[72,576]{1,0:T(8,128)(2,1)}, u32[]{:S(2)}) copy-start(bf16[72,576]{1,0:T(8,128)(2,1)} %refs_0_.1) | copy-start | bytes 248836
  23.0 5.0 %copy-start.3 = (bf16[576,72]{0,1:T(8,128)(2,1)S(1)}, bf16[576,72]{0,1:T(8,128)(2,1)}, u32[]{:S(2)}) copy-start(bf16[576,72]{0,1:T(8,128)(2,1)} %param.15) | copy-start | bytes 248836
  23.0 8.5 %copy-start.7 = (bf16[72,3,144]{2,0,1:T(8,128)(2,1)S(1)}, bf16[72,3,144]{2,0,1:T(8,128)(2,1)}, u32[]{:S(2)}) copy-start(bf16[72,3,144]{2,0,1:T(8,128)(2,1)} %param.10) | copy-start | bytes 186628
  23.0 43.4 %all-to-all-start = ((bf16[8,144,640]{2,1,0:T(8,128)(2,1)}), bf16[8,144,640]{2,1,0:T(8,128)(2,1)S(1)}, u32[]{:S(2)}, u32[]{:S(2)}) async-start(bf16[8,144,640]{2,1,0:T(8,128)(2,1)} %get-tuple-element.11), calls=%async_computation | async-start | bytes 2949120 | tf_op jit(solution)/shard_map/all_to_all | solution.py:296
  27.9 120.8 %all-gather.5.cloned.1.call-start = ((), (), s32[]{:S(2)}) async-start(), calls=%async_computation.8 | async-start | bytes 7206912 | tf_op jit(solution)/shard_map/all_gather | solution.py:298
  28.1 41.8 %collective-permute-start.1 = (bf16[72,1152]{1,0:T(8,128)(2,1)S(1)}, bf16[72,1152]{1,0:T(8,128)(2,1)}, u32[]{:S(2)}, u32[]{:S(2)}) collective-permute-start(bf16[72,1152]{1,0:T(8,128)(2,1)S(1)} %shard_map.88.mlp_ref), channel_id=1, source_target_pairs={{0,4},{4,0},{8,12},{12,8},{16,20},{20,16},{24,28},{28,24},{1,5},{5... | collective-permute-start | bytes 497672 | tf_op jit(solution)/shard_map/ppermute | solution.py:306
  69.0 0.9 copy-start
  71.9 15.2 %all-to-all-start.1 = ((bf16[8,144,256]{2,1,0:T(8,128)(2,1)}), bf16[8,144,256]{2,1,0:T(8,128)(2,1)S(1)}, u32[]{:S(2)}, u32[]{:S(2)}) async-start(bf16[8,144,256]{2,1,0:T(8,128)(2,1)} %copy-done), calls=%async_computation.1 | async-start | bytes 1179648 | tf_op jit(solution)/shard_map/all_to_all | solution.py:296
Sparse Core Ops, SparseCore 0:
  21.7 59.6 all-gather.2
  83.5 63.0 all-gather.4
